TPU v7x, 32 devices: a whole 2x2x4 slice. The times are simulated.
32 devices in a mesh: seq: 4 (over y, core), dp: 8 (over z, x).
Axes of the slice: x: 2, y: 2, z: 4, core: 2. Of those that a mesh axis runs over, the one named last changes fastest.
Arguments:
- tokens: bfloat16 [16, 1024, 1024], P('dp', 'seq'), may hold values from -6 to 6
- lengths: int32 [16], P('dp'), may hold values from 256 to 1024, as said below
- cotangent: bfloat16 [16, 1024, 1024], P('dp', 'seq'), may hold values from -6 to 6
- first_gain: bfloat16 [1024], P(('seq', 'dp')), may hold values from 0.5 to 1.5
- first_bias: bfloat16 [1024], P(('seq', 'dp')), may hold values from -1 to 1
- mix_key: bfloat16 [1024], P(('seq', 'dp')), may hold values from 0 to 1
- mix_value: bfloat16 [1024], P(('seq', 'dp')), may hold values from 0 to 1
- mix_recept: bfloat16 [1024], P(('seq', 'dp')), may hold values from 0 to 1
- time_decay: bfloat16 [1024], P(('seq', 'dp')), as said below
- time_first: bfloat16 [1024], P(('seq', 'dp')), may hold values from -1 to 1
- key_weight: bfloat16 [1024, 1024], P(('seq', 'dp')), may hold values from -0.1875 to 0.1875
- value_weight: bfloat16 [1024, 1024], P(('seq', 'dp')), may hold values from -0.1875 to 0.1875
- recept_weight: bfloat16 [1024, 1024], P(('seq', 'dp')), may hold values from -0.1875 to 0.1875
- output_weight: bfloat16 [1024, 1024], P(('seq', 'dp')), may hold values from -0.75 to 0.75
- second_gain: bfloat16 [1024], P(('seq', 'dp')), may hold values from 0.5 to 1.5
- second_bias: bfloat16 [1024], P(('seq', 'dp')), may hold values from -1 to 1
- shift_key: bfloat16 [1024], P(('seq', 'dp')), may hold values from 0 to 1
- shift_recept: bfloat16 [1024], P(('seq', 'dp')), may hold values from 0 to 1
- up_weight: bfloat16 [1024, 4096], P(('seq', 'dp')), may hold values from -0.1875 to 0.1875
- gate_weight: bfloat16 [1024, 1024], P(('seq', 'dp')), may hold values from -0.1875 to 0.1875
- down_weight: bfloat16 [4096, 1024], P(('seq', 'dp')), may hold values from -0.09375 to 0.09375
Outputs:
- output: bfloat16 [16, 1024, 1024], P('dp', 'seq')
- tokens_grad: float32 [16, 1024, 1024], P('dp', 'seq')
- grad_first_gain: float32 [1024], P(('seq', 'dp'))
- grad_first_bias: float32 [1024], P(('seq', 'dp'))
- grad_mix_key: float32 [1024], P(('seq', 'dp'))
- grad_mix_value: float32 [1024], P(('seq', 'dp'))
- grad_mix_recept: float32 [1024], P(('seq', 'dp'))
- grad_time_decay: float32 [1024], P(('seq', 'dp'))
- grad_time_first: float32 [1024], P(('seq', 'dp'))
- grad_key_weight: float32 [1024, 1024], P(('seq', 'dp'))
- grad_value_weight: float32 [1024, 1024], P(('seq', 'dp'))
- grad_recept_weight: float32 [1024, 1024], P(('seq', 'dp'))
- grad_output_weight: float32 [1024, 1024], P(('seq', 'dp'))
- grad_second_gain: float32 [1024], P(('seq', 'dp'))
- grad_second_bias: float32 [1024], P(('seq', 'dp'))
- grad_shift_key: float32 [1024], P(('seq', 'dp'))
- grad_shift_recept: float32 [1024], P(('seq', 'dp'))
- grad_up_weight: float32 [1024, 4096], P(('seq', 'dp'))
- grad_gate_weight: float32 [1024, 1024], P(('seq', 'dp'))
- grad_down_weight: float32 [4096, 1024], P(('seq', 'dp'))
Inputs may be any that keep to these rules, and one draw needn't show every extreme that they name: `lengths`: each sequence has between 256 and 1024 live tokens at its start, the rest of its slots are padding; some sequence has each of the two. exp(time_decay) lies between 0.3 / 1024 and 0.08.
All inputs are finite; a program needn't handle non-finite values.
Results may differ from a plain program's by a relative error of at most 0.013.
Values may be sent and summed in bfloat16 or wider, within the bound.
No kernel may reach another device: no remote copies, remote signals or barrier semaphores. Data moves between devices by JAX's collectives and lax.ppermute only.
A program may use at most 256 MiB of HBM per device.

v0:
```python
import functools

import jax
import jax.numpy as jnp
from jax import lax
from jax.experimental import pallas as pl
from jax.experimental.pallas import tpu as pltpu
from jax.sharding import PartitionSpec as P

EPS = 1e-05

def norm_stats(field):
    center = field - jnp.mean(field, axis=-1, keepdims=True)
    inverse = lax.rsqrt(jnp.mean(center * center, axis=-1, keepdims=True) + EPS)
    return (center * inverse, inverse)


def norm_back(grad_normed, normalized, inverse):
    mean_grad = jnp.mean(grad_normed, axis=-1, keepdims=True)
    mean_proj = jnp.mean(grad_normed * normalized, axis=-1, keepdims=True)
    return inverse * (grad_normed - mean_grad - normalized * mean_proj)


SEQ = ("y", "core")
DP = ("z", "x")
ALL = ("y", "core", "z", "x")


def scan_tiles(rate, reverse):
    row = lax.broadcasted_iota(jnp.int32, (8, rate.shape[-1]), 0)
    steps = []
    for distance in (1, 2, 4):
        inside = row < 8 - distance if reverse else row >= distance
        steps.append((distance, jnp.where(inside, jnp.exp(-float(distance) * rate), 0.0)))
    return row, steps


def turn(x, distance, reverse):
    return pltpu.roll(x, 8 - distance if reverse else distance, 0)


def scan_rows(x, steps, reverse):
    for distance, factor in steps:
        x = x + factor * turn(x, distance, reverse)
    return x


def wkv_kernel(k_ref, v_ref, r_ref, a0_ref, b0_ref, u_ref, rate_ref, a_ref, b_ref, mixed_ref):
    seqs, span, lanes = k_ref.shape
    rate = rate_ref[...]
    boost = jnp.exp(u_ref[...])
    row, steps = scan_tiles(rate, False)
    falling = jnp.exp(-row.astype(jnp.float32) * rate)
    fall_all = jnp.exp(-8.0 * rate)
    first = row < 1
    pair = 16

    def body(i, carry):
        at = pl.ds(pl.multiple_of(i * pair, pair), pair)
        new = []
        for n in range(seqs):
            k16, v16, r16 = (ref[n, at, :] for ref in (k_ref, v_ref, r_ref))
            state = carry[2 * n : 2 * n + 2]
            tiles = []
            for g in range(2):
                k, v, r = (t[g * 8 : g * 8 + 8] for t in (k16, v16, r16))
                weight = jnp.exp(k)
                bonus = boost * weight
                sums = [scan_rows(t, steps, False) for t in (weight * v, weight)]
                a, b = (
                    falling * c + jnp.where(first, 0.0, turn(t, 1, False))
                    for c, t in zip(state, sums)
                )
                state = tuple(fall_all * c + t[7:8] for c, t in zip(state, sums))
                mixed = jax.nn.sigmoid(r) * ((a + bonus * v) / (b + bonus))
                tiles.append((a, b, mixed))
            a, b, mixed = (jnp.concatenate(t, axis=0) for t in zip(*tiles))
            a_ref[n, at, :] = a
            b_ref[n, at, :] = b
            mixed_ref[n, at, :] = mixed.astype(mixed_ref.dtype)
            new += state
        return tuple(new)

    start = []
    for n in range(seqs):
        start += [a0_ref[n : n + 1, :], b0_ref[n : n + 1, :]]
    lax.fori_loop(0, span // pair, body, tuple(start), unroll=2)


def wkv_back_kernel(
    k_ref, v_ref, r_ref, a_ref, b_ref, g_ref, p0_ref, q0_ref, u_ref, rate_ref,
    k_out, v_out, rate_out, first_out,
):
    seqs, span, lanes = k_ref.shape
    rate = rate_ref[...]
    boost = jnp.exp(u_ref[...])
    row, steps = scan_tiles(rate, True)
    falling = jnp.exp((row.astype(jnp.float32) - 7.0) * rate)
    fall_all = jnp.exp(-8.0 * rate)
    last = row > 6
    pair = 16
    count = span // pair

    def body(i, carry):
        at = pl.ds(pl.multiple_of((count - 1 - i) * pair, pair), pair)
        new = []
        rate_sum, first_sum = carry[-2:]
        for n in range(seqs):
            loaded = [ref[n, at, :] for ref in (k_ref, v_ref, r_ref, a_ref, b_ref, g_ref)]
            state = carry[2 * n : 2 * n + 2]
            tiles = []
            for g in (1, 0):
                k, v, r, a, b, grad = (t[g * 8 : g * 8 + 8] for t in loaded)
                weight = jnp.exp(k)
                bonus = boost * weight
                over = 1.0 / (b + bonus)
                wkv = (a + bonus * v) * over
                alpha = grad * jax.nn.sigmoid(r) * over
                sums = [scan_rows(t, steps, True) for t in (alpha, -alpha * wkv)]
                p, q = (
                    falling * c + jnp.where(last, 0.0, turn(t, 1, True))
                    for c, t in zip(state, sums)
                )
                state = tuple(fall_all * c + t[0:1] for c, t in zip(state, sums))
                share = alpha * bonus
                own = share * (v - wkv)
                tiles.append((own + weight * (p * v + q), share + weight * p))
                rate_sum = rate_sum + (a * p + b * q)
                first_sum = first_sum + own
            k_grad, v_grad = (jnp.concatenate(t, axis=0) for t in zip(*tiles[::-1]))
            k_out[n, at, :] = k_grad.astype(k_out.dtype)
            v_out[n, at, :] = v_grad.astype(v_out.dtype)
            new += state
        return tuple(new) + (rate_sum, first_sum)

    start = []
    for n in range(seqs):
        start += [p0_ref[n : n + 1, :], q0_ref[n : n + 1, :]]
    zero = jnp.zeros((8, lanes), jnp.float32)
    done = lax.fori_loop(0, count, body, tuple(start) + (zero, zero), unroll=2)
    rate_out[...] = -rate * jnp.exp(-rate) * jnp.sum(done[-2], axis=0, keepdims=True)
    first_out[...] = jnp.sum(done[-1], axis=0, keepdims=True)


def first_kernel(flag_ref, tok_ref, prev_ref, vec_ref, w_ref, x0_ref, x1_ref, x2_ref, y_ref, local_ref, gap_ref, normed, before, key):
    seqs, span, channels = tok_ref.shape
    j = pl.program_id(0)

    @pl.when(j == 0)
    def _():
        gain, bias = (vec_ref[0:1, :], vec_ref[1:2, :])
        for n in range(seqs):
            rows = pl.ds(n * span, span)
            field = norm_stats(tok_ref[n].astype(jnp.float32))[0] * gain + bias
            edge = norm_stats(prev_ref[n : n + 1, :].astype(jnp.float32))[0] * gain + bias
            edge = jnp.where(flag_ref[0] > 0, edge, 0.0)
            row = lax.broadcasted_iota(jnp.int32, field.shape, 0)
            normed[rows, :] = field
            earlier = jnp.where(row < 1, edge, pltpu.roll(field, 1, 0))
            before[rows, :] = earlier
            gap_ref[rows, :] = field - earlier

    mix = vec_ref[pl.ds(2 + j, 1), :]
    x = (normed[...] * mix + before[...] * (1.0 - mix)).astype(jnp.bfloat16)
    y = jnp.dot(x, w_ref[0], preferred_element_type=jnp.float32)
    y_ref[0] = y.reshape(seqs, span, channels)
    for k, ref in enumerate((x0_ref, x1_ref, x2_ref)):

        @pl.when(j == k)
        def _(ref=ref):
            ref[...] = x.reshape(seqs, span, channels)

    @pl.when(j == 0)
    def _():
        key[...] = y

    @pl.when(j == 1)
    def _():
        rate = vec_ref[5:6, :]
        place = lax.broadcasted_iota(jnp.int32, (span, channels), 0).astype(jnp.float32)
        fall = (place - (span - 1.0)) * rate
        for n in range(seqs):
            rows = slice(n * span, (n + 1) * span)
            weight = jnp.exp(key[rows, :] + fall)
            local_ref[0, n : n + 1, :] = jnp.sum(weight * y[rows], axis=0, keepdims=True)
            local_ref[1, n : n + 1, :] = jnp.sum(weight, axis=0, keepdims=True)


def first_projections(flag, tokens, prev, vectors, mats):
    seqs, span, channels = tokens.shape
    fixed = lambda *shape: pl.BlockSpec(shape, lambda j: (0,) * len(shape))
    rows = (seqs * span, channels)
    outs = pl.pallas_call(
        first_kernel,
        grid=(3,),
        out_shape=[jax.ShapeDtypeStruct(tokens.shape, jnp.bfloat16)] * 3
        + [jax.ShapeDtypeStruct((3, *tokens.shape), jnp.float32)]
        + [jax.ShapeDtypeStruct((2, seqs, channels), jnp.float32), jax.ShapeDtypeStruct(rows, jnp.float32)],
        in_specs=[
            pl.BlockSpec(memory_space=pltpu.SMEM),
            fixed(*tokens.shape),
            fixed(*prev.shape),
            fixed(*vectors.shape),
            pl.BlockSpec((1, channels, channels), lambda j: (j, 0, 0)),
        ],
        out_specs=[fixed(*tokens.shape)] * 3
        + [pl.BlockSpec((1, *tokens.shape), lambda j: (j, 0, 0, 0)), fixed(2, seqs, channels), fixed(*rows)],
        scratch_shapes=[pltpu.VMEM(rows, jnp.float32)] * 3,
        compiler_params=pltpu.CompilerParams(vmem_limit_bytes=48 << 20),
        cost_estimate=pl.CostEstimate(flops=1 << 20, bytes_accessed=1 << 16, transcendentals=0),
    )(flag, tokens, prev, vectors, mats)
    return outs[:3], outs[3], outs[4], outs[5]


def ffn_back_kernel(grad_ref, relu_ref, down_ref, up_ref, up_grad_ref, out_ref):
    wide = (((1,), (1,)), ((), ()))
    squared = lax.dot_general(grad_ref[...], down_ref[...], wide, preferred_element_type=jnp.float32)
    up_grad = (squared * (2.0 * relu_ref[...].astype(jnp.float32))).astype(jnp.bfloat16)
    up_grad_ref[...] = up_grad
    part = lax.dot_general(up_grad, up_ref[...], wide, preferred_element_type=jnp.float32)

    @pl.when(pl.program_id(0) == 0)
    def _():
        out_ref[...] = part

    @pl.when(pl.program_id(0) > 0)
    def _():
        out_ref[...] += part


def ffn_backward(grad, relu_up, down, up):
    rows, channels = grad.shape
    hidden = up.shape[1]
    block = 1024
    column = pl.BlockSpec((rows, block), lambda j: (0, j))
    return pl.pallas_call(
        ffn_back_kernel,
        grid=(hidden // block,),
        out_shape=[
            jax.ShapeDtypeStruct((rows, hidden), jnp.bfloat16),
            jax.ShapeDtypeStruct((rows, channels), jnp.float32),
        ],
        in_specs=[
            pl.BlockSpec((rows, channels), lambda j: (0, 0)),
            column,
            pl.BlockSpec((block, channels), lambda j: (j, 0)),
            pl.BlockSpec((channels, block), lambda j: (0, j)),
        ],
        out_specs=[column, pl.BlockSpec((rows, channels), lambda j: (0, 0))],
        compiler_params=pltpu.CompilerParams(vmem_limit_bytes=40 << 20),
        cost_estimate=pl.CostEstimate(
            flops=1 << 20, bytes_accessed=24 << 20, transcendentals=0
        ),
    )(grad, relu_up, down, up)


def in_grads_kernel(k_ref, v_ref, r_ref, gap_ref, mix_ref, w_ref, now_ref, next_ref, sum_ref):
    j = pl.program_id(0)
    grad = jnp.where(j == 0, k_ref[...], jnp.where(j == 1, v_ref[...], r_ref[...]))
    wide = (((1,), (1,)), ((), ()))
    part = lax.dot_general(grad, w_ref[0], wide, preferred_element_type=jnp.float32)
    mix = mix_ref[pl.ds(j, 1), :]
    now = part * mix
    sum_ref[pl.ds(j, 1), :] = jnp.sum(part * gap_ref[...], axis=0, keepdims=True)

    @pl.when(j == 0)
    def _():
        now_ref[...] = now
        next_ref[...] = part - now

    @pl.when(j > 0)
    def _():
        now_ref[...] += now
        next_ref[...] += part - now


def input_gradients(grads, gap, mixes, mats):
    rows, channels = gap.shape
    fixed = lambda *shape: pl.BlockSpec(shape, lambda j: (0,) * len(shape))
    return pl.pallas_call(
        in_grads_kernel,
        grid=(3,),
        out_shape=[jax.ShapeDtypeStruct(gap.shape, jnp.float32)] * 2
        + [jax.ShapeDtypeStruct((3, channels), jnp.float32)],
        in_specs=[fixed(rows, channels)] * 4
        + [fixed(3, channels), pl.BlockSpec((1, channels, channels), lambda j: (j, 0, 0))],
        out_specs=[fixed(rows, channels)] * 2 + [fixed(3, channels)],
        compiler_params=pltpu.CompilerParams(vmem_limit_bytes=40 << 20),
        cost_estimate=pl.CostEstimate(flops=1 << 20, bytes_accessed=8 << 20, transcendentals=0),
    )(*grads, gap, mixes, mats)


LANES = 256


def wkv_specs(seqs, span):
    field = pl.BlockSpec((seqs, span, LANES), lambda j: (0, 0, j))
    state = pl.BlockSpec((seqs, LANES), lambda j: (0, j))
    vector = pl.BlockSpec((1, LANES), lambda j: (0, j))
    return field, state, vector


def stacked_specs(seqs, span):
    shape = (None, seqs, span, LANES)
    return [pl.BlockSpec(shape, lambda j, n=n: (n, 0, 0, j)) for n in range(3)]


def wkv_forward(kvr, a0, b0, u, rate):
    shape = kvr.shape[1:]
    _, span, channels = shape
    seqs = shape[0]
    field, state, vector = wkv_specs(seqs, span)
    return pl.pallas_call(
        wkv_kernel,
        grid=(channels // LANES,),
        out_shape=[jax.ShapeDtypeStruct(shape, t) for t in (jnp.float32, jnp.float32, jnp.bfloat16)],
        in_specs=stacked_specs(seqs, span) + [state] * 2 + [vector] * 2,
        out_specs=[field] * 3,
        compiler_params=pltpu.CompilerParams(vmem_limit_bytes=32 << 20),
        cost_estimate=pl.CostEstimate(flops=1 << 20, bytes_accessed=1 << 16, transcendentals=0),
    )(kvr, kvr, kvr, a0, b0, u[None], rate[None])


def wkv_backward(kvr, a, b, grad, p0, q0, u, rate):
    seqs, span, channels = a.shape
    field, state, vector = wkv_specs(seqs, span)
    k_grad, v_grad, decay_grad, first_grad = pl.pallas_call(
        wkv_back_kernel,
        grid=(channels // LANES,),
        out_shape=[jax.ShapeDtypeStruct(a.shape, jnp.bfloat16)] * 2
        + [jax.ShapeDtypeStruct((1, channels), jnp.float32)] * 2,
        in_specs=stacked_specs(seqs, span) + [field] * 3 + [state] * 2 + [vector] * 2,
        out_specs=[field] * 2 + [vector] * 2,
        compiler_params=pltpu.CompilerParams(vmem_limit_bytes=32 << 20),
        cost_estimate=pl.CostEstimate(flops=1 << 20, bytes_accessed=1 << 16, transcendentals=0),
    )(kvr, kvr, kvr, a, b, grad, p0, q0, u[None], rate[None])
    return k_grad, v_grad, decay_grad[0], first_grad[0]


def matmul(form, left, right):
    return jnp.einsum(form, left, right, preferred_element_type=jnp.float32)


def shifted(block, axis, distance):
    count = lax.axis_size(axis)
    route = [(i - distance, i) for i in range(count) if 0 <= i - distance < count]
    return lax.ppermute(block, axis, route)


def previous_rows(field):
    came = shifted(field[:, -1, :], SEQ, 1)
    return jnp.concatenate([came[:, None, :], field[:, :-1, :]], axis=1)


def next_rows(field):
    came = shifted(field[:, 0, :], SEQ, -1)
    return jnp.concatenate([field[:, 1:, :], came[:, None, :]], axis=1)


def entering(factor, states, reverse):
    block = jnp.stack(states)
    low, high = in_order(block, spread(block, "core")[0])
    near, far = (high, low) if reverse else (low, high)
    chip = factor * near + far
    total, power = (jnp.zeros_like(block), jnp.ones_like(factor))
    for k in range(1, lax.axis_size("y")):
        total = total + power * shifted(chip, "y", -k if reverse else k)
        power = power * factor * factor
    core = lax.axis_index("core")
    total = jnp.where(core == (1 if reverse else 0), total, factor * total + near)
    return (total[0], total[1])


def in_order(own, other):
    core = lax.axis_index("core")
    return (jnp.where(core == 0, own, other), jnp.where(core == 0, other, own))


def own_half(x, own=True):
    half = x.shape[-1] // 2
    core = lax.axis_index("core")
    return jnp.where((core == 0) == own, x[..., :half], x[..., half:])


def after(x, deps):
    return lax.optimization_barrier((x, deps))[0] if jax.tree.leaves(deps) else x


def spread(block, axis):
    count = lax.axis_size(axis)
    return [
        lax.ppermute(block, axis, [(i, (i + k) % count) for i in range(count)])
        for k in range(1, count)
    ]


def cross(block, first, k):
    ys, cs, zs, xs = (lax.axis_size(axis) for axis in ALL)
    route = []
    for i in range(ys * cs * zs * xs):
        y, c, z, x = (i // (cs * zs * xs), i // (zs * xs) % cs, i // xs % zs, i % xs)
        if (c == 0) == first:
            x = (x + k) % xs
        else:
            y = (y + k) % ys
        route.append((i, ((y * cs + c) * zs + z) * xs + x))
    return lax.ppermute(block, ALL, route)


def beside_z(own):
    half = own.shape[1] // 2
    rows = lax.all_gather(own, "z", axis=0)
    return (rows[:, :, :half], rows[:, :, half:])


def beside_xy(pair, axes):
    return [[block] + spread(block, axis) for block, axis in zip(pair, axes)]


def other_core(parts):
    return [[spread(block, "core")[0] for block in part] for part in parts]


def assemble_kernel(entries, grid, at_ref, *refs):
    n_out = 1 + max(entry[2] for entry in entries)
    sources, outs, sems = (refs[: -n_out - 1], refs[-n_out - 1 : -1], refs[-1])
    ys, cs, zs, xs = grid
    y, c, x = (at_ref[j] for j in range(3))

    def back(at, k, count):
        return lax.rem(at - k + count, count)

    index = 0
    for dc in range(cs):
        for half, lead in enumerate((xs, ys)):
            for far in range(ys if half == 0 else xs):
                source = sources[index]
                index += 1

                def copy(k, _, source=source, dc=dc, half=half, far=far):
                    near, dz = (k // zs, lax.rem(k, zs))
                    dy, dx = (far, near) if half == 0 else (near, far)
                    block = back(y, dy, ys) * cs + back(c, dc, cs)
                    block = (block * zs + dz) * xs + back(x, dx, xs)
                    for first, rows, out, column, lead_at in entries:
                        width = source.shape[-1]
                        pltpu.make_async_copy(
                            source.at[near, dz, pl.ds(first, rows), :],
                            outs[out].at[lead_at, block, :, pl.ds(column + half * width, width)],
                            sems.at[out],
                        ).start()
                    return 0

                lax.fori_loop(0, lead * zs, copy, 0)
    for out in range(n_out):
        pltpu.make_async_copy(outs[out], outs[out], sems.at[out]).wait()


def assemble(mine, other, entries, shapes, grid):
    sources = [b for part in mine for b in part] + [b for part in other for b in part]
    at = jnp.stack([lax.axis_index(axis) for axis in ("y", "core", "x")]).astype(jnp.int32)
    count = grid[0] * grid[1] * grid[2] * grid[3]
    outs = pl.pallas_call(
        functools.partial(assemble_kernel, entries, grid),
        out_shape=[jax.ShapeDtypeStruct((n, count, *shape), jnp.bfloat16) for n, *shape in shapes],
        in_specs=[pl.BlockSpec(memory_space=pltpu.SMEM)]
        + [pl.BlockSpec(memory_space=pl.ANY)] * len(sources),
        out_specs=[pl.BlockSpec(memory_space=pltpu.VMEM)] * len(shapes),
        scratch_shapes=[pltpu.SemaphoreType.DMA((len(shapes),))],
        compiler_params=pltpu.CompilerParams(vmem_limit_bytes=40 << 20),
    )(at, *sources)
    return [out.reshape(out.shape[0], -1, out.shape[-1]) for out in outs]


class Partial:
    def __init__(self, parts, first, deps=()):
        self.parts, self.first = (parts, first)
        self.sent, self.came = ([], [])
        for k in range(1, lax.axis_size("x")):
            blocks = [after(self.take(p, k), deps) for p in parts]
            self.sent += blocks
            self.came.append([cross(block, first, k) for block in blocks])

    def take(self, p, k):
        count = lax.axis_size("x")
        x, y = (lax.rem(lax.axis_index(axis) + k, count) for axis in ("x", "y"))
        core = lax.axis_index("core")
        if self.first:
            by_x = lax.dynamic_index_in_dim(p, x, 3, keepdims=False).transpose(2, 1, 0, 3, 4)
            by_y = lax.dynamic_index_in_dim(p, y, 0, keepdims=False).transpose(1, 0, 2, 3, 4)
            return jnp.where(core == 0, by_x, by_y)
        return lax.dynamic_index_in_dim(p, jnp.where(core == 0, y, x), 2, keepdims=False)

    def finish(self, deps=()):
        totals = [self.take(p, 0).astype(jnp.float32) for p in self.parts]
        for blocks in after(self.came, deps):
            totals = [total + block.astype(jnp.float32) for total, block in zip(totals, blocks)]
        return [total.astype(jnp.bfloat16) for total in totals]


def stacked(parts, width):
    cut = [p[..., j : j + width] for p in parts for j in range(0, p.shape[-1], width)]
    return jnp.concatenate(cut, axis=2)


def over_z_direct(total):
    count, at = (lax.axis_size("z"), lax.axis_index("z"))
    block = lambda k: lax.dynamic_index_in_dim(total, lax.rem(at + k, count), 0, keepdims=False)
    out = block(0).astype(jnp.float32)
    for k in range(1, count):
        route = [(i, (i + k) % count) for i in range(count)]
        out = out + lax.ppermute(block(k), "z", route).astype(jnp.float32)
    return out.astype(jnp.bfloat16)


def over_z(total):
    zs, cores, rows, columns = total.shape
    flat = total.reshape(zs * cores * rows, columns)
    return lax.psum_scatter(flat, "z", scatter_dimension=0, tiled=True).reshape(cores, rows, columns)


def to_owner(total):
    core = lax.axis_index("core")
    came = spread(lax.dynamic_index_in_dim(total, 1 - core, 0, keepdims=False), "core")[0]
    return in_order(lax.dynamic_index_in_dim(total, core, 0, keepdims=False), came)


def per_device(
    tokens,
    lengths,
    cotangent,
    first_gain,
    first_bias,
    mix_key,
    mix_value,
    mix_recept,
    time_decay,
    time_first,
    key_weight,
    value_weight,
    recept_weight,
    output_weight,
    second_gain,
    second_bias,
    shift_key,
    shift_recept,
    up_weight,
    gate_weight,
    down_weight,
):
    grid = tuple(lax.axis_size(axis) for axis in ALL)
    count = grid[0] * grid[1] * grid[2] * grid[3]
    seq_count, piece_len, channels = tokens.shape
    hidden = up_weight.shape[1]
    mine = channels // count
    blocks = hidden // channels

    vectors = (
        first_gain,
        first_bias,
        mix_key,
        mix_value,
        mix_recept,
        time_decay,
        time_first,
        second_gain,
        second_bias,
        shift_key,
        shift_recept,
    )
    n_vec = len(vectors)
    packed = jnp.pad(jnp.stack(vectors), ((0, 16 - n_vec), (0, channels - mine)))
    pieces = (
        [key_weight, value_weight, recept_weight, packed],
        [output_weight] + [up_weight[:, j * channels : (j + 1) * channels] for j in range(blocks)],
        [gate_weight, down_weight],
    )
    places = (
        [(0, 0, 0), (0, 0, 1), (0, 0, 2), (1, 0, 0)],
        [(0, 0, 0)] + [(1, j * channels, 0) for j in range(blocks)],
        [(0, 0, 0), (1, 0, 0)],
    )
    chunks = [jnp.concatenate(piece) for piece in pieces]
    plans = []
    for piece, place in zip(pieces, places):
        first, entries, shapes = (0, [], {})
        for part, (out, column, lead) in zip(piece, place):
            entries.append((first, part.shape[0], out, column, lead))
            shapes[out] = (lead + 1, part.shape[0], column + channels)
            first += part.shape[0]
        plans.append((entries, [shapes[o] for o in sorted(shapes)]))
    stepwise = mine % 16 == 0

    def whole(at):
        gathered = lax.all_gather(chunks[at], ALL, axis=0)
        entries, shapes = plans[at]
        outs = []
        for out, (leads, _, columns) in enumerate(shapes):
            parts = [gathered[:, f : f + r] for f, r, o, _, _ in entries if o == out]
            if leads == 1:
                parts = [jnp.concatenate(parts, axis=-1)]
            outs.append(jnp.stack([p.reshape(-1, columns) for p in parts]))
        return outs

    if stepwise:
        half = channels // 2
        xy2 = beside_xy((chunks[2][:, :half], chunks[2][:, half:]), ("x", "y"))
        z0 = beside_z(chunks[0])
        z1 = beside_z(after(chunks[1], z0))
        z2 = [lax.all_gather(jnp.stack(part), "z", axis=1) for part in after(xy2, z0)]
        xy0 = beside_xy(after(z0, xy2), ("x", "y"))
        yx0 = beside_xy([jnp.stack(part) for part in xy0], ("y", "x"))
        xy1 = beside_xy(after(z1, yx0), ("x", "y"))
        first_mats, vecs = assemble(yx0, other_core(yx0), *plans[0], grid)
    else:
        first_mats, vecs = whole(0)
    vecs = vecs.reshape(count, 16, channels)[:, :n_vec, :mine]
    vecs = jnp.moveaxis(vecs, 1, 0).reshape(n_vec, channels).astype(jnp.float32)
    (
        norm_gain,
        norm_bias,
        key_mix,
        value_mix,
        recept_mix,
        decay_log,
        boost_log_scale,
        gain_two,
        bias_two,
        chan_key_mix,
        chan_recept_mix,
    ) = (vecs[j] for j in range(n_vec))
    seq_index = lax.axis_index(SEQ)
    positions = seq_index * piece_len + jnp.arange(piece_len, dtype=jnp.int32)
    live_mask = (positions[None, :] < lengths[:, None]).astype(jnp.float32)[:, :, None]
    field = tokens.astype(jnp.float32)
    normed_one, inverse_one = norm_stats(field)
    fading_rate_vector = jnp.exp(decay_log)
    place = jnp.arange(piece_len, dtype=jnp.float32)[:, None]
    piece_fall = jnp.exp(-piece_len * fading_rate_vector)
    rows = jnp.stack([norm_gain, norm_bias, key_mix, value_mix, recept_mix, fading_rate_vector])
    ins, kvr, local, gap_one = first_projections(
        (seq_index > 0).astype(jnp.int32)[None], tokens, shifted(tokens[:, -1, :], SEQ, 1), rows, first_mats
    )
    if stepwise:
        pair = [jnp.stack(part) for part in after(xy1, (ins, local))]
        local = after(local, pair)
        yx1 = beside_xy(pair, ("y", "x"))
        core1 = other_core([[part[0]] for part in yx1])
    key_in, value_in, recept_in = ins
    lookup_matrix_output, content_matrix_output, recept_proj = kvr
    local = (local[0], local[1])
    starting_accumulator, starting_normalizer = entering(piece_fall, local, False)
    if stepwise:
        starting_accumulator, starting_normalizer = after(
            (starting_accumulator, starting_normalizer), (yx1, core1, z2)
        )
    state_a, state_b, mixed_out = wkv_forward(
        kvr,
        starting_accumulator,
        starting_normalizer,
        boost_log_scale,
        fading_rate_vector,
    )
    if stepwise:
        yx2 = beside_xy(after(tuple(z2), yx1), ("y", "x"))
        rest1 = other_core([part[1:] for part in yx1])
        core1 = [one + rest for one, rest in zip(core1, rest1)]
        yx1 = after(yx1, (state_a, state_b))
        (output_mat,), (up_mat,) = assemble(yx1, core1, *plans[1], grid)
    else:
        (output_mat,), (up_mat,) = whole(1)
    branch = matmul("nlc,cd->nld", mixed_out, output_mat)
    residual = field + branch
    normed_two_raw, inverse_two = norm_stats(residual)
    normed_two = normed_two_raw * gain_two + bias_two
    before_two = previous_rows(normed_two)
    ffn_key = (normed_two * chan_key_mix + before_two * (1.0 - chan_key_mix)).astype(jnp.bfloat16)
    ffn_recept = (normed_two * chan_recept_mix + before_two * (1.0 - chan_recept_mix)).astype(
        jnp.bfloat16
    )
    flat_key = ffn_key.reshape(seq_count * piece_len, channels)
    relu_up = jax.nn.relu(jnp.dot(flat_key, up_mat, preferred_element_type=jnp.float32))
    squared, relu_up = (jnp.square(relu_up).astype(jnp.bfloat16), relu_up.astype(jnp.bfloat16))
    if stepwise:
        core2 = other_core([[part] for part in after(tuple(z2), (ffn_key, ffn_recept))])
        yx2 = after(yx2, (squared, relu_up, core2))
        rest2 = other_core([part[1:] for part in yx2])
        core2 = [one + rest for one, rest in zip(core2, rest2)]
        (gate_mat,), (down_mat,) = assemble(yx2, core2, *plans[2], grid)
    else:
        (gate_mat,), (down_mat,) = whole(2)
    squared = squared.reshape(seq_count, piece_len, hidden)
    down_proj = matmul("nlf,fd->nld", squared, down_mat)
    gate_value = jax.nn.sigmoid(matmul("nlc,cd->nld", ffn_recept, gate_mat))
    output = ((residual + gate_value * down_proj) * live_mask).astype(jnp.bfloat16)

    def outer(left, right):
        return jnp.einsum("nlc,nld->cd", left, right, preferred_element_type=jnp.float32)

    def to_core(left, right):
        send = outer(left, own_half(right, False)).astype(jnp.bfloat16)
        return send, spread(send, "core")[0]

    def both_cores(left, right, came):
        rows = outer(left, own_half(right)) + came.astype(jnp.float32)
        return rows.astype(jnp.bfloat16).reshape(*grid, -1, rows.shape[-1])

    seed = cotangent.astype(jnp.float32) * live_mask
    down_grad = (seed * gate_value).astype(jnp.bfloat16)
    gate_grad = (seed * down_proj * gate_value * (1.0 - gate_value)).astype(jnp.bfloat16)
    width = channels // 2
    down_send, down_came = to_core(squared, down_grad)
    gate_send, gate_came = to_core(ffn_recept, gate_grad)
    ffn_recept_grad = matmul("nld,cd->nlc", after(gate_grad, (down_send, gate_send)), gate_mat)
    late = (down_grad, gate_grad, down_came, gate_came)
    d_grad, g_grad, down_came, gate_came = after(late, ffn_recept_grad)
    way1 = Partial([both_cores(squared, d_grad, down_came), both_cores(ffn_recept, g_grad, gate_came)], True)
    flat = (seq_count * piece_len, -1)
    up_grad, ffn_key_grad = ffn_backward(
        after(down_grad, way1.sent).reshape(flat), relu_up, down_mat, up_mat
    )
    up_grad = up_grad.reshape(seq_count, piece_len, hidden)
    ffn_key_grad = ffn_key_grad.reshape(tokens.shape)
    up_send, up_came = to_core(ffn_key, up_grad)
    u_grad, up_came = after((up_grad, up_came), up_send)
    grad_up_part = both_cores(ffn_key, u_grad, up_came)
    normed_two_grad = (
        ffn_key_grad * chan_key_mix
        + ffn_recept_grad * chan_recept_mix
        + next_rows(ffn_key_grad * (1.0 - chan_key_mix) + ffn_recept_grad * (1.0 - chan_recept_mix))
    )
    gap_two = normed_two - before_two
    grad_chan_key = jnp.sum(ffn_key_grad * gap_two, axis=(0, 1))
    grad_chan_recept = jnp.sum(ffn_recept_grad * gap_two, axis=(0, 1))
    grad_gain_two = jnp.sum(normed_two_grad * normed_two_raw, axis=(0, 1))
    grad_bias_two = jnp.sum(normed_two_grad, axis=(0, 1))
    residual_grad = seed + norm_back(normed_two_grad * gain_two, normed_two_raw, inverse_two)
    branch_grad = residual_grad.astype(jnp.bfloat16)
    back1 = Partial(way1.finish(deps=(branch_grad,)), False)
    branch_grad = after(branch_grad, back1.sent)
    mixed_grad = matmul("nld,cd->nlc", branch_grad, output_mat)
    out_send, out_came = to_core(mixed_out, branch_grad)
    bonus = jnp.exp(boost_log_scale) * jnp.exp(lookup_matrix_output)
    over = 1.0 / (state_b + bonus)
    blended = (state_a + bonus * content_matrix_output) * over
    recept_sig = jax.nn.sigmoid(recept_proj)
    recept_grad = (mixed_grad * blended * recept_sig * (1.0 - recept_sig)).astype(jnp.bfloat16)
    alpha = mixed_grad * recept_sig * over * jnp.exp(-place * fading_rate_vector)
    local = (jnp.sum(alpha, axis=1), -jnp.sum(alpha * blended, axis=1))
    carry_p, carry_q = entering(piece_fall, local, True)
    z1 = over_z(stacked(back1.finish(), width))
    recept_send, recept_came = to_core(recept_in, recept_grad)
    g_out, g_recept, out_came, recept_came = after((branch_grad, recept_grad, out_came, recept_came), recept_send)
    part_out = both_cores(mixed_out, g_out, out_came)
    part_recept = both_cores(recept_in, g_recept, recept_came)
    way2 = Partial([grad_up_part, part_out, part_recept], True, deps=back1.came)
    carry_p, carry_q = after((carry_p, carry_q), way2.sent)
    key_grad, value_grad, grad_decay, boost_adjoint_term = wkv_backward(
        kvr,
        state_a,
        state_b,
        mixed_grad,
        carry_p,
        carry_q,
        boost_log_scale,
        fading_rate_vector,
    )
    key_send, key_came = to_core(key_in, key_grad)
    value_send, value_came = to_core(value_in, value_grad)
    late = (key_grad, value_grad, key_came, value_came)
    back2 = Partial(way2.finish(deps=(key_send, value_send)), False)
    k_grad, v_grad, key_came, value_came = after(late, back2.sent)
    part_key = both_cores(key_in, k_grad, key_came)
    part_value = both_cores(value_in, v_grad, value_came)
    way3 = Partial([part_key, part_value], True, deps=back2.came)
    z2 = over_z(stacked(back2.finish(deps=way3.sent), width))
    flat = (seq_count * piece_len, channels)
    grads = [g.reshape(flat) for g in after((k_grad, v_grad, recept_grad), (part_key, part_value))]
    mixes = jnp.stack([key_mix, value_mix, recept_mix])
    now_part, next_part, grad_mixes = input_gradients(grads, gap_one, mixes, first_mats)
    back3 = Partial(way3.finish(), False)
    now_part, next_part = after((now_part, next_part), way3.sent)
    normed_grad = now_part.reshape(tokens.shape) + next_rows(next_part.reshape(tokens.shape))
    grad_key_mix, grad_value_mix, grad_recept_mix = grad_mixes
    grad_gain_one = jnp.sum(normed_grad * normed_one, axis=(0, 1))
    grad_bias_one = jnp.sum(normed_grad, axis=(0, 1))
    tokens_grad = residual_grad + norm_back(normed_grad * norm_gain, normed_one, inverse_one)
    sums = jnp.concatenate(
        [
            grad_gain_one,
            grad_bias_one,
            grad_key_mix,
            grad_value_mix,
            grad_recept_mix,
            grad_decay,
            boost_adjoint_term,
            grad_gain_two,
            grad_bias_two,
            grad_chan_key,
            grad_chan_recept,
        ]
    )
    for axis in ("core", "x", "y", "z"):
        sums = sums + sum(spread(sums, axis))
    sums = lax.dynamic_slice_in_dim(sums.reshape(n_vec, channels), lax.axis_index(ALL) * mine, mine, 1)
    z3 = over_z_direct(stacked(back3.finish(), width))
    first, second, third = (to_owner(z) for z in (z1, z2, z3))

    def rows_of(pair, at, rows=mine, columns=1):
        cut = [h[at + j * rows : at + (j + 1) * rows] for h in pair for j in range(columns)]
        return jnp.concatenate(cut, axis=1).astype(jnp.float32)

    return (
        output,
        tokens_grad,
        *(sums[j] for j in range(7)),
        rows_of(third, 0),
        rows_of(third, mine),
        rows_of(second, (blocks + 1) * mine),
        rows_of(second, blocks * mine),
        *(sums[j] for j in range(7, n_vec)),
        rows_of(second, 0, columns=blocks),
        rows_of(first, hidden // count),
        rows_of(first, 0, hidden // count),
    )


def solution(mesh):
    seq, dp = (mesh.shape["seq"], mesh.shape["dp"])
    wide = len({device.coords[0] for device in mesh.devices.reshape(-1)})
    fine = jax.sharding.Mesh(mesh.devices.reshape(seq // 2, 2, dp // wide, wide), ALL)
    field, vector, matrix = (P(DP, SEQ, None), P(ALL), P(ALL, None))
    return jax.shard_map(
        per_device,
        mesh=fine,
        in_specs=(field, P(DP), field) + (vector,) * 7 + (matrix,) * 4 + (vector,) * 4 + (matrix,) * 3,
        out_specs=(field, field) + (vector,) * 7 + (matrix,) * 4 + (vector,) * 4 + (matrix,) * 3,
        check_vma=False,
    )
```

profile of v0, /device:TPU:9, one launch (start us, length us, event | category | flops | bytes accessed | tf_op | source)
XLA Modules:
  0.0 450.4 jit_solution(10362731761811518789)
XLA Ops:
  14.1 17.6 %all-gather = bf16[448,1024]{1,0:T(8,128)(2,1)S(1)} all-gather(bf16[112,1024]{1,0:T(8,128)(2,1)S(1)} %fusion.93), channel_id=2, replica_groups=mesh['y'=2,'core'=2,'z'=4,'x'=2] {'z'}, dimensions={0}, use_global_device_ids=true | all-gather | bytes 1146880 | tf_op jit(solution)/shard_map/all_gather | solution.py:412
  34.6 7.3 %collective-permute-done.5 = bf16[4,112,512]{2,1,0:T(8,128)(2,1)S(1)} collective-permute-done((bf16[4,112,512]{2,1,0:T(8,128)(2,1)S(1)}, bf16[4,112,512]{2,1,0:T(8,128)(2,1)S(1)}, u32[]{:S(2)}, u32[]{:S(2)}) %collective-permute-start.5) | collective-permute-done | bytes 458784 | tf_op jit(solution)/shard_map/ppermute | solution.py:392
  45.7 4.0 collective-permute-start.9
  49.7 12.8 %collective-permute-done.6.refs_3_ = bf16[2,4,112,512]{3,2,1,0:T(8,128)(2,1)} collective-permute-done((bf16[2,4,112,512]{3,2,1,0:T(8,128)(2,1)S(1)}, bf16[2,4,112,512]{3,2,1,0:T(8,128)(2,1)}, u32[]{:S(2)}, u32[]{:S(2)}) %collective-permute-start.6) | collective-permute-done | bytes 917536 | tf_op jit(solution)/shard_map/ppermute | solution.py:392
  62.5 4.4 collective-permute-start.10
  70.2 2.2 fusion.107
  74.9 3.5 collective-permute-start
  78.5 6.8 %shard_map.356 = (bf16[3,32,32,1024]{3,2,1,0:T(8,128)(2,1)}, bf16[1,32,16,1024]{3,2,1,0:T(8,128)(2,1)S(1)}) custom-call(s32[3]{0:T(128)S(1)} %pad_add_fusion.at_ref, bf16[2,4,112,512]{3,2,1,0:T(8,128)(2,1)S(1)} %pad_maximum_fusion.5.refs_0_, bf16[2,4,112,512]{3,2,1,0:T(8,128)(2,1)} %collective-permute-done.4.refs_1_, ...), custom_call_target="tpu_custom_call" | custom-call | tf_op jit(solution)/shard_map/pallas_call | solution.py:463
  88.0 10.1 %shard_map.357 = (bf16[2,256,1024]{2,1,0:T(8,128)(2,1)S(1)}, bf16[2,256,1024]{2,1,0:T(8,128)(2,1)S(1)}, bf16[2,256,1024]{2,1,0:T(8,128)(2,1)S(1)}, f32[3,2,256,1...) custom-call(s32[1]{0:T(128)} %bitcast.flag_ref, bf16[2,256,1024]{2,1,0:T(8,128)(2,1)S(1)} %copy-done.1, ...), custom_call_target="tpu_custom_call" | custom-call | flops 1048576 | bytes 65536 | tf_op jit(solution)/shard_map/pallas_call | solution.py:193
  99.1 2.2 pad_maximum_fusion.3.refs_2_
  101.6 2.3 pad_maximum_fusion.2.refs_0_
  104.7 3.2 collective-permute-start.18
  108.0 22.9 %collective-permute-done.16.refs_3_ = bf16[2,4,160,512]{3,2,1,0:T(8,128)(2,1)} collective-permute-done((bf16[2,4,160,512]{3,2,1,0:T(8,128)(2,1)S(1)}, bf16[2,4,160,512]{3,2,1,0:T(8,128)(2,1)}, u32[]{:S(2)}, u32[]{:S(2)}) %collective-permute-start.16) | collective-permute-done | bytes 1310752 | tf_op jit(solution)/shard_map/ppermute | solution.py:392
  131.0 2.4 collective-permute-done.15.refs_1_
  133.4 2.0 collective-permute-start.19
  135.5 2.4 collective-permute-done.13
  138.0 1.9 collective-permute-start.14
  140.9 2.8 copy-done
  143.6 4.7 %shard_map.358 = (f32[2,256,1024]{2,1,0:T(8,128)S(1)}, f32[2,256,1024]{2,1,0:T(8,128)S(1)}, bf16[2,256,1024]{2,1,0:T(8,128)(2,1)S(1)}) custom-call(f32[3,2,256,1024]{3,2,1,0:T(8,128)S(1)} %copy-done, f32[3,2,256,1024]{3,2,1,0:T(8,128)S(1)} %copy-done, f32[3,2,256,1024]{3,2,1,0:T(8,128)S(1)} %copy-done, f32[2,1024]{1,0:T(2,128)S(1)} %get-tuple-element.130.a0_ref, ...), custom_call_target="tpu_custom_call" | custom-call | flops 1048576 | bytes 65536 | tf_op jit(solution)/shard_map/pallas_call | solution.py:313
  151.1 7.8 %shard_map.359 = (bf16[1,32,32,1024]{3,2,1,0:T(8,128)(2,1)S(1)}, bf16[1,32,32,4096]{3,2,1,0:T(8,128)(2,1)}) custom-call(s32[3]{0:T(128)S(1)} %pad_add_fusion.at_ref, bf16[2,4,160,512]{3,2,1,0:T(8,128)(2,1)} %pad_maximum_fusion.2.refs_0_, bf16[2,4,160,512]{3,2,1,0:T(8,128)(2,1)} %collective-permute-done.15.refs_1_, ...), custom_call_target="tpu_custom_call" | custom-call | tf_op jit(solution)/shard_map/pallas_call | solution.py:463
  161.1 5.4 %collective-permute-start.21 = (f32[2,1024]{1,0:T(2,128)S(1)}, f32[2,1024]{1,0:T(2,128)S(1)}, u32[]{:S(2)}, u32[]{:S(2)}) collective-permute-start(f32[2,1024]{1,0:T(2,128)S(1)} %bitcast.514), channel_id=1, source_target_pairs={{0,8},{8,16},{16,24},{1,9},{9,17},{17,25},{2,10},{10,18},{18,26},{... | collective-permute-start | bytes 24584 | tf_op jit(solution)/shard_map/ppermute | solution.py:347
  167.9 2.3 add_convert_fusion.2
  171.0 6.0 %multiply_convert_fusion = (bf16[512,4096]{1,0:T(8,128)(2,1)}, bf16[512,4096]{1,0:T(8,128)(2,1)S(1)}) fusion(bf16[512,1024]{1,0:T(8,128)(2,1)S(1)} %bitcast.496, bf16[1024,4096]{1,0:T(8,128)(2,1)S(1)} %bitcast.471), kind=kOutput, calls=%fused_computation.6 | convolution fusion | flops 4303355904 | bytes 17825792 | tf_op jit(solution)/shard_map/dot_general | solution.py:682
  177.1 3.0 maximum_convert_fusion.relu_ref
  180.1 16.4 %collective-permute-done.22.refs_1_ = bf16[2,4,160,512]{3,2,1,0:T(8,128)(2,1)} collective-permute-done((bf16[2,4,160,512]{3,2,1,0:T(8,128)(2,1)S(1)}, bf16[2,4,160,512]{3,2,1,0:T(8,128)(2,1)}, u32[]{:S(2)}, u32[]{:S(2)}) %collective-permute-start.22) | collective-permute-done | bytes 1310752 | tf_op jit(solution)/shard_map/ppermute | solution.py:392
  200.2 2.9 collective-permute-done.26.refs_5_
  203.1 1.9 collective-permute-done.27.refs_7_
  209.0 7.3 %shard_map.360 = (bf16[1,32,32,1024]{3,2,1,0:T(8,128)(2,1)S(1)}, bf16[1,32,128,1024]{3,2,1,0:T(8,128)(2,1)}) custom-call(s32[3]{0:T(128)S(1)} %pad_add_fusion.at_ref, bf16[2,4,160,512]{3,2,1,0:T(8,128)(2,1)S(1)} %bitcast.441, bf16[2,4,160,512]{3,2,1,0:T(8,128)(2,1)} %collective-permute-done.22.refs_1_, bf16[2,4,160,512]{3,2,1,0:T(8,128)(2,1)S(1)} %bitcast.444, ...), custom_call_target="tpu_custom_call" | custom-call | tf_op jit(solution)/shard_map/pallas_call | solution.py:463
  216.3 7.7 %fusion.114 = f32[2,256,1024]{2,1,0:T(8,128)S(1)} fusion(bf16[2,256,4096]{2,1,0:T(8,128)(2,1)S(1)} %bitcast.530, bf16[4096,1024,1]{1,0,2:T(8,128)(2,1)} %bitcast.472), kind=kOutput, calls=%fused_computation.326 | convolution fusion | flops 4294967296 | bytes 14680064 | tf_op jit(solution)/shard_map/nlf,fd->nld/dot_general | solution.py:341
  224.1 3.1 multiply_convert_fusion.1
  227.2 4.6 %bitcast_convert_fusion.1 = bf16[4096,512]{1,0:T(8,128)(2,1)} fusion(bf16[2,256,4096]{2,1,0:T(8,128)(2,1)S(1)} %bitcast.531, bf16[2,256,1024]{2,1,0:T(8,128)(2,1)S(1)} %get-tuple-element.156, pred[]{:T(512)S(6)} %eq.7), kind=kOutput, calls=%fused_computation.5 | convolution fusion | flops 2149842944 | bytes 9437185 | tf_op jit(solution)/shard_map/nlc,nld->cd/dot_general | solution.py:698
  232.4 1.8 bitcast_convert_fusion.6
  237.1 3.3 fusion.115
  240.8 2.1 fusion.26
  243.0 5.1 %fusion.1 = bf16[4096,512]{1,0:T(8,128)(2,1)S(1)} fusion(bf16[4096,512]{1,0:T(8,128)(2,1)} %collective-permute-done.28, bf16[2,256,4096]{2,1,0:T(8,128)(2,1)S(1)} %bitcast.532, bf16[2,256,1024]{2,1,0:T(8,128)(2,1)S(1)} %get-tuple-element.156, pred[]{:T(512)S(6)} %eq.6), kind=kOutput, calls=%fused_computation.4 | convolution fusion | flops 2154037248 | bytes 13631489 | tf_op jit(solution)/shard_map/nlc,nld->cd/dot_general | solution.py:698
  248.2 1.8 constant_dynamic-slice_fusion.1
  253.8 13.5 %shard_map.361 = (bf16[512,4096]{1,0:T(8,128)(2,1)S(1)}, f32[512,1024]{1,0:T(8,128)S(1)}) custom-call(bf16[512,1024]{1,0:T(8,128)(2,1)S(1)} %bitcast.448, bf16[512,4096]{1,0:T(8,128)(2,1)S(1)} %copy-done.2, bf16[4096,1024]{1,0:T(8,128)(2,1)} %bitcast.473, bf16[1024,4096]{1,0:T(8,128)(2,1)} %bitcast.468), custom_call_target="tpu_custom_call" | custom-call | flops 1048576 | bytes 25165824 | tf_op jit(solution)/shard_map/pallas_call | solution.py:236
  270.4 3.2 collective-permute-start.30
  273.6 4.5 bitcast_convert_fusion
  281.2 2.3 collective-permute-done.32
  283.5 2.8 add_convert_fusion.1
  288.6 5.7 %fusion.25 = (bf16[2,256,1024]{2,1,0:T(8,128)(2,1)S(1)}, f32[2,256,1024]{2,1,0:T(8,128)S(1)}, f32[2,256,1024]{2,1,0:T(8,128)S(1)}, f32[2,256,1024]{2,1,0:T(8,128)}) fusion(f32[3,2,256,1024]{3,2,1,0:T(8,128)} %get-tuple-element.113.k_ref.v_ref.r_ref, f32[2,256,1024]{2,1,0:T(8,128)S(1)} %copy-done.6, f32[2,256,1024]{2,1,0:T(8,128)S(1)} %copy-done.4, ...), kind=kOutput, calls=%fused_computation.60 | convolution fusion | flops 1082654720 | bytes 22024192 | tf_op jit(solution)/shard_map/nld,cd->nlc/dot_general | solution.py:341
  299.4 1.8 bitcast_convert_fusion.4
  303.1 2.5 collective-permute-start.38
  308.3 6.2 %fusion = bf16[1024,2048]{1,0:T(8,128)(2,1)S(1)} fusion(bf16[1024,2048]{1,0:T(8,128)(2,1)} %collective-permute-done.35, bf16[2,256,1024]{2,1,0:T(8,128)(2,1)} %copy-done.69, bf16[2,256,4096]{2,1,0:T(8,128)(2,1)} %bitcast.453, pred[]{:T(512)S(6)} %eq.6), kind=kOutput, calls=%fused_computation.1 | convolution fusion | flops 2154823680 | bytes 13631489 | tf_op jit(solution)/shard_map/nlc,nld->cd/dot_general | solution.py:698
  314.4 2.0 dynamic-slice_bitcast_fusion
  319.4 2.1 fusion.19
  323.3 2.3 fusion.18
  329.2 6.3 %shard_map.362 = (bf16[2,256,1024]{2,1,0:T(8,128)(2,1)S(1)}, bf16[2,256,1024]{2,1,0:T(8,128)(2,1)S(1)}, f32[1,1024]{1,0:T(1,128)S(1)}, f32[1,1024]{1,0:T(1,128)S(1)}) custom-call(f32[3,2,256,1024]{3,2,1,0:T(8,128)S(1)} %bitcast.434, f32[3,2,256,1024]{3,2,1,0:T(8,128)S(1)} %bitcast.434, f32[3,2,256,1024]{3,2,1,0:T(8,128)S(1)} %bitcast.434, ...), custom_call_target="tpu_custom_call" | custom-call | flops 1048576 | bytes 65536 | tf_op jit(solution)/shard_map/pallas_call | solution.py:327
  337.5 1.8 bitcast_convert_fusion.2
  340.2 1.8 collective-permute-start.64
  345.1 4.8 %collective-permute-done.44 = bf16[4,2,2,32,512]{4,3,0,1,2:T(8,128)(2,1)} collective-permute-done((bf16[4,2,2,32,512]{4,3,0,1,2:T(8,128)(2,1)}, bf16[4,2,2,32,512]{4,3,0,1,2:T(8,128)(2,1)}, u32[]{:S(2)}, u32[]{:S(2)}) %collective-permute-start.44) | collective-permute-done | bytes 524320 | tf_op jit(solution)/shard_map/ppermute | solution.py:407
  349.8 5.6 %collective-permute-done.43 = bf16[4,2,2,32,512]{4,3,0,1,2:T(8,128)(2,1)} collective-permute-done((bf16[4,2,2,32,512]{4,3,0,1,2:T(8,128)(2,1)}, bf16[4,2,2,32,512]{4,3,0,1,2:T(8,128)(2,1)}, u32[]{:S(2)}, u32[]{:S(2)}) %collective-permute-start.43) | collective-permute-done | bytes 524320 | tf_op jit(solution)/shard_map/ppermute | solution.py:407
  358.1 2.7 add_convert_fusion
  367.6 7.2 %shard_map.363 = (f32[512,1024]{1,0:T(8,128)S(1)}, f32[512,1024]{1,0:T(8,128)S(1)}, f32[3,1024]{1,0:T(4,128)S(1)}) custom-call(bf16[512,1024]{1,0:T(8,128)(2,1)S(1)} %bitcast.446, bf16[512,1024]{1,0:T(8,128)(2,1)S(1)} %bitcast.447, bf16[512,1024]{1,0:T(8,128)(2,1)S(1)} %bitcast.445, f32[512,1024]{1,0:T(8,128)S(1)} %copy-done.9, ...), custom_call_target="tpu_custom_call" | custom-call | flops 1048576 | bytes 8388608 | tf_op jit(solution)/shard_map/pallas_call | solution.py:280
  380.4 3.7 collective-permute-start.48
  387.3 2.6 fusion.11
  397.1 1.8 add_convert_fusion.4
  402.4 3.9 fusion.10
  410.0 3.7 collective-permute-start.60
  414.3 5.3 %collective-permute-done.54 = f32[11264]{0:T(1024)S(1)} collective-permute-done((f32[11264]{0:T(1024)S(1)}, f32[11264]{0:T(1024)S(1)}, u32[]{:S(2)}, u32[]{:S(2)}) %collective-permute-start.54) | collective-permute-done | bytes 45088 | tf_op jit(solution)/shard_map/ppermute | solution.py:392
  419.7 5.6 %collective-permute-done.59 = bf16[2,64,512]{2,1,0:T(8,128)(2,1)S(1)} collective-permute-done((bf16[2,64,512]{2,1,0:T(8,128)(2,1)S(1)}, bf16[2,64,512]{2,1,0:T(8,128)(2,1)S(1)}, u32[]{:S(2)}, u32[]{:S(2)}) %collective-permute-start.59) | collective-permute-done | bytes 131104 | tf_op jit(solution)/shard_map/ppermute | solution.py:512
  425.3 8.2 %collective-permute-done.60 = bf16[2,64,512]{2,1,0:T(8,128)(2,1)S(1)} collective-permute-done((bf16[2,64,512]{2,1,0:T(8,128)(2,1)S(1)}, bf16[2,64,512]{2,1,0:T(8,128)(2,1)S(1)}, u32[]{:S(2)}, u32[]{:S(2)}) %collective-permute-start.60) | collective-permute-done | bytes 131104 | tf_op jit(solution)/shard_map/ppermute | solution.py:512
  433.5 2.2 collective-permute-done.61
  (481 shorter events, 120.1 us)
Async XLA Ops:
  7.2 63.0 %all-gather.8.cloned.1.call-start = ((), (), s32[]{:S(2)}) async-start(), calls=%async_computation.4 | async-start | bytes 1638400 | tf_op jit(solution)/shard_map/all_gather | solution.py:412
  9.1 22.7 %collective-permute-start.1 = (bf16[160,512]{1,0:T(8,128)(2,1)S(1)}, bf16[160,512]{1,0:T(8,128)(2,1)S(1)}, u32[]{:S(2)}, u32[]{:S(2)}) collective-permute-start(bf16[160,512]{1,0:T(8,128)(2,1)S(1)} %get-tuple-element.126), channel_id=1, source_target_pairs={{0,1},{1,0},{2,3},{3,2},{4,5},{5,4},{6,7},{7,6},{8,9},{9,8},{10,11... | collective-permute-start | bytes 491528 | tf_op jit(solution)/shard_map/ppermute | solution.py:392
  10.4 21.4 %collective-permute-start.2 = (bf16[160,512]{1,0:T(8,128)(2,1)S(1)}, bf16[160,512]{1,0:T(8,128)(2,1)S(1)}, u32[]{:S(2)}, u32[]{:S(2)}) collective-permute-start(bf16[160,512]{1,0:T(8,128)(2,1)S(1)} %get-tuple-element.128), channel_id=1, source_target_pairs={{0,16},{16,0},{1,17},{17,1},{2,18},{18,2},{3,19},{19,3},{4,20},{20... | collective-permute-start | bytes 491528 | tf_op jit(solution)/shard_map/ppermute | solution.py:392
  32.5 9.5 %collective-permute-start.5 = (bf16[4,112,512]{2,1,0:T(8,128)(2,1)S(1)}, bf16[4,112,512]{2,1,0:T(8,128)(2,1)S(1)}, u32[]{:S(2)}, u32[]{:S(2)}) collective-permute-start(bf16[4,112,512]{2,1,0:T(8,128)(2,1)S(1)} %get-tuple-element.110), channel_id=1, source_target_pairs={{0,16},{16,0},{1,17},{17,1},{2,18},{18,2},{3,19},{19,3},{4,20},{20... | collective-permute-start | bytes 1376264 | tf_op jit(solution)/shard_map/ppermute | solution.py:392
  32.7 11.6 %collective-permute-start.3 = (bf16[4,112,512]{2,1,0:T(8,128)(2,1)S(1)}, bf16[4,112,512]{2,1,0:T(8,128)(2,1)}, u32[]{:S(2)}, u32[]{:S(2)}) collective-permute-start(bf16[4,112,512]{2,1,0:T(8,128)(2,1)S(1)} %get-tuple-element.109), channel_id=1, source_target_pairs={{0,1},{1,0},{2,3},{3,2},{4,5},{5,4},{6,7},{7,6},{8,9},{9,8},{10,11... | collective-permute-start | bytes 1376264 | tf_op jit(solution)/shard_map/ppermute | solution.py:392
  34.6 106.2 %all-gather.10.cloned.1.call-start = ((), (), s32[]{:S(2)}) async-start(), calls=%async_computation.5 | async-start | bytes 1638400 | tf_op jit(solution)/shard_map/all_gather | solution.py:610
  43.9 18.5 %collective-permute-start.6 = (bf16[2,4,112,512]{3,2,1,0:T(8,128)(2,1)S(1)}, bf16[2,4,112,512]{3,2,1,0:T(8,128)(2,1)}, u32[]{:S(2)}, u32[]{:S(2)}) collective-permute-start(bf16[2,4,112,512]{3,2,1,0:T(8,128)(2,1)S(1)} %pad_maximum_fusion.6.refs_2_), channel_id=1, source_target_pairs={{0,1},{1,0},{2,3},{3,2},{4,5},{5,4},{6,7},{7,6},{8,9},{9,8},{10,11... | collective-permute-start | bytes 2752520 | tf_op jit(solution)/shard_map/ppermute | solution.py:392
  45.4 21.5 %collective-permute-start.4 = (bf16[2,4,112,512]{3,2,1,0:T(8,128)(2,1)S(1)}, bf16[2,4,112,512]{3,2,1,0:T(8,128)(2,1)}, u32[]{:S(2)}, u32[]{:S(2)}) collective-permute-start(bf16[2,4,112,512]{3,2,1,0:T(8,128)(2,1)S(1)} %pad_maximum_fusion.5.refs_0_), channel_id=1, source_target_pairs={{0,16},{16,0},{1,17},{17,1},{2,18},{18,2},{3,19},{19,3},{4,20},{20... | collective-permute-start | bytes 2752520 | tf_op jit(solution)/shard_map/ppermute | solution.py:392
  45.7 28.0 %collective-permute-start.9 = (bf16[2,4,112,512]{3,2,1,0:T(8,128)(2,1)S(1)}, bf16[2,4,112,512]{3,2,1,0:T(8,128)(2,1)}, u32[]{:S(2)}, u32[]{:S(2)}) collective-permute-start(bf16[2,4,112,512]{3,2,1,0:T(8,128)(2,1)S(1)} %pad_maximum_fusion.6.refs_2_), channel_id=1, source_target_pairs={{0,8},{8,0},{1,9},{9,1},{2,10},{10,2},{3,11},{11,3},{4,12},{12,4},... | collective-permute-start | bytes 2752520 | tf_op jit(solution)/shard_map/ppermute | solution.py:392
  49.7 25.2 %collective-permute-start.7 = (bf16[2,4,112,512]{3,2,1,0:T(8,128)(2,1)S(1)}, bf16[2,4,112,512]{3,2,1,0:T(8,128)(2,1)}, u32[]{:S(2)}, u32[]{:S(2)}) collective-permute-start(bf16[2,4,112,512]{3,2,1,0:T(8,128)(2,1)S(1)} %pad_maximum_fusion.5.refs_0_), channel_id=1, source_target_pairs={{0,8},{8,0},{1,9},{9,1},{2,10},{10,2},{3,11},{11,3},{4,12},{12,4},... | collective-permute-start | bytes 2752520 | tf_op jit(solution)/shard_map/ppermute | solution.py:392
  62.5 16.0 %collective-permute-start.10 = (bf16[2,4,112,512]{3,2,1,0:T(8,128)(2,1)}, bf16[2,4,112,512]{3,2,1,0:T(8,128)(2,1)}, u32[]{:S(2)}, u32[]{:S(2)}) collective-permute-start(bf16[2,4,112,512]{3,2,1,0:T(8,128)(2,1)} %collective-permute-done.6.refs_3_), channel_id=1, source_target_pairs={{0,8},{8,0},{1,9},{9,1},{2,10},{10,2},{3,11},{11,3},{4,12},{12,4},... | collective-permute-start | bytes 2752520 | tf_op jit(solution)/shard_map/ppermute | solution.py:392
  66.9 11.6 %collective-permute-start.8 = (bf16[2,4,112,512]{3,2,1,0:T(8,128)(2,1)}, bf16[2,4,112,512]{3,2,1,0:T(8,128)(2,1)}, u32[]{:S(2)}, u32[]{:S(2)}) collective-permute-start(bf16[2,4,112,512]{3,2,1,0:T(8,128)(2,1)} %collective-permute-done.4.refs_1_), channel_id=1, source_target_pairs={{0,8},{8,0},{1,9},{9,1},{2,10},{10,2},{3,11},{11,3},{4,12},{12,4},... | collective-permute-start | bytes 2752520 | tf_op jit(solution)/shard_map/ppermute | solution.py:392
  69.1 71.7 %all-gather.12.cloned.1.call-start = ((), (), s32[]{:S(2)}) async-start(), calls=%async_computation.6 | async-start | bytes 1638400 | tf_op jit(solution)/shard_map/all_gather | solution.py:610
  72.5 26.6 %collective-permute-start.11 = (bf16[4,160,512]{2,1,0:T(8,128)(2,1)S(1)}, bf16[4,160,512]{2,1,0:T(8,128)(2,1)}, u32[]{:S(2)}, u32[]{:S(2)}) collective-permute-start(bf16[4,160,512]{2,1,0:T(8,128)(2,1)S(1)} %get-tuple-element.121), channel_id=1, source_target_pairs={{0,1},{1,0},{2,3},{3,2},{4,5},{5,4},{6,7},{7,6},{8,9},{9,8},{10,11... | collective-permute-start | bytes 1966088 | tf_op jit(solution)/shard_map/ppermute | solution.py:392
  73.7 25.4 %collective-permute-start.12 = (bf16[4,160,512]{2,1,0:T(8,128)(2,1)}, bf16[4,160,512]{2,1,0:T(8,128)(2,1)}, u32[]{:S(2)}, u32[]{:S(2)}) collective-permute-start(bf16[4,160,512]{2,1,0:T(8,128)(2,1)} %get-tuple-element.123), channel_id=1, source_target_pairs={{0,16},{16,0},{1,17},{17,1},{2,18},{18,2},{3,19},{19,3},{4,20},{20... | collective-permute-start | bytes 1966088 | tf_op jit(solution)/shard_map/ppermute | solution.py:392
  74.9 13.1 %collective-permute-start = (bf16[2,1024]{1,0:T(2,128)(2,1)S(1)}, bf16[2,1024]{1,0:T(2,128)(2,1)S(1)}, u32[]{:S(2)}, u32[]{:S(2)}) collective-permute-start(bf16[2,1024]{1,0:T(2,128)(2,1)S(1)} %bitcast.517), channel_id=1, source_target_pairs={{0,8},{8,16},{16,24},{1,9},{9,17},{17,25},{2,10},{10,18},{18,26},{... | collective-permute-start | bytes 12296 | tf_op jit(solution)/shard_map/ppermute | solution.py:347
  101.3 29.6 %collective-permute-start.16 = (bf16[2,4,160,512]{3,2,1,0:T(8,128)(2,1)S(1)}, bf16[2,4,160,512]{3,2,1,0:T(8,128)(2,1)}, u32[]{:S(2)}, u32[]{:S(2)}) collective-permute-start(bf16[2,4,160,512]{3,2,1,0:T(8,128)(2,1)S(1)} %pad_maximum_fusion.3.refs_2_), channel_id=1, source_target_pairs={{0,1},{1,0},{2,3},{3,2},{4,5},{5,4},{6,7},{7,6},{8,9},{9,8},{10,11... | collective-permute-start | bytes 3932168 | tf_op jit(solution)/shard_map/ppermute | solution.py:392
  103.9 29.5 %collective-permute-start.15 = (bf16[2,4,160,512]{3,2,1,0:T(8,128)(2,1)}, bf16[2,4,160,512]{3,2,1,0:T(8,128)(2,1)}, u32[]{:S(2)}, u32[]{:S(2)}) collective-permute-start(bf16[2,4,160,512]{3,2,1,0:T(8,128)(2,1)} %pad_maximum_fusion.2.refs_0_), channel_id=1, source_target_pairs={{0,16},{16,0},{1,17},{17,1},{2,18},{18,2},{3,19},{19,3},{4,20},{20... | collective-permute-start | bytes 3932168 | tf_op jit(solution)/shard_map/ppermute | solution.py:392
  104.7 234.5 %reduce-scatter.5.cloned.1.call-start = ((), (), s32[]{:S(2)}) async-start(), calls=%async_computation.3 | async-start | bytes 1638400 | tf_op jit(solution)/shard_map/reduce_scatter | solution.py:519
  104.7 36.1 %collective-permute-start.18 = (bf16[2,4,160,512]{3,2,1,0:T(8,128)(2,1)S(1)}, bf16[2,4,160,512]{3,2,1,0:T(8,128)(2,1)}, u32[]{:S(2)}, u32[]{:S(2)}) collective-permute-start(bf16[2,4,160,512]{3,2,1,0:T(8,128)(2,1)S(1)} %pad_maximum_fusion.3.refs_2_), channel_id=1, source_target_pairs={{0,8},{8,0},{1,9},{9,1},{2,10},{10,2},{3,11},{11,3},{4,12},{12,4},... | collective-permute-start | bytes 3932168 | tf_op jit(solution)/shard_map/ppermute | solution.py:392
  107.9 32.9 %collective-permute-start.17 = (bf16[2,4,160,512]{3,2,1,0:T(8,128)(2,1)}, bf16[2,4,160,512]{3,2,1,0:T(8,128)(2,1)}, u32[]{:S(2)}, u32[]{:S(2)}) collective-permute-start(bf16[2,4,160,512]{3,2,1,0:T(8,128)(2,1)} %pad_maximum_fusion.2.refs_0_), channel_id=1, source_target_pairs={{0,8},{8,0},{1,9},{9,1},{2,10},{10,2},{3,11},{11,3},{4,12},{12,4},... | collective-permute-start | bytes 3932168 | tf_op jit(solution)/shard_map/ppermute | solution.py:392
  130.9 20.1 %collective-permute-start.20 = (bf16[2,4,160,512]{3,2,1,0:T(8,128)(2,1)}, bf16[2,4,160,512]{3,2,1,0:T(8,128)(2,1)}, u32[]{:S(2)}, u32[]{:S(2)}) collective-permute-start(bf16[2,4,160,512]{3,2,1,0:T(8,128)(2,1)} %collective-permute-done.16.refs_3_), channel_id=1, source_target_pairs={{0,8},{8,0},{1,9},{9,1},{2,10},{10,2},{3,11},{11,3},{4,12},{12,4},... | collective-permute-start | bytes 3932168 | tf_op jit(solution)/shard_map/ppermute | solution.py:392
  133.4 17.7 %collective-permute-start.19 = (bf16[2,4,160,512]{3,2,1,0:T(8,128)(2,1)}, bf16[2,4,160,512]{3,2,1,0:T(8,128)(2,1)}, u32[]{:S(2)}, u32[]{:S(2)}) collective-permute-start(bf16[2,4,160,512]{3,2,1,0:T(8,128)(2,1)} %collective-permute-done.15.refs_1_), channel_id=1, source_target_pairs={{0,8},{8,0},{1,9},{9,1},{2,10},{10,2},{3,11},{11,3},{4,12},{12,4},... | collective-permute-start | bytes 3932168 | tf_op jit(solution)/shard_map/ppermute | solution.py:392
  161.1 6.8 %collective-permute-start.21 = (f32[2,1024]{1,0:T(2,128)S(1)}, f32[2,1024]{1,0:T(2,128)S(1)}, u32[]{:S(2)}, u32[]{:S(2)}) collective-permute-start(f32[2,1024]{1,0:T(2,128)S(1)} %bitcast.514), channel_id=1, source_target_pairs={{0,8},{8,16},{16,24},{1,9},{9,17},{17,25},{2,10},{10,18},{18,26},{... | collective-permute-start | bytes 24584 | tf_op jit(solution)/shard_map/ppermute | solution.py:347
  166.5 29.9 %collective-permute-start.22 = (bf16[2,4,160,512]{3,2,1,0:T(8,128)(2,1)S(1)}, bf16[2,4,160,512]{3,2,1,0:T(8,128)(2,1)}, u32[]{:S(2)}, u32[]{:S(2)}) collective-permute-start(bf16[2,4,160,512]{3,2,1,0:T(8,128)(2,1)S(1)} %bitcast.439), channel_id=1, source_target_pairs={{0,16},{16,0},{1,17},{17,1},{2,18},{18,2},{3,19},{19,3},{4,20},{20... | collective-permute-start | bytes 3932168 | tf_op jit(solution)/shard_map/ppermute | solution.py:392
  166.6 30.1 %collective-permute-start.23 = (bf16[2,4,160,512]{3,2,1,0:T(8,128)(2,1)S(1)}, bf16[2,4,160,512]{3,2,1,0:T(8,128)(2,1)}, u32[]{:S(2)}, u32[]{:S(2)}) collective-permute-start(bf16[2,4,160,512]{3,2,1,0:T(8,128)(2,1)S(1)} %bitcast.442), channel_id=1, source_target_pairs={{0,1},{1,0},{2,3},{3,2},{4,5},{5,4},{6,7},{7,6},{8,9},{9,8},{10,11... | collective-permute-start | bytes 3932168 | tf_op jit(solution)/shard_map/ppermute | solution.py:392
  170.2 26.5 %collective-permute-start.24 = (bf16[2,4,160,512]{3,2,1,0:T(8,128)(2,1)S(1)}, bf16[2,4,160,512]{3,2,1,0:T(8,128)(2,1)S(1)}, u32[]{:S(2)}, u32[]{:S(2)}) collective-permute-start(bf16[2,4,160,512]{3,2,1,0:T(8,128)(2,1)S(1)} %bitcast.440), channel_id=1, source_target_pairs={{0,8},{8,0},{1,9},{9,1},{2,10},{10,2},{3,11},{11,3},{4,12},{12,4},... | collective-permute-start | bytes 3932168 | tf_op jit(solution)/shard_map/ppermute | solution.py:392
  170.9 26.8 %collective-permute-start.25 = (bf16[2,4,160,512]{3,2,1,0:T(8,128)(2,1)S(1)}, bf16[2,4,160,512]{3,2,1,0:T(8,128)(2,1)S(1)}, u32[]{:S(2)}, u32[]{:S(2)}) collective-permute-start(bf16[2,4,160,512]{3,2,1,0:T(8,128)(2,1)S(1)} %bitcast.443), channel_id=1, source_target_pairs={{0,8},{8,0},{1,9},{9,1},{2,10},{10,2},{3,11},{11,3},{4,12},{12,4},... | collective-permute-start | bytes 3932168 | tf_op jit(solution)/shard_map/ppermute | solution.py:392
  198.8 4.3 collective-permute-start.26
  200.1 4.9 %collective-permute-start.27 = (bf16[2,4,160,512]{3,2,1,0:T(8,128)(2,1)}, bf16[2,4,160,512]{3,2,1,0:T(8,128)(2,1)}, u32[]{:S(2)}, u32[]{:S(2)}) collective-permute-start(bf16[2,4,160,512]{3,2,1,0:T(8,128)(2,1)} %collective-permute-done.23.refs_3_), channel_id=1, source_target_pairs={{0,8},{8,0},{1,9},{9,1},{2,10},{10,2},{3,11},{11,3},{4,12},{12,4},... | collective-permute-start | bytes 3932168 | tf_op jit(solution)/shard_map/ppermute | solution.py:392
  231.8 9.0 %collective-permute-start.28 = (bf16[4096,512]{1,0:T(8,128)(2,1)}, bf16[4096,512]{1,0:T(8,128)(2,1)}, u32[]{:S(2)}, u32[]{:S(2)}) collective-permute-start(bf16[4096,512]{1,0:T(8,128)(2,1)} %bitcast_convert_fusion.1), channel_id=1, source_target_pairs={{0,8},{8,0},{1,9},{9,1},{2,10},{10,2},{3,11},{11,3},{4,12},{12,4},... | collective-permute-start | bytes 12582920 | tf_op jit(solution)/shard_map/ppermute | solution.py:392
  234.1 6.6 %collective-permute-start.29 = (bf16[1024,512]{1,0:T(8,128)(2,1)}, bf16[1024,512]{1,0:T(8,128)(2,1)}, u32[]{:S(2)}, u32[]{:S(2)}) collective-permute-start(bf16[1024,512]{1,0:T(8,128)(2,1)} %bitcast_convert_fusion.6), channel_id=1, source_target_pairs={{0,8},{8,0},{1,9},{9,1},{2,10},{10,2},{3,11},{11,3},{4,12},{12,4},... | collective-permute-start | bytes 3145736 | tf_op jit(solution)/shard_map/ppermute | solution.py:392
  252.4 31.1 %collective-permute-start.31 = (bf16[4,2,2,128,512]{4,3,0,1,2:T(8,128)(2,1)}, bf16[4,2,2,128,512]{4,3,0,1,2:T(8,128)(2,1)}, u32[]{:S(2)}, u32[]{:S(2)}) collective-permute-start(bf16[4,2,2,128,512]{4,3,0,1,2:T(8,128)(2,1)} %bitcast_select_fusion.2), channel_id=1, source_target_pairs={{0,1},{1,0},{2,3},{3,2},{4,5},{5,4},{6,7},{7,6},{8,24},{9,25},{10,... | collective-permute-start | bytes 6291464 | tf_op jit(solution)/shard_map/ppermute | solution.py:407
  269.8 13.7 %collective-permute-start.32 = (bf16[4,2,2,32,512]{4,3,0,1,2:T(8,128)(2,1)S(1)}, bf16[4,2,2,32,512]{4,3,0,1,2:T(8,128)(2,1)S(1)}, u32[]{:S(2)}, u32[]{:S(2)}) collective-permute-start(bf16[4,2,2,32,512]{4,3,0,1,2:T(8,128)(2,1)S(1)} %copy-done.75), channel_id=1, source_target_pairs={{0,1},{1,0},{2,3},{3,2},{4,5},{5,4},{6,7},{7,6},{8,24},{9,25},{10,... | collective-permute-start | bytes 1572872 | tf_op jit(solution)/shard_map/ppermute | solution.py:407
  270.4 7.7 %collective-permute-start.30 = (f32[2,1024]{1,0:T(2,128)S(1)}, f32[2,1024]{1,0:T(2,128)S(1)}, u32[]{:S(2)}, u32[]{:S(2)}) collective-permute-start(f32[2,1024]{1,0:T(2,128)S(1)} %bitcast.515), channel_id=1, source_target_pairs={{8,0},{16,8},{24,16},{9,1},{17,9},{25,17},{10,2},{18,10},{26,18},{... | collective-permute-start | bytes 24584 | tf_op jit(solution)/shard_map/ppermute | solution.py:347
  278.1 30.2 %collective-permute-start.35 = (bf16[1024,2048]{1,0:T(8,128)(2,1)}, bf16[1024,2048]{1,0:T(8,128)(2,1)}, u32[]{:S(2)}, u32[]{:S(2)}) collective-permute-start(bf16[1024,2048]{1,0:T(8,128)(2,1)} %bitcast_convert_fusion), channel_id=1, source_target_pairs={{0,8},{8,0},{1,9},{9,1},{2,10},{10,2},{3,11},{11,3},{4,12},{12,4},... | collective-permute-start | bytes 12582920 | tf_op jit(solution)/shard_map/ppermute | solution.py:392
  286.5 19.3 %collective-permute-start.36 = (bf16[4,2,128,512]{3,2,0,1:T(8,128)(2,1)S(1)}, bf16[4,2,128,512]{3,2,0,1:T(8,128)(2,1)S(1)}, u32[]{:S(2)}, u32[]{:S(2)}) collective-permute-start(bf16[4,2,128,512]{3,2,0,1:T(8,128)(2,1)S(1)} %dynamic-slice_bitcast_fusion.3), channel_id=1, source_target_pairs={{0,16},{1,17},{2,18},{3,19},{4,20},{5,21},{6,22},{7,23},{8,9},{9,8... | collective-permute-start | bytes 3145736 | tf_op jit(solution)/shard_map/ppermute | solution.py:407
  288.1 17.6 %collective-permute-start.37 = (bf16[4,2,32,512]{3,2,0,1:T(8,128)(2,1)S(1)}, bf16[4,2,32,512]{3,2,0,1:T(8,128)(2,1)S(1)}, u32[]{:S(2)}, u32[]{:S(2)}) collective-permute-start(bf16[4,2,32,512]{3,2,0,1:T(8,128)(2,1)S(1)} %dynamic-slice_bitcast_fusion.18), channel_id=1, source_target_pairs={{0,16},{1,17},{2,18},{3,19},{4,20},{5,21},{6,22},{7,23},{8,9},{9,8... | collective-permute-start | bytes 786440 | tf_op jit(solution)/shard_map/ppermute | solution.py:407
  294.7 3.3 collective-permute-start.33
  298.1 5.0 %collective-permute-start.34 = (f32[2,2,1024]{2,1,0:T(2,128)S(1)}, f32[2,2,1024]{2,1,0:T(2,128)S(1)}, u32[]{:S(2)}, u32[]{:S(2)}) collective-permute-start(f32[2,2,1024]{2,1,0:T(2,128)S(1)} %select_add_fusion), channel_id=1, source_target_pairs={{16,0},{17,1},{18,2},{19,3},{20,4},{21,5},{22,6},{23,7},{24,8},{25... | collective-permute-start | bytes 49160 | tf_op jit(solution)/shard_map/ppermute | solution.py:347
  301.2 6.3 %collective-permute-start.39 = (bf16[1024,512]{1,0:T(8,128)(2,1)}, bf16[1024,512]{1,0:T(8,128)(2,1)}, u32[]{:S(2)}, u32[]{:S(2)}) collective-permute-start(bf16[1024,512]{1,0:T(8,128)(2,1)} %bitcast_convert_fusion.4), channel_id=1, source_target_pairs={{0,8},{8,0},{1,9},{9,1},{2,10},{10,2},{3,11},{11,3},{4,12},{12,4},... | collective-permute-start | bytes 3145736 | tf_op jit(solution)/shard_map/ppermute | solution.py:392
  303.1 5.2 %collective-permute-start.38 = (bf16[1024,512]{1,0:T(8,128)(2,1)}, bf16[1024,512]{1,0:T(8,128)(2,1)}, u32[]{:S(2)}, u32[]{:S(2)}) collective-permute-start(bf16[1024,512]{1,0:T(8,128)(2,1)} %bitcast_convert_fusion.5), channel_id=1, source_target_pairs={{0,8},{8,0},{1,9},{9,1},{2,10},{10,2},{3,11},{11,3},{4,12},{12,4},... | collective-permute-start | bytes 3145736 | tf_op jit(solution)/shard_map/ppermute | solution.py:392
  307.4 130.0 %reduce-scatter.3.cloned.1.call-start = ((), (), s32[]{:S(2)}) async-start(), calls=%async_computation.2 | async-start | bytes 1966080 | tf_op jit(solution)/shard_map/reduce_scatter | solution.py:519
  318.7 36.7 %collective-permute-start.42 = (bf16[4,2,2,32,2048]{4,3,0,1,2:T(8,128)(2,1)}, bf16[4,2,2,32,2048]{4,3,0,1,2:T(8,128)(2,1)}, u32[]{:S(2)}, u32[]{:S(2)}) collective-permute-start(bf16[4,2,2,32,2048]{4,3,0,1,2:T(8,128)(2,1)} %bitcast_select_fusion), channel_id=1, source_target_pairs={{0,1},{1,0},{2,3},{3,2},{4,5},{5,4},{6,7},{7,6},{8,24},{9,25},{10,... | collective-permute-start | bytes 6291464 | tf_op jit(solution)/shard_map/ppermute | solution.py:407
  327.7 22.1 %collective-permute-start.44 = (bf16[4,2,2,32,512]{4,3,0,1,2:T(8,128)(2,1)}, bf16[4,2,2,32,512]{4,3,0,1,2:T(8,128)(2,1)}, u32[]{:S(2)}, u32[]{:S(2)}) collective-permute-start(bf16[4,2,2,32,512]{4,3,0,1,2:T(8,128)(2,1)} %get-tuple-element.170), channel_id=1, source_target_pairs={{0,1},{1,0},{2,3},{3,2},{4,5},{5,4},{6,7},{7,6},{8,24},{9,25},{10,... | collective-permute-start | bytes 1572872 | tf_op jit(solution)/shard_map/ppermute | solution.py:407
  328.5 27.0 %collective-permute-start.43 = (bf16[4,2,2,32,512]{4,3,0,1,2:T(8,128)(2,1)}, bf16[4,2,2,32,512]{4,3,0,1,2:T(8,128)(2,1)}, u32[]{:S(2)}, u32[]{:S(2)}) collective-permute-start(bf16[4,2,2,32,512]{4,3,0,1,2:T(8,128)(2,1)} %get-tuple-element.167), channel_id=1, source_target_pairs={{0,1},{1,0},{2,3},{3,2},{4,5},{5,4},{6,7},{7,6},{8,24},{9,25},{10,... | collective-permute-start | bytes 1572872 | tf_op jit(solution)/shard_map/ppermute | solution.py:407
  342.9 21.0 %collective-permute-start.41 = (bf16[1024,512]{1,0:T(8,128)(2,1)S(1)}, bf16[1024,512]{1,0:T(8,128)(2,1)S(1)}, u32[]{:S(2)}, u32[]{:S(2)}) collective-permute-start(bf16[1024,512]{1,0:T(8,128)(2,1)S(1)} %copy-done.88), channel_id=1, source_target_pairs={{0,8},{8,0},{1,9},{9,1},{2,10},{10,2},{3,11},{11,3},{4,12},{12,4},... | collective-permute-start | bytes 3145736 | tf_op jit(solution)/shard_map/ppermute | solution.py:392
  343.1 20.8 %collective-permute-start.40 = (bf16[1024,512]{1,0:T(8,128)(2,1)S(1)}, bf16[1024,512]{1,0:T(8,128)(2,1)S(1)}, u32[]{:S(2)}, u32[]{:S(2)}) collective-permute-start(bf16[1024,512]{1,0:T(8,128)(2,1)S(1)} %bitcast_convert_fusion.3), channel_id=1, source_target_pairs={{0,8},{8,0},{1,9},{9,1},{2,10},{10,2},{3,11},{11,3},{4,12},{12,4},... | collective-permute-start | bytes 3145736 | tf_op jit(solution)/shard_map/ppermute | solution.py:392
  356.8 21.5 %collective-permute-start.47 = (bf16[4,2,32,512]{3,2,0,1:T(8,128)(2,1)S(1)}, bf16[4,2,32,512]{3,2,0,1:T(8,128)(2,1)S(1)}, u32[]{:S(2)}, u32[]{:S(2)}) collective-permute-start(bf16[4,2,32,512]{3,2,0,1:T(8,128)(2,1)S(1)} %dynamic-slice_bitcast_fusion.16), channel_id=1, source_target_pairs={{0,16},{1,17},{2,18},{3,19},{4,20},{5,21},{6,22},{7,23},{8,9},{9,8... | collective-permute-start | bytes 786440 | tf_op jit(solution)/shard_map/ppermute | solution.py:407
  361.0 17.3 %collective-permute-start.45 = (bf16[4,2,32,2048]{3,2,0,1:T(8,128)(2,1)S(1)}, bf16[4,2,32,2048]{3,2,0,1:T(8,128)(2,1)S(1)}, u32[]{:S(2)}, u32[]{:S(2)}) collective-permute-start(bf16[4,2,32,2048]{3,2,0,1:T(8,128)(2,1)S(1)} %dynamic-slice_bitcast_fusion.2), channel_id=1, source_target_pairs={{0,16},{1,17},{2,18},{3,19},{4,20},{5,21},{6,22},{7,23},{8,9},{9,8... | collective-permute-start | bytes 3145736 | tf_op jit(solution)/shard_map/ppermute | solution.py:407
  362.8 15.5 %collective-permute-start.46 = (bf16[4,2,32,512]{3,2,0,1:T(8,128)(2,1)S(1)}, bf16[4,2,32,512]{3,2,0,1:T(8,128)(2,1)S(1)}, u32[]{:S(2)}, u32[]{:S(2)}) collective-permute-start(bf16[4,2,32,512]{3,2,0,1:T(8,128)(2,1)S(1)} %dynamic-slice_bitcast_fusion.17), channel_id=1, source_target_pairs={{0,16},{1,17},{2,18},{3,19},{4,20},{5,21},{6,22},{7,23},{8,9},{9,8... | collective-permute-start | bytes 786440 | tf_op jit(solution)/shard_map/ppermute | solution.py:407
  378.3 18.8 %collective-permute-start.57 = (bf16[4,2,2,32,512]{4,3,0,1,2:T(8,128)(2,1)}, bf16[4,2,2,32,512]{4,3,0,1,2:T(8,128)(2,1)}, u32[]{:S(2)}, u32[]{:S(2)}) collective-permute-start(bf16[4,2,2,32,512]{4,3,0,1,2:T(8,128)(2,1)} %bitcast_select_fusion.4), channel_id=1, source_target_pairs={{0,1},{1,0},{2,3},{3,2},{4,5},{5,4},{6,7},{7,6},{8,24},{9,25},{10,... | collective-permute-start | bytes 1572872 | tf_op jit(solution)/shard_map/ppermute | solution.py:407
  378.8 21.4 %collective-permute-start.55 = (bf16[4,2,2,32,512]{4,3,0,1,2:T(8,128)(2,1)}, bf16[4,2,2,32,512]{4,3,0,1,2:T(8,128)(2,1)}, u32[]{:S(2)}, u32[]{:S(2)}) collective-permute-start(bf16[4,2,2,32,512]{4,3,0,1,2:T(8,128)(2,1)} %bitcast_select_fusion.5), channel_id=1, source_target_pairs={{0,1},{1,0},{2,3},{3,2},{4,5},{5,4},{6,7},{7,6},{8,24},{9,25},{10,... | collective-permute-start | bytes 1572872 | tf_op jit(solution)/shard_map/ppermute | solution.py:407
  380.4 6.9 %collective-permute-start.48 = (f32[2,1024]{1,0:T(2,128)S(1)}, f32[2,1024]{1,0:T(2,128)S(1)}, u32[]{:S(2)}, u32[]{:S(2)}) collective-permute-start(f32[2,1024]{1,0:T(2,128)S(1)} %bitcast.513), channel_id=1, source_target_pairs={{8,0},{16,8},{24,16},{9,1},{17,9},{25,17},{10,2},{18,10},{26,18},{... | collective-permute-start | bytes 24584 | tf_op jit(solution)/shard_map/ppermute | solution.py:347
  392.7 3.0 collective-permute-start.50
  395.6 10.7 %collective-permute-start.51 = (f32[11264]{0:T(1024)S(1)}, f32[11264]{0:T(1024)S(1)}, u32[]{:S(2)}, u32[]{:S(2)}) collective-permute-start(f32[11264]{0:T(1024)S(1)} %add.384), channel_id=1, source_target_pairs={{0,16},{16,0},{1,17},{17,1},{2,18},{18,2},{3,19},{19,3},{4,20},{20... | collective-permute-start | bytes 135176 | tf_op jit(solution)/shard_map/ppermute | solution.py:392
  399.0 10.6 %collective-permute-start.58 = (bf16[4,2,32,512]{3,2,0,1:T(8,128)(2,1)S(1)}, bf16[4,2,32,512]{3,2,0,1:T(8,128)(2,1)S(1)}, u32[]{:S(2)}, u32[]{:S(2)}) collective-permute-start(bf16[4,2,32,512]{3,2,0,1:T(8,128)(2,1)S(1)} %dynamic-slice_bitcast_fusion.14), channel_id=1, source_target_pairs={{0,16},{1,17},{2,18},{3,19},{4,20},{5,21},{6,22},{7,23},{8,9},{9,8... | collective-permute-start | bytes 786440 | tf_op jit(solution)/shard_map/ppermute | solution.py:407
  401.9 7.8 %collective-permute-start.56 = (bf16[4,2,32,512]{3,2,0,1:T(8,128)(2,1)S(1)}, bf16[4,2,32,512]{3,2,0,1:T(8,128)(2,1)S(1)}, u32[]{:S(2)}, u32[]{:S(2)}) collective-permute-start(bf16[4,2,32,512]{3,2,0,1:T(8,128)(2,1)S(1)} %dynamic-slice_bitcast_fusion.15), channel_id=1, source_target_pairs={{0,16},{1,17},{2,18},{3,19},{4,20},{5,21},{6,22},{7,23},{8,9},{9,8... | collective-permute-start | bytes 786440 | tf_op jit(solution)/shard_map/ppermute | solution.py:407
  406.3 7.3 %collective-permute-start.52 = (f32[11264]{0:T(1024)S(1)}, f32[11264]{0:T(1024)S(1)}, u32[]{:S(2)}, u32[]{:S(2)}) collective-permute-start(f32[11264]{0:T(1024)S(1)} %add.385), channel_id=1, source_target_pairs={{0,2},{2,4},{4,6},{6,0},{1,3},{3,5},{5,7},{7,1},{8,10},{10,12},{12... | collective-permute-start | bytes 135176 | tf_op jit(solution)/shard_map/ppermute | solution.py:392
  407.7 6.6 %collective-permute-start.53 = (f32[11264]{0:T(1024)S(1)}, f32[11264]{0:T(1024)S(1)}, u32[]{:S(2)}, u32[]{:S(2)}) collective-permute-start(f32[11264]{0:T(1024)S(1)} %add.385), channel_id=1, source_target_pairs={{0,4},{2,6},{4,0},{6,2},{1,5},{3,7},{5,1},{7,3},{8,12},{10,14},{12... | collective-permute-start | bytes 135176 | tf_op jit(solution)/shard_map/ppermute | solution.py:392
  408.2 11.5 %collective-permute-start.54 = (f32[11264]{0:T(1024)S(1)}, f32[11264]{0:T(1024)S(1)}, u32[]{:S(2)}, u32[]{:S(2)}) collective-permute-start(f32[11264]{0:T(1024)S(1)} %add.385), channel_id=1, source_target_pairs={{0,6},{2,0},{4,2},{6,4},{1,7},{3,1},{5,3},{7,5},{8,14},{10,8},{12,... | collective-permute-start | bytes 135176 | tf_op jit(solution)/shard_map/ppermute | solution.py:392
  409.8 15.5 %collective-permute-start.59 = (bf16[2,64,512]{2,1,0:T(8,128)(2,1)S(1)}, bf16[2,64,512]{2,1,0:T(8,128)(2,1)S(1)}, u32[]{:S(2)}, u32[]{:S(2)}) collective-permute-start(bf16[2,64,512]{2,1,0:T(8,128)(2,1)S(1)} %get-tuple-element.249), channel_id=1, source_target_pairs={{0,2},{2,4},{4,6},{6,0},{1,3},{3,5},{5,7},{7,1},{8,10},{10,12},{12... | collective-permute-start | bytes 393224 | tf_op jit(solution)/shard_map/ppermute | solution.py:512
  410.0 23.5 %collective-permute-start.60 = (bf16[2,64,512]{2,1,0:T(8,128)(2,1)S(1)}, bf16[2,64,512]{2,1,0:T(8,128)(2,1)S(1)}, u32[]{:S(2)}, u32[]{:S(2)}) collective-permute-start(bf16[2,64,512]{2,1,0:T(8,128)(2,1)S(1)} %get-tuple-element.250), channel_id=1, source_target_pairs={{0,4},{2,6},{4,0},{6,2},{1,5},{3,7},{5,1},{7,3},{8,12},{10,14},{12... | collective-permute-start | bytes 393224 | tf_op jit(solution)/shard_map/ppermute | solution.py:512
  413.6 22.0 %collective-permute-start.61 = (bf16[2,64,512]{2,1,0:T(8,128)(2,1)S(1)}, bf16[2,64,512]{2,1,0:T(8,128)(2,1)S(1)}, u32[]{:S(2)}, u32[]{:S(2)}) collective-permute-start(bf16[2,64,512]{2,1,0:T(8,128)(2,1)S(1)} %get-tuple-element.251), channel_id=1, source_target_pairs={{0,6},{2,0},{4,2},{6,4},{1,7},{3,1},{5,3},{7,5},{8,14},{10,8},{12,... | collective-permute-start | bytes 393224 | tf_op jit(solution)/shard_map/ppermute | solution.py:512
  (103 other events, 618.2 us)
Sparse Core Ops, SparseCore 0:
  34.7 35.5 all-gather.7
  72.4 31.6 all-gather.9
  106.2 32.3 all-gather.11
  307.6 28.2 reduce-scatter.4
  387.4 46.3 reduce-scatter.2
where the time goes:
time: 459 us; the launch traced here: 450 us
  waiting for transfers between devices  112 us (24%)
  starting transfers between devices  73.9 us (16%)
  Pallas kernels  63.6 us (14%)
  matrix products  63.3 us (14%)
  other arithmetic  56.1 us (12%)
  local copies, waits for them, and re-layouts  47.5 us (10%)
  blocking collectives  17.6 us (4%)
  between operations  16.1 us (4%)
    ppermute x42, waiting for transfers between devices, spread(): lax.ppermute(block, axis, [(i, (i + k) % count) for i in range(count)])  79.7 us
    ppermute x42, starting transfers between devices, spread(): lax.ppermute(block, axis, [(i, (i + k) % count) for i in range(count)])  40.2 us
    dot_general x14, matrix products, outer(): jnp.einsum('nlc,nld->cd', left, right, preferred_element_type=jnp.float32)  36.1 us
    unnamed x224, local copies, waits for them, and re-layouts  24.9 us
    pallas_call x3, Pallas kernels, assemble(): pl.pallas_call(functools.partial(assemble_kernel, entries, grid), out_sha...  21.9 us
    dot_general x5, matrix products, matmul(): return jnp.einsum(form, left, right, preferred_element_type=jnp.float32)  21.2 us
    ppermute x6, starting transfers between devices, shifted(): return lax.ppermute(block, axis, route)  19.1 us
    all_gather x1, blocking collectives, beside_z(): rows = lax.all_gather(own, 'z', axis=0)  17.6 us
  transfers between devices with their start and end apart: 70, of which 27 were waited for; matrix products, arithmetic and copies ran while one was open for 24% of the time, Pallas kernels for 11%

commit v1 on v0

--- a/solution.py
+++ b/solution.py
@@ -673,6 +673,8 @@
     residual = field + branch
     normed_two_raw, inverse_two = norm_stats(residual)
     normed_two = normed_two_raw * gain_two + bias_two
+    if stepwise:
+        normed_two = after(normed_two, yx2)
     before_two = previous_rows(normed_two)
     ffn_key = (normed_two * chan_key_mix + before_two * (1.0 - chan_key_mix)).astype(jnp.bfloat16)
     ffn_recept = (normed_two * chan_recept_mix + before_two * (1.0 - chan_recept_mix)).astype(

time: 459 us -> 450 us (0.980)
  the two profiles are of different devices: /device:TPU:9 before, /device:TPU:0 now
where the time goes in v1:
time: 450 us; the launch traced here: 443 us
  waiting for transfers between devices  107 us (24%)
  starting transfers between devices  65.9 us (15%)
  matrix products  64.5 us (14%)
  Pallas kernels  63.7 us (14%)
  other arithmetic  55.6 us (12%)
  local copies, waits for them, and re-layouts  48.7 us (11%)
  blocking collectives  21.4 us (5%)
  between operations  16.1 us (4%)
    ppermute x42, waiting for transfers between devices, spread(): lax.ppermute(block, axis, [(i, (i + k) % count) for i in range(count)])  68 us
    dot_general x14, matrix products, outer(): jnp.einsum('nlc,nld->cd', left, right, preferred_element_type=jnp.float32)  36.8 us
    ppermute x42, starting transfers between devices, spread(): lax.ppermute(block, axis, [(i, (i + k) % count) for i in range(count)])  36.3 us
    unnamed x227, local copies, waits for them, and re-layouts  25.1 us
    pallas_call x3, Pallas kernels, assemble(): pl.pallas_call(functools.partial(assemble_kernel, entries, grid), out_sha...  21.9 us
    dot_general x5, matrix products, matmul(): return jnp.einsum(form, left, right, preferred_element_type=jnp.float32)  21.6 us
    all_gather x1, blocking collectives, beside_z(): rows = lax.all_gather(own, 'z', axis=0)  21.4 us
    ppermute x14, starting transfers between devices, cross(): return lax.ppermute(block, ALL, route)  16 us
  transfers between devices with their start and end apart: 70, of which 26 were waited for; matrix products, arithmetic and copies ran while one was open for 24% of the time, Pallas kernels for 13%

profile of v1, /device:TPU:0, one launch (start us, length us, event | category | flops | bytes accessed | tf_op | source)
XLA Modules:
  0.0 442.7 jit_solution(11239029596518014493)
XLA Ops:
  9.1 3.0 collective-permute-start.1
  16.1 21.4 %all-gather = bf16[448,1024]{1,0:T(8,128)(2,1)S(1)} all-gather(bf16[112,1024]{1,0:T(8,128)(2,1)S(1)} %fusion.93), channel_id=2, replica_groups=mesh['y'=2,'core'=2,'z'=4,'x'=2] {'z'}, dimensions={0}, use_global_device_ids=true | all-gather | bytes 1146880 | tf_op jit(solution)/shard_map/all_gather | solution.py:412
  41.0 5.8 %collective-permute-done.5 = bf16[4,112,512]{2,1,0:T(8,128)(2,1)S(1)} collective-permute-done((bf16[4,112,512]{2,1,0:T(8,128)(2,1)S(1)}, bf16[4,112,512]{2,1,0:T(8,128)(2,1)S(1)}, u32[]{:S(2)}, u32[]{:S(2)}) %collective-permute-start.5) | collective-permute-done | bytes 458784 | tf_op jit(solution)/shard_map/ppermute | solution.py:392
  50.4 1.9 collective-permute-start.4
  52.9 14.1 %collective-permute-done.6.refs_3_ = bf16[2,4,112,512]{3,2,1,0:T(8,128)(2,1)} collective-permute-done((bf16[2,4,112,512]{3,2,1,0:T(8,128)(2,1)S(1)}, bf16[2,4,112,512]{3,2,1,0:T(8,128)(2,1)}, u32[]{:S(2)}, u32[]{:S(2)}) %collective-permute-start.6) | collective-permute-done | bytes 917536 | tf_op jit(solution)/shard_map/ppermute | solution.py:392
  68.4 4.3 all-gather.8.cloned.1.call-done
  72.7 2.2 fusion.107
  79.3 6.8 %shard_map.356 = (bf16[3,32,32,1024]{3,2,1,0:T(8,128)(2,1)}, bf16[1,32,16,1024]{3,2,1,0:T(8,128)(2,1)S(1)}) custom-call(s32[3]{0:T(128)S(1)} %pad_add_fusion.at_ref, bf16[2,4,112,512]{3,2,1,0:T(8,128)(2,1)S(1)} %pad_maximum_fusion.5.refs_0_, bf16[2,4,112,512]{3,2,1,0:T(8,128)(2,1)} %collective-permute-done.4.refs_1_, ...), custom_call_target="tpu_custom_call" | custom-call | tf_op jit(solution)/shard_map/pallas_call | solution.py:463
  87.7 10.1 %shard_map.357 = (bf16[2,256,1024]{2,1,0:T(8,128)(2,1)S(1)}, bf16[2,256,1024]{2,1,0:T(8,128)(2,1)S(1)}, bf16[2,256,1024]{2,1,0:T(8,128)(2,1)S(1)}, f32[3,2,256,1...) custom-call(s32[1]{0:T(128)} %bitcast.flag_ref, bf16[2,256,1024]{2,1,0:T(8,128)(2,1)S(1)} %copy-done.1, ...), custom_call_target="tpu_custom_call" | custom-call | flops 1048576 | bytes 65536 | tf_op jit(solution)/shard_map/pallas_call | solution.py:193
  98.9 2.2 pad_maximum_fusion.3.refs_2_
  101.7 2.3 pad_maximum_fusion.2.refs_0_
  104.0 3.8 collective-permute-start.15
  109.2 23.3 %collective-permute-done.16.refs_3_ = bf16[2,4,160,512]{3,2,1,0:T(8,128)(2,1)} collective-permute-done((bf16[2,4,160,512]{3,2,1,0:T(8,128)(2,1)S(1)}, bf16[2,4,160,512]{3,2,1,0:T(8,128)(2,1)}, u32[]{:S(2)}, u32[]{:S(2)}) %collective-permute-start.16) | collective-permute-done | bytes 1310752 | tf_op jit(solution)/shard_map/ppermute | solution.py:392
  133.0 3.1 collective-permute-done.15.refs_1_
  136.8 2.0 collective-permute-done.13
  138.8 2.4 collective-permute-start.14
  142.6 2.4 collective-permute-start.21
  146.4 2.8 copy-done
  149.2 4.7 %shard_map.358 = (f32[2,256,1024]{2,1,0:T(8,128)S(1)}, f32[2,256,1024]{2,1,0:T(8,128)S(1)}, bf16[2,256,1024]{2,1,0:T(8,128)(2,1)S(1)}) custom-call(f32[3,2,256,1024]{3,2,1,0:T(8,128)S(1)} %copy-done, f32[3,2,256,1024]{3,2,1,0:T(8,128)S(1)} %copy-done, f32[3,2,256,1024]{3,2,1,0:T(8,128)S(1)} %copy-done, f32[2,1024]{1,0:T(2,128)S(1)} %get-tuple-element.131.a0_ref, ...), custom_call_target="tpu_custom_call" | custom-call | flops 1048576 | bytes 65536 | tf_op jit(solution)/shard_map/pallas_call | solution.py:313
  156.6 7.8 %shard_map.359 = (bf16[1,32,32,1024]{3,2,1,0:T(8,128)(2,1)S(1)}, bf16[1,32,32,4096]{3,2,1,0:T(8,128)(2,1)}) custom-call(s32[3]{0:T(128)S(1)} %pad_add_fusion.at_ref, bf16[2,4,160,512]{3,2,1,0:T(8,128)(2,1)} %pad_maximum_fusion.2.refs_0_, bf16[2,4,160,512]{3,2,1,0:T(8,128)(2,1)} %collective-permute-done.15.refs_1_, ...), custom_call_target="tpu_custom_call" | custom-call | tf_op jit(solution)/shard_map/pallas_call | solution.py:463
  167.1 6.3 %collective-permute-done.21.refs_1_ = bf16[2,4,160,512]{3,2,1,0:T(8,128)(2,1)} collective-permute-done((bf16[2,4,160,512]{3,2,1,0:T(8,128)(2,1)}, bf16[2,4,160,512]{3,2,1,0:T(8,128)(2,1)}, u32[]{:S(2)}, u32[]{:S(2)}) %collective-permute-start.21) | collective-permute-done | bytes 1310752 | tf_op jit(solution)/shard_map/ppermute | solution.py:392
  181.5 6.1 %multiply_convert_fusion = (bf16[512,4096]{1,0:T(8,128)(2,1)}, bf16[512,4096]{1,0:T(8,128)(2,1)S(1)}) fusion(bf16[512,1024]{1,0:T(8,128)(2,1)S(1)} %bitcast.495, bf16[1024,4096]{1,0:T(8,128)(2,1)S(1)} %bitcast.470), kind=kOutput, calls=%fused_computation.6 | convolution fusion | flops 4303355904 | bytes 17825792 | tf_op jit(solution)/shard_map/dot_general | solution.py:684
  187.6 3.0 maximum_convert_fusion.relu_ref
  193.3 2.8 collective-permute-done.26.refs_5_
  196.1 1.9 collective-permute-done.27.refs_7_
  201.9 7.3 %shard_map.360 = (bf16[1,32,32,1024]{3,2,1,0:T(8,128)(2,1)S(1)}, bf16[1,32,128,1024]{3,2,1,0:T(8,128)(2,1)}) custom-call(s32[3]{0:T(128)S(1)} %pad_add_fusion.at_ref, bf16[2,4,160,512]{3,2,1,0:T(8,128)(2,1)S(1)} %bitcast.440, bf16[2,4,160,512]{3,2,1,0:T(8,128)(2,1)} %collective-permute-done.21.refs_1_, bf16[2,4,160,512]{3,2,1,0:T(8,128)(2,1)S(1)} %bitcast.443, ...), custom_call_target="tpu_custom_call" | custom-call | tf_op jit(solution)/shard_map/pallas_call | solution.py:463
  209.3 8.1 %fusion.114 = f32[2,256,1024]{2,1,0:T(8,128)S(1)} fusion(bf16[2,256,4096]{2,1,0:T(8,128)(2,1)S(1)} %bitcast.528, bf16[4096,1024,1]{1,0,2:T(8,128)(2,1)} %bitcast.471), kind=kOutput, calls=%fused_computation.326 | convolution fusion | flops 4294967296 | bytes 14680064 | tf_op jit(solution)/shard_map/nlf,fd->nld/dot_general | solution.py:341
  217.5 3.1 multiply_convert_fusion.1
  220.6 4.6 %bitcast_convert_fusion.1 = bf16[4096,512]{1,0:T(8,128)(2,1)} fusion(bf16[2,256,4096]{2,1,0:T(8,128)(2,1)S(1)} %bitcast.529, bf16[2,256,1024]{2,1,0:T(8,128)(2,1)S(1)} %get-tuple-element.158, pred[]{:T(512)S(6)} %eq.7), kind=kOutput, calls=%fused_computation.5 | convolution fusion | flops 2149842944 | bytes 9437185 | tf_op jit(solution)/shard_map/nlc,nld->cd/dot_general | solution.py:700
  225.8 1.7 bitcast_convert_fusion.6
  230.5 3.3 fusion.115
  234.2 2.9 fusion.26
  237.1 5.1 %fusion.1 = bf16[4096,512]{1,0:T(8,128)(2,1)S(1)} fusion(bf16[4096,512]{1,0:T(8,128)(2,1)} %collective-permute-done.28, bf16[2,256,4096]{2,1,0:T(8,128)(2,1)S(1)} %bitcast.530, bf16[2,256,1024]{2,1,0:T(8,128)(2,1)S(1)} %get-tuple-element.158, pred[]{:T(512)S(6)} %eq.6), kind=kOutput, calls=%fused_computation.4 | convolution fusion | flops 2154037248 | bytes 13631489 | tf_op jit(solution)/shard_map/nlc,nld->cd/dot_general | solution.py:700
  247.5 13.5 %shard_map.361 = (bf16[512,4096]{1,0:T(8,128)(2,1)S(1)}, f32[512,1024]{1,0:T(8,128)S(1)}) custom-call(bf16[512,1024]{1,0:T(8,128)(2,1)S(1)} %bitcast.447, bf16[512,4096]{1,0:T(8,128)(2,1)S(1)} %copy-done.2, bf16[4096,1024]{1,0:T(8,128)(2,1)} %bitcast.472, bf16[1024,4096]{1,0:T(8,128)(2,1)} %bitcast.467), custom_call_target="tpu_custom_call" | custom-call | flops 1048576 | bytes 25165824 | tf_op jit(solution)/shard_map/pallas_call | solution.py:236
  266.1 4.5 %bitcast_convert_fusion = bf16[1024,2048]{1,0:T(8,128)(2,1)} fusion(bf16[2,256,1024]{2,1,0:T(8,128)(2,1)S(1)} %copy-done.72, bf16[2,256,4096]{2,1,0:T(8,128)(2,1)S(1)} %bitcast.451, pred[]{:T(512)S(6)} %eq.7), kind=kOutput, calls=%fused_computation.2 | convolution fusion | flops 2150629376 | bytes 9437185 | tf_op jit(solution)/shard_map/nlc,nld->cd/dot_general | solution.py:700
  272.2 1.8 multiply_reduce_fusion.2
  275.3 2.6 collective-permute-done.32
  277.9 2.8 add_convert_fusion.1
  280.9 2.6 collective-permute-start.36
  283.9 5.7 %fusion.25 = (bf16[2,256,1024]{2,1,0:T(8,128)(2,1)S(1)}, f32[2,256,1024]{2,1,0:T(8,128)S(1)}, f32[2,256,1024]{2,1,0:T(8,128)S(1)}, f32[2,256,1024]{2,1,0:T(8,128)}) fusion(f32[3,2,256,1024]{3,2,1,0:T(8,128)} %get-tuple-element.114.k_ref.v_ref.r_ref, f32[2,256,1024]{2,1,0:T(8,128)S(1)} %copy-done.6, f32[2,256,1024]{2,1,0:T(8,128)S(1)} %copy-done.4, ...), kind=kOutput, calls=%fused_computation.60 | convolution fusion | flops 1082654720 | bytes 22024192 | tf_op jit(solution)/shard_map/nld,cd->nlc/dot_general | solution.py:341
  291.1 1.7 bitcast_convert_fusion.5
  294.2 1.8 bitcast_convert_fusion.4
  296.0 3.4 collective-permute-done.34
  302.4 6.2 %fusion = bf16[1024,2048]{1,0:T(8,128)(2,1)S(1)} fusion(bf16[1024,2048]{1,0:T(8,128)(2,1)} %collective-permute-done.35, bf16[2,256,1024]{2,1,0:T(8,128)(2,1)} %copy-done.71, bf16[2,256,4096]{2,1,0:T(8,128)(2,1)} %bitcast.452, pred[]{:T(512)S(6)} %eq.6), kind=kOutput, calls=%fused_computation.1 | convolution fusion | flops 2154823680 | bytes 13631489 | tf_op jit(solution)/shard_map/nlc,nld->cd/dot_general | solution.py:700
  308.6 2.0 dynamic-slice_bitcast_fusion
  314.3 2.1 fusion.19
  318.2 2.3 fusion.18
  324.7 6.3 %shard_map.362 = (bf16[2,256,1024]{2,1,0:T(8,128)(2,1)S(1)}, bf16[2,256,1024]{2,1,0:T(8,128)(2,1)S(1)}, f32[1,1024]{1,0:T(1,128)S(1)}, f32[1,1024]{1,0:T(1,128)S(1)}) custom-call(f32[3,2,256,1024]{3,2,1,0:T(8,128)S(1)} %bitcast.433, f32[3,2,256,1024]{3,2,1,0:T(8,128)S(1)} %bitcast.433, f32[3,2,256,1024]{3,2,1,0:T(8,128)S(1)} %bitcast.433, ...), custom_call_target="tpu_custom_call" | custom-call | flops 1048576 | bytes 65536 | tf_op jit(solution)/shard_map/pallas_call | solution.py:327
  332.9 1.7 bitcast_convert_fusion.2
  338.9 6.0 %collective-permute-done.44 = bf16[4,2,2,32,512]{4,3,0,1,2:T(8,128)(2,1)} collective-permute-done((bf16[4,2,2,32,512]{4,3,0,1,2:T(8,128)(2,1)}, bf16[4,2,2,32,512]{4,3,0,1,2:T(8,128)(2,1)}, u32[]{:S(2)}, u32[]{:S(2)}) %collective-permute-start.44) | collective-permute-done | bytes 524320 | tf_op jit(solution)/shard_map/ppermute | solution.py:407
  344.8 5.6 %collective-permute-done.43 = bf16[4,2,2,32,512]{4,3,0,1,2:T(8,128)(2,1)} collective-permute-done((bf16[4,2,2,32,512]{4,3,0,1,2:T(8,128)(2,1)}, bf16[4,2,2,32,512]{4,3,0,1,2:T(8,128)(2,1)}, u32[]{:S(2)}, u32[]{:S(2)}) %collective-permute-start.43) | collective-permute-done | bytes 524320 | tf_op jit(solution)/shard_map/ppermute | solution.py:407
  352.6 2.6 add_convert_fusion
  362.6 7.1 %shard_map.363 = (f32[512,1024]{1,0:T(8,128)S(1)}, f32[512,1024]{1,0:T(8,128)S(1)}, f32[3,1024]{1,0:T(4,128)S(1)}) custom-call(bf16[512,1024]{1,0:T(8,128)(2,1)S(1)} %bitcast.445, bf16[512,1024]{1,0:T(8,128)(2,1)S(1)} %bitcast.446, bf16[512,1024]{1,0:T(8,128)(2,1)S(1)} %bitcast.444, f32[512,1024]{1,0:T(8,128)S(1)} %copy-done.9, ...), custom_call_target="tpu_custom_call" | custom-call | flops 1048576 | bytes 8388608 | tf_op jit(solution)/shard_map/pallas_call | solution.py:280
  377.4 1.7 slice.431
  380.4 2.6 fusion.11
  388.0 2.6 collective-permute-done.50
  391.9 1.8 add_convert_fusion.4
  397.6 3.9 fusion.10
  401.5 1.7 collective-permute-start.52
  403.2 2.0 collective-permute-start.53
  405.2 2.0 collective-permute-start.54
  408.8 3.5 collective-permute-start.61
  413.4 5.2 %collective-permute-done.59 = bf16[2,64,512]{2,1,0:T(8,128)(2,1)S(1)} collective-permute-done((bf16[2,64,512]{2,1,0:T(8,128)(2,1)S(1)}, bf16[2,64,512]{2,1,0:T(8,128)(2,1)S(1)}, u32[]{:S(2)}, u32[]{:S(2)}) %collective-permute-start.59) | collective-permute-done | bytes 131104 | tf_op jit(solution)/shard_map/ppermute | solution.py:512
  418.6 9.9 %collective-permute-done.60 = bf16[2,64,512]{2,1,0:T(8,128)(2,1)S(1)} collective-permute-done((bf16[2,64,512]{2,1,0:T(8,128)(2,1)S(1)}, bf16[2,64,512]{2,1,0:T(8,128)(2,1)S(1)}, u32[]{:S(2)}, u32[]{:S(2)}) %collective-permute-start.60) | collective-permute-done | bytes 131104 | tf_op jit(solution)/shard_map/ppermute | solution.py:512
  (485 shorter events, 124.7 us)
Async XLA Ops:
  7.2 65.5 %all-gather.8.cloned.1.call-start = ((), (), s32[]{:S(2)}) async-start(), calls=%async_computation.4 | async-start | bytes 1638400 | tf_op jit(solution)/shard_map/all_gather | solution.py:412
  9.1 28.5 %collective-permute-start.1 = (bf16[160,512]{1,0:T(8,128)(2,1)S(1)}, bf16[160,512]{1,0:T(8,128)(2,1)S(1)}, u32[]{:S(2)}, u32[]{:S(2)}) collective-permute-start(bf16[160,512]{1,0:T(8,128)(2,1)S(1)} %get-tuple-element.127), channel_id=1, source_target_pairs={{0,1},{1,0},{2,3},{3,2},{4,5},{5,4},{6,7},{7,6},{8,9},{9,8},{10,11... | collective-permute-start | bytes 491528 | tf_op jit(solution)/shard_map/ppermute | solution.py:392
  12.1 25.5 %collective-permute-start.2 = (bf16[160,512]{1,0:T(8,128)(2,1)S(1)}, bf16[160,512]{1,0:T(8,128)(2,1)S(1)}, u32[]{:S(2)}, u32[]{:S(2)}) collective-permute-start(bf16[160,512]{1,0:T(8,128)(2,1)S(1)} %get-tuple-element.129), channel_id=1, source_target_pairs={{0,16},{16,0},{1,17},{17,1},{2,18},{18,2},{3,19},{19,3},{4,20},{20... | collective-permute-start | bytes 491528 | tf_op jit(solution)/shard_map/ppermute | solution.py:392
  38.3 8.5 %collective-permute-start.5 = (bf16[4,112,512]{2,1,0:T(8,128)(2,1)S(1)}, bf16[4,112,512]{2,1,0:T(8,128)(2,1)S(1)}, u32[]{:S(2)}, u32[]{:S(2)}) collective-permute-start(bf16[4,112,512]{2,1,0:T(8,128)(2,1)S(1)} %get-tuple-element.111), channel_id=1, source_target_pairs={{0,16},{16,0},{1,17},{17,1},{2,18},{18,2},{3,19},{19,3},{4,20},{20... | collective-permute-start | bytes 1376264 | tf_op jit(solution)/shard_map/ppermute | solution.py:392
  38.8 10.6 %collective-permute-start.3 = (bf16[4,112,512]{2,1,0:T(8,128)(2,1)S(1)}, bf16[4,112,512]{2,1,0:T(8,128)(2,1)}, u32[]{:S(2)}, u32[]{:S(2)}) collective-permute-start(bf16[4,112,512]{2,1,0:T(8,128)(2,1)S(1)} %get-tuple-element.110), channel_id=1, source_target_pairs={{0,1},{1,0},{2,3},{3,2},{4,5},{5,4},{6,7},{7,6},{8,9},{9,8},{10,11... | collective-permute-start | bytes 1376264 | tf_op jit(solution)/shard_map/ppermute | solution.py:392
  40.9 101.6 %all-gather.10.cloned.1.call-start = ((), (), s32[]{:S(2)}) async-start(), calls=%async_computation.5 | async-start | bytes 1638400 | tf_op jit(solution)/shard_map/all_gather | solution.py:610
  48.8 18.3 %collective-permute-start.6 = (bf16[2,4,112,512]{3,2,1,0:T(8,128)(2,1)S(1)}, bf16[2,4,112,512]{3,2,1,0:T(8,128)(2,1)}, u32[]{:S(2)}, u32[]{:S(2)}) collective-permute-start(bf16[2,4,112,512]{3,2,1,0:T(8,128)(2,1)S(1)} %pad_maximum_fusion.6.refs_2_), channel_id=1, source_target_pairs={{0,1},{1,0},{2,3},{3,2},{4,5},{5,4},{6,7},{7,6},{8,9},{9,8},{10,11... | collective-permute-start | bytes 2752520 | tf_op jit(solution)/shard_map/ppermute | solution.py:392
  50.4 16.6 %collective-permute-start.4 = (bf16[2,4,112,512]{3,2,1,0:T(8,128)(2,1)S(1)}, bf16[2,4,112,512]{3,2,1,0:T(8,128)(2,1)}, u32[]{:S(2)}, u32[]{:S(2)}) collective-permute-start(bf16[2,4,112,512]{3,2,1,0:T(8,128)(2,1)S(1)} %pad_maximum_fusion.5.refs_0_), channel_id=1, source_target_pairs={{0,16},{16,0},{1,17},{17,1},{2,18},{18,2},{3,19},{19,3},{4,20},{20... | collective-permute-start | bytes 2752520 | tf_op jit(solution)/shard_map/ppermute | solution.py:392
  52.4 24.1 %collective-permute-start.9 = (bf16[2,4,112,512]{3,2,1,0:T(8,128)(2,1)S(1)}, bf16[2,4,112,512]{3,2,1,0:T(8,128)(2,1)}, u32[]{:S(2)}, u32[]{:S(2)}) collective-permute-start(bf16[2,4,112,512]{3,2,1,0:T(8,128)(2,1)S(1)} %pad_maximum_fusion.6.refs_2_), channel_id=1, source_target_pairs={{0,8},{8,0},{1,9},{9,1},{2,10},{10,2},{3,11},{11,3},{4,12},{12,4},... | collective-permute-start | bytes 2752520 | tf_op jit(solution)/shard_map/ppermute | solution.py:392
  52.4 25.6 %collective-permute-start.7 = (bf16[2,4,112,512]{3,2,1,0:T(8,128)(2,1)S(1)}, bf16[2,4,112,512]{3,2,1,0:T(8,128)(2,1)}, u32[]{:S(2)}, u32[]{:S(2)}) collective-permute-start(bf16[2,4,112,512]{3,2,1,0:T(8,128)(2,1)S(1)} %pad_maximum_fusion.5.refs_0_), channel_id=1, source_target_pairs={{0,8},{8,0},{1,9},{9,1},{2,10},{10,2},{3,11},{11,3},{4,12},{12,4},... | collective-permute-start | bytes 2752520 | tf_op jit(solution)/shard_map/ppermute | solution.py:392
  67.0 12.2 %collective-permute-start.10 = (bf16[2,4,112,512]{3,2,1,0:T(8,128)(2,1)}, bf16[2,4,112,512]{3,2,1,0:T(8,128)(2,1)}, u32[]{:S(2)}, u32[]{:S(2)}) collective-permute-start(bf16[2,4,112,512]{3,2,1,0:T(8,128)(2,1)} %collective-permute-done.6.refs_3_), channel_id=1, source_target_pairs={{0,8},{8,0},{1,9},{9,1},{2,10},{10,2},{3,11},{11,3},{4,12},{12,4},... | collective-permute-start | bytes 2752520 | tf_op jit(solution)/shard_map/ppermute | solution.py:392
  67.1 12.2 %collective-permute-start.8 = (bf16[2,4,112,512]{3,2,1,0:T(8,128)(2,1)}, bf16[2,4,112,512]{3,2,1,0:T(8,128)(2,1)}, u32[]{:S(2)}, u32[]{:S(2)}) collective-permute-start(bf16[2,4,112,512]{3,2,1,0:T(8,128)(2,1)} %collective-permute-done.4.refs_1_), channel_id=1, source_target_pairs={{0,8},{8,0},{1,9},{9,1},{2,10},{10,2},{3,11},{11,3},{4,12},{12,4},... | collective-permute-start | bytes 2752520 | tf_op jit(solution)/shard_map/ppermute | solution.py:392
  68.3 74.2 %all-gather.12.cloned.1.call-start = ((), (), s32[]{:S(2)}) async-start(), calls=%async_computation.6 | async-start | bytes 1638400 | tf_op jit(solution)/shard_map/all_gather | solution.py:610
  74.9 23.9 %collective-permute-start.11 = (bf16[4,160,512]{2,1,0:T(8,128)(2,1)S(1)}, bf16[4,160,512]{2,1,0:T(8,128)(2,1)}, u32[]{:S(2)}, u32[]{:S(2)}) collective-permute-start(bf16[4,160,512]{2,1,0:T(8,128)(2,1)S(1)} %get-tuple-element.122), channel_id=1, source_target_pairs={{0,1},{1,0},{2,3},{3,2},{4,5},{5,4},{6,7},{7,6},{8,9},{9,8},{10,11... | collective-permute-start | bytes 1966088 | tf_op jit(solution)/shard_map/ppermute | solution.py:392
  76.4 22.4 %collective-permute-start.12 = (bf16[4,160,512]{2,1,0:T(8,128)(2,1)}, bf16[4,160,512]{2,1,0:T(8,128)(2,1)}, u32[]{:S(2)}, u32[]{:S(2)}) collective-permute-start(bf16[4,160,512]{2,1,0:T(8,128)(2,1)} %get-tuple-element.124), channel_id=1, source_target_pairs={{0,16},{16,0},{1,17},{17,1},{2,18},{18,2},{3,19},{19,3},{4,20},{20... | collective-permute-start | bytes 1966088 | tf_op jit(solution)/shard_map/ppermute | solution.py:392
  78.0 9.8 %collective-permute-start = (bf16[2,1024]{1,0:T(2,128)(2,1)S(1)}, bf16[2,1024]{1,0:T(2,128)(2,1)S(1)}, u32[]{:S(2)}, u32[]{:S(2)}) collective-permute-start(bf16[2,1024]{1,0:T(2,128)(2,1)S(1)} %bitcast.515), channel_id=1, source_target_pairs={{0,8},{8,16},{16,24},{1,9},{9,17},{17,25},{2,10},{10,18},{18,26},{... | collective-permute-start | bytes 12296 | tf_op jit(solution)/shard_map/ppermute | solution.py:347
  101.1 31.4 %collective-permute-start.16 = (bf16[2,4,160,512]{3,2,1,0:T(8,128)(2,1)S(1)}, bf16[2,4,160,512]{3,2,1,0:T(8,128)(2,1)}, u32[]{:S(2)}, u32[]{:S(2)}) collective-permute-start(bf16[2,4,160,512]{3,2,1,0:T(8,128)(2,1)S(1)} %pad_maximum_fusion.3.refs_2_), channel_id=1, source_target_pairs={{0,1},{1,0},{2,3},{3,2},{4,5},{5,4},{6,7},{7,6},{8,9},{9,8},{10,11... | collective-permute-start | bytes 3932168 | tf_op jit(solution)/shard_map/ppermute | solution.py:392
  104.0 32.2 %collective-permute-start.15 = (bf16[2,4,160,512]{3,2,1,0:T(8,128)(2,1)}, bf16[2,4,160,512]{3,2,1,0:T(8,128)(2,1)}, u32[]{:S(2)}, u32[]{:S(2)}) collective-permute-start(bf16[2,4,160,512]{3,2,1,0:T(8,128)(2,1)} %pad_maximum_fusion.2.refs_0_), channel_id=1, source_target_pairs={{0,16},{16,0},{1,17},{17,1},{2,18},{18,2},{3,19},{19,3},{4,20},{20... | collective-permute-start | bytes 3932168 | tf_op jit(solution)/shard_map/ppermute | solution.py:392
  108.6 226.1 %reduce-scatter.5.cloned.1.call-start = ((), (), s32[]{:S(2)}) async-start(), calls=%async_computation.3 | async-start | bytes 1638400 | tf_op jit(solution)/shard_map/reduce_scatter | solution.py:519
  108.6 36.3 %collective-permute-start.18 = (bf16[2,4,160,512]{3,2,1,0:T(8,128)(2,1)S(1)}, bf16[2,4,160,512]{3,2,1,0:T(8,128)(2,1)}, u32[]{:S(2)}, u32[]{:S(2)}) collective-permute-start(bf16[2,4,160,512]{3,2,1,0:T(8,128)(2,1)S(1)} %pad_maximum_fusion.3.refs_2_), channel_id=1, source_target_pairs={{0,8},{8,0},{1,9},{9,1},{2,10},{10,2},{3,11},{11,3},{4,12},{12,4},... | collective-permute-start | bytes 3932168 | tf_op jit(solution)/shard_map/ppermute | solution.py:392
  108.7 37.7 %collective-permute-start.17 = (bf16[2,4,160,512]{3,2,1,0:T(8,128)(2,1)}, bf16[2,4,160,512]{3,2,1,0:T(8,128)(2,1)}, u32[]{:S(2)}, u32[]{:S(2)}) collective-permute-start(bf16[2,4,160,512]{3,2,1,0:T(8,128)(2,1)} %pad_maximum_fusion.2.refs_0_), channel_id=1, source_target_pairs={{0,8},{8,0},{1,9},{9,1},{2,10},{10,2},{3,11},{11,3},{4,12},{12,4},... | collective-permute-start | bytes 3932168 | tf_op jit(solution)/shard_map/ppermute | solution.py:392
  132.5 24.1 %collective-permute-start.20 = (bf16[2,4,160,512]{3,2,1,0:T(8,128)(2,1)}, bf16[2,4,160,512]{3,2,1,0:T(8,128)(2,1)}, u32[]{:S(2)}, u32[]{:S(2)}) collective-permute-start(bf16[2,4,160,512]{3,2,1,0:T(8,128)(2,1)} %collective-permute-done.16.refs_3_), channel_id=1, source_target_pairs={{0,8},{8,0},{1,9},{9,1},{2,10},{10,2},{3,11},{11,3},{4,12},{12,4},... | collective-permute-start | bytes 3932168 | tf_op jit(solution)/shard_map/ppermute | solution.py:392
  136.1 20.5 %collective-permute-start.19 = (bf16[2,4,160,512]{3,2,1,0:T(8,128)(2,1)}, bf16[2,4,160,512]{3,2,1,0:T(8,128)(2,1)}, u32[]{:S(2)}, u32[]{:S(2)}) collective-permute-start(bf16[2,4,160,512]{3,2,1,0:T(8,128)(2,1)} %collective-permute-done.15.refs_1_), channel_id=1, source_target_pairs={{0,8},{8,0},{1,9},{9,1},{2,10},{10,2},{3,11},{11,3},{4,12},{12,4},... | collective-permute-start | bytes 3932168 | tf_op jit(solution)/shard_map/ppermute | solution.py:392
  138.8 3.6 collective-permute-start.14
  142.6 30.8 %collective-permute-start.21 = (bf16[2,4,160,512]{3,2,1,0:T(8,128)(2,1)}, bf16[2,4,160,512]{3,2,1,0:T(8,128)(2,1)}, u32[]{:S(2)}, u32[]{:S(2)}) collective-permute-start(bf16[2,4,160,512]{3,2,1,0:T(8,128)(2,1)} %bitcast.438), channel_id=1, source_target_pairs={{0,16},{16,0},{1,17},{17,1},{2,18},{18,2},{3,19},{19,3},{4,20},{20... | collective-permute-start | bytes 3932168 | tf_op jit(solution)/shard_map/ppermute | solution.py:392
  144.9 29.9 %collective-permute-start.22 = (bf16[2,4,160,512]{3,2,1,0:T(8,128)(2,1)}, bf16[2,4,160,512]{3,2,1,0:T(8,128)(2,1)}, u32[]{:S(2)}, u32[]{:S(2)}) collective-permute-start(bf16[2,4,160,512]{3,2,1,0:T(8,128)(2,1)} %bitcast.441), channel_id=1, source_target_pairs={{0,1},{1,0},{2,3},{3,2},{4,5},{5,4},{6,7},{7,6},{8,9},{9,8},{10,11... | collective-permute-start | bytes 3932168 | tf_op jit(solution)/shard_map/ppermute | solution.py:392
  180.3 10.2 %collective-permute-start.24 = (bf16[2,4,160,512]{3,2,1,0:T(8,128)(2,1)S(1)}, bf16[2,4,160,512]{3,2,1,0:T(8,128)(2,1)S(1)}, u32[]{:S(2)}, u32[]{:S(2)}) collective-permute-start(bf16[2,4,160,512]{3,2,1,0:T(8,128)(2,1)S(1)} %bitcast.439), channel_id=1, source_target_pairs={{0,8},{8,0},{1,9},{9,1},{2,10},{10,2},{3,11},{11,3},{4,12},{12,4},... | collective-permute-start | bytes 3932168 | tf_op jit(solution)/shard_map/ppermute | solution.py:392
  181.4 10.2 %collective-permute-start.25 = (bf16[2,4,160,512]{3,2,1,0:T(8,128)(2,1)S(1)}, bf16[2,4,160,512]{3,2,1,0:T(8,128)(2,1)S(1)}, u32[]{:S(2)}, u32[]{:S(2)}) collective-permute-start(bf16[2,4,160,512]{3,2,1,0:T(8,128)(2,1)S(1)} %bitcast.442), channel_id=1, source_target_pairs={{0,8},{8,0},{1,9},{9,1},{2,10},{10,2},{3,11},{11,3},{4,12},{12,4},... | collective-permute-start | bytes 3932168 | tf_op jit(solution)/shard_map/ppermute | solution.py:392
  192.7 3.4 collective-permute-start.26
  193.1 4.9 %collective-permute-start.27 = (bf16[2,4,160,512]{3,2,1,0:T(8,128)(2,1)}, bf16[2,4,160,512]{3,2,1,0:T(8,128)(2,1)}, u32[]{:S(2)}, u32[]{:S(2)}) collective-permute-start(bf16[2,4,160,512]{3,2,1,0:T(8,128)(2,1)} %collective-permute-done.22.refs_3_), channel_id=1, source_target_pairs={{0,8},{8,0},{1,9},{9,1},{2,10},{10,2},{3,11},{11,3},{4,12},{12,4},... | collective-permute-start | bytes 3932168 | tf_op jit(solution)/shard_map/ppermute | solution.py:392
  225.2 9.0 %collective-permute-start.28 = (bf16[4096,512]{1,0:T(8,128)(2,1)}, bf16[4096,512]{1,0:T(8,128)(2,1)}, u32[]{:S(2)}, u32[]{:S(2)}) collective-permute-start(bf16[4096,512]{1,0:T(8,128)(2,1)} %bitcast_convert_fusion.1), channel_id=1, source_target_pairs={{0,8},{8,0},{1,9},{9,1},{2,10},{10,2},{3,11},{11,3},{4,12},{12,4},... | collective-permute-start | bytes 12582920 | tf_op jit(solution)/shard_map/ppermute | solution.py:392
  227.5 6.6 %collective-permute-start.29 = (bf16[1024,512]{1,0:T(8,128)(2,1)}, bf16[1024,512]{1,0:T(8,128)(2,1)}, u32[]{:S(2)}, u32[]{:S(2)}) collective-permute-start(bf16[1024,512]{1,0:T(8,128)(2,1)} %bitcast_convert_fusion.6), channel_id=1, source_target_pairs={{0,8},{8,0},{1,9},{9,1},{2,10},{10,2},{3,11},{11,3},{4,12},{12,4},... | collective-permute-start | bytes 3145736 | tf_op jit(solution)/shard_map/ppermute | solution.py:392
  246.0 31.9 %collective-permute-start.31 = (bf16[4,2,2,128,512]{4,3,0,1,2:T(8,128)(2,1)}, bf16[4,2,2,128,512]{4,3,0,1,2:T(8,128)(2,1)}, u32[]{:S(2)}, u32[]{:S(2)}) collective-permute-start(bf16[4,2,2,128,512]{4,3,0,1,2:T(8,128)(2,1)} %bitcast_select_fusion.2), channel_id=1, source_target_pairs={{0,1},{1,0},{2,3},{3,2},{4,5},{5,4},{6,7},{7,6},{8,24},{9,25},{10,... | collective-permute-start | bytes 6291464 | tf_op jit(solution)/shard_map/ppermute | solution.py:407
  263.4 14.5 %collective-permute-start.32 = (bf16[4,2,2,32,512]{4,3,0,1,2:T(8,128)(2,1)S(1)}, bf16[4,2,2,32,512]{4,3,0,1,2:T(8,128)(2,1)S(1)}, u32[]{:S(2)}, u32[]{:S(2)}) collective-permute-start(bf16[4,2,2,32,512]{4,3,0,1,2:T(8,128)(2,1)S(1)} %copy-done.77), channel_id=1, source_target_pairs={{0,1},{1,0},{2,3},{3,2},{4,5},{5,4},{6,7},{7,6},{8,24},{9,25},{10,... | collective-permute-start | bytes 1572872 | tf_op jit(solution)/shard_map/ppermute | solution.py:407
  264.8 7.4 %collective-permute-start.30 = (f32[2,1024]{1,0:T(2,128)S(1)}, f32[2,1024]{1,0:T(2,128)S(1)}, u32[]{:S(2)}, u32[]{:S(2)}) collective-permute-start(f32[2,1024]{1,0:T(2,128)S(1)} %bitcast.513), channel_id=1, source_target_pairs={{8,0},{16,8},{24,16},{9,1},{17,9},{25,17},{10,2},{18,10},{26,18},{... | collective-permute-start | bytes 24584 | tf_op jit(solution)/shard_map/ppermute | solution.py:347
  270.6 31.8 %collective-permute-start.35 = (bf16[1024,2048]{1,0:T(8,128)(2,1)}, bf16[1024,2048]{1,0:T(8,128)(2,1)}, u32[]{:S(2)}, u32[]{:S(2)}) collective-permute-start(bf16[1024,2048]{1,0:T(8,128)(2,1)} %bitcast_convert_fusion), channel_id=1, source_target_pairs={{0,8},{8,0},{1,9},{9,1},{2,10},{10,2},{3,11},{11,3},{4,12},{12,4},... | collective-permute-start | bytes 12582920 | tf_op jit(solution)/shard_map/ppermute | solution.py:392
  280.9 18.7 %collective-permute-start.36 = (bf16[4,2,128,512]{3,2,0,1:T(8,128)(2,1)S(1)}, bf16[4,2,128,512]{3,2,0,1:T(8,128)(2,1)S(1)}, u32[]{:S(2)}, u32[]{:S(2)}) collective-permute-start(bf16[4,2,128,512]{3,2,0,1:T(8,128)(2,1)S(1)} %dynamic-slice_bitcast_fusion.3), channel_id=1, source_target_pairs={{0,16},{1,17},{2,18},{3,19},{4,20},{5,21},{6,22},{7,23},{8,9},{9,8... | collective-permute-start | bytes 3145736 | tf_op jit(solution)/shard_map/ppermute | solution.py:407
  283.8 15.7 %collective-permute-start.37 = (bf16[4,2,32,512]{3,2,0,1:T(8,128)(2,1)S(1)}, bf16[4,2,32,512]{3,2,0,1:T(8,128)(2,1)S(1)}, u32[]{:S(2)}, u32[]{:S(2)}) collective-permute-start(bf16[4,2,32,512]{3,2,0,1:T(8,128)(2,1)S(1)} %dynamic-slice_bitcast_fusion.18), channel_id=1, source_target_pairs={{0,16},{1,17},{2,18},{3,19},{4,20},{5,21},{6,22},{7,23},{8,9},{9,8... | collective-permute-start | bytes 786440 | tf_op jit(solution)/shard_map/ppermute | solution.py:407
  290.0 2.8 collective-permute-start.33
  292.9 6.5 %collective-permute-start.34 = (f32[2,2,1024]{2,1,0:T(2,128)S(1)}, f32[2,2,1024]{2,1,0:T(2,128)S(1)}, u32[]{:S(2)}, u32[]{:S(2)}) collective-permute-start(f32[2,2,1024]{2,1,0:T(2,128)S(1)} %select_add_fusion), channel_id=1, source_target_pairs={{16,0},{17,1},{18,2},{19,3},{20,4},{21,5},{22,6},{23,7},{24,8},{25... | collective-permute-start | bytes 49160 | tf_op jit(solution)/shard_map/ppermute | solution.py:347
  296.0 5.3 %collective-permute-start.39 = (bf16[1024,512]{1,0:T(8,128)(2,1)}, bf16[1024,512]{1,0:T(8,128)(2,1)}, u32[]{:S(2)}, u32[]{:S(2)}) collective-permute-start(bf16[1024,512]{1,0:T(8,128)(2,1)} %bitcast_convert_fusion.4), channel_id=1, source_target_pairs={{0,8},{8,0},{1,9},{9,1},{2,10},{10,2},{3,11},{11,3},{4,12},{12,4},... | collective-permute-start | bytes 3145736 | tf_op jit(solution)/shard_map/ppermute | solution.py:392
  299.4 3.0 collective-permute-start.38
  301.2 128.7 %reduce-scatter.3.cloned.1.call-start = ((), (), s32[]{:S(2)}) async-start(), calls=%async_computation.2 | async-start | bytes 1966080 | tf_op jit(solution)/shard_map/reduce_scatter | solution.py:519
  312.9 37.6 %collective-permute-start.42 = (bf16[4,2,2,32,2048]{4,3,0,1,2:T(8,128)(2,1)}, bf16[4,2,2,32,2048]{4,3,0,1,2:T(8,128)(2,1)}, u32[]{:S(2)}, u32[]{:S(2)}) collective-permute-start(bf16[4,2,2,32,2048]{4,3,0,1,2:T(8,128)(2,1)} %bitcast_select_fusion), channel_id=1, source_target_pairs={{0,1},{1,0},{2,3},{3,2},{4,5},{5,4},{6,7},{7,6},{8,24},{9,25},{10,... | collective-permute-start | bytes 6291464 | tf_op jit(solution)/shard_map/ppermute | solution.py:407
  322.6 22.2 %collective-permute-start.44 = (bf16[4,2,2,32,512]{4,3,0,1,2:T(8,128)(2,1)}, bf16[4,2,2,32,512]{4,3,0,1,2:T(8,128)(2,1)}, u32[]{:S(2)}, u32[]{:S(2)}) collective-permute-start(bf16[4,2,2,32,512]{4,3,0,1,2:T(8,128)(2,1)} %get-tuple-element.172), channel_id=1, source_target_pairs={{0,1},{1,0},{2,3},{3,2},{4,5},{5,4},{6,7},{7,6},{8,24},{9,25},{10,... | collective-permute-start | bytes 1572872 | tf_op jit(solution)/shard_map/ppermute | solution.py:407
  323.3 27.2 %collective-permute-start.43 = (bf16[4,2,2,32,512]{4,3,0,1,2:T(8,128)(2,1)}, bf16[4,2,2,32,512]{4,3,0,1,2:T(8,128)(2,1)}, u32[]{:S(2)}, u32[]{:S(2)}) collective-permute-start(bf16[4,2,2,32,512]{4,3,0,1,2:T(8,128)(2,1)} %get-tuple-element.169), channel_id=1, source_target_pairs={{0,1},{1,0},{2,3},{3,2},{4,5},{5,4},{6,7},{7,6},{8,24},{9,25},{10,... | collective-permute-start | bytes 1572872 | tf_op jit(solution)/shard_map/ppermute | solution.py:407
  336.6 22.3 %collective-permute-start.41 = (bf16[1024,512]{1,0:T(8,128)(2,1)S(1)}, bf16[1024,512]{1,0:T(8,128)(2,1)S(1)}, u32[]{:S(2)}, u32[]{:S(2)}) collective-permute-start(bf16[1024,512]{1,0:T(8,128)(2,1)S(1)} %copy-done.90), channel_id=1, source_target_pairs={{0,8},{8,0},{1,9},{9,1},{2,10},{10,2},{3,11},{11,3},{4,12},{12,4},... | collective-permute-start | bytes 3145736 | tf_op jit(solution)/shard_map/ppermute | solution.py:392
  337.1 21.8 %collective-permute-start.40 = (bf16[1024,512]{1,0:T(8,128)(2,1)S(1)}, bf16[1024,512]{1,0:T(8,128)(2,1)S(1)}, u32[]{:S(2)}, u32[]{:S(2)}) collective-permute-start(bf16[1024,512]{1,0:T(8,128)(2,1)S(1)} %bitcast_convert_fusion.3), channel_id=1, source_target_pairs={{0,8},{8,0},{1,9},{9,1},{2,10},{10,2},{3,11},{11,3},{4,12},{12,4},... | collective-permute-start | bytes 3145736 | tf_op jit(solution)/shard_map/ppermute | solution.py:392
  351.8 21.5 %collective-permute-start.47 = (bf16[4,2,32,512]{3,2,0,1:T(8,128)(2,1)S(1)}, bf16[4,2,32,512]{3,2,0,1:T(8,128)(2,1)S(1)}, u32[]{:S(2)}, u32[]{:S(2)}) collective-permute-start(bf16[4,2,32,512]{3,2,0,1:T(8,128)(2,1)S(1)} %dynamic-slice_bitcast_fusion.16), channel_id=1, source_target_pairs={{0,16},{1,17},{2,18},{3,19},{4,20},{5,21},{6,22},{7,23},{8,9},{9,8... | collective-permute-start | bytes 786440 | tf_op jit(solution)/shard_map/ppermute | solution.py:407
  355.4 17.9 %collective-permute-start.45 = (bf16[4,2,32,2048]{3,2,0,1:T(8,128)(2,1)S(1)}, bf16[4,2,32,2048]{3,2,0,1:T(8,128)(2,1)S(1)}, u32[]{:S(2)}, u32[]{:S(2)}) collective-permute-start(bf16[4,2,32,2048]{3,2,0,1:T(8,128)(2,1)S(1)} %dynamic-slice_bitcast_fusion.2), channel_id=1, source_target_pairs={{0,16},{1,17},{2,18},{3,19},{4,20},{5,21},{6,22},{7,23},{8,9},{9,8... | collective-permute-start | bytes 3145736 | tf_op jit(solution)/shard_map/ppermute | solution.py:407
  358.1 15.2 %collective-permute-start.46 = (bf16[4,2,32,512]{3,2,0,1:T(8,128)(2,1)S(1)}, bf16[4,2,32,512]{3,2,0,1:T(8,128)(2,1)S(1)}, u32[]{:S(2)}, u32[]{:S(2)}) collective-permute-start(bf16[4,2,32,512]{3,2,0,1:T(8,128)(2,1)S(1)} %dynamic-slice_bitcast_fusion.17), channel_id=1, source_target_pairs={{0,16},{1,17},{2,18},{3,19},{4,20},{5,21},{6,22},{7,23},{8,9},{9,8... | collective-permute-start | bytes 786440 | tf_op jit(solution)/shard_map/ppermute | solution.py:407
  373.3 18.6 %collective-permute-start.57 = (bf16[4,2,2,32,512]{4,3,0,1,2:T(8,128)(2,1)}, bf16[4,2,2,32,512]{4,3,0,1,2:T(8,128)(2,1)}, u32[]{:S(2)}, u32[]{:S(2)}) collective-permute-start(bf16[4,2,2,32,512]{4,3,0,1,2:T(8,128)(2,1)} %bitcast_select_fusion.4), channel_id=1, source_target_pairs={{0,1},{1,0},{2,3},{3,2},{4,5},{5,4},{6,7},{7,6},{8,24},{9,25},{10,... | collective-permute-start | bytes 1572872 | tf_op jit(solution)/shard_map/ppermute | solution.py:407
  374.8 19.8 %collective-permute-start.55 = (bf16[4,2,2,32,512]{4,3,0,1,2:T(8,128)(2,1)}, bf16[4,2,2,32,512]{4,3,0,1,2:T(8,128)(2,1)}, u32[]{:S(2)}, u32[]{:S(2)}) collective-permute-start(bf16[4,2,2,32,512]{4,3,0,1,2:T(8,128)(2,1)} %bitcast_select_fusion.5), channel_id=1, source_target_pairs={{0,1},{1,0},{2,3},{3,2},{4,5},{5,4},{6,7},{7,6},{8,24},{9,25},{10,... | collective-permute-start | bytes 1572872 | tf_op jit(solution)/shard_map/ppermute | solution.py:407
  375.9 4.4 %collective-permute-start.48 = (f32[2,1024]{1,0:T(2,128)S(1)}, f32[2,1024]{1,0:T(2,128)S(1)}, u32[]{:S(2)}, u32[]{:S(2)}) collective-permute-start(f32[2,1024]{1,0:T(2,128)S(1)} %bitcast.512), channel_id=1, source_target_pairs={{8,0},{16,8},{24,16},{9,1},{17,9},{25,17},{10,2},{18,10},{26,18},{... | collective-permute-start | bytes 24584 | tf_op jit(solution)/shard_map/ppermute | solution.py:347
  386.5 4.1 collective-permute-start.50
  390.6 10.8 %collective-permute-start.51 = (f32[11264]{0:T(1024)S(1)}, f32[11264]{0:T(1024)S(1)}, u32[]{:S(2)}, u32[]{:S(2)}) collective-permute-start(f32[11264]{0:T(1024)S(1)} %add.384), channel_id=1, source_target_pairs={{0,16},{16,0},{1,17},{17,1},{2,18},{18,2},{3,19},{19,3},{4,20},{20... | collective-permute-start | bytes 135176 | tf_op jit(solution)/shard_map/ppermute | solution.py:392
  393.8 13.4 %collective-permute-start.58 = (bf16[4,2,32,512]{3,2,0,1:T(8,128)(2,1)S(1)}, bf16[4,2,32,512]{3,2,0,1:T(8,128)(2,1)S(1)}, u32[]{:S(2)}, u32[]{:S(2)}) collective-permute-start(bf16[4,2,32,512]{3,2,0,1:T(8,128)(2,1)S(1)} %dynamic-slice_bitcast_fusion.14), channel_id=1, source_target_pairs={{0,16},{1,17},{2,18},{3,19},{4,20},{5,21},{6,22},{7,23},{8,9},{9,8... | collective-permute-start | bytes 786440 | tf_op jit(solution)/shard_map/ppermute | solution.py:407
  396.3 10.9 %collective-permute-start.56 = (bf16[4,2,32,512]{3,2,0,1:T(8,128)(2,1)S(1)}, bf16[4,2,32,512]{3,2,0,1:T(8,128)(2,1)S(1)}, u32[]{:S(2)}, u32[]{:S(2)}) collective-permute-start(bf16[4,2,32,512]{3,2,0,1:T(8,128)(2,1)S(1)} %dynamic-slice_bitcast_fusion.15), channel_id=1, source_target_pairs={{0,16},{1,17},{2,18},{3,19},{4,20},{5,21},{6,22},{7,23},{8,9},{9,8... | collective-permute-start | bytes 786440 | tf_op jit(solution)/shard_map/ppermute | solution.py:407
  401.5 7.3 %collective-permute-start.52 = (f32[11264]{0:T(1024)S(1)}, f32[11264]{0:T(1024)S(1)}, u32[]{:S(2)}, u32[]{:S(2)}) collective-permute-start(f32[11264]{0:T(1024)S(1)} %add.385), channel_id=1, source_target_pairs={{0,2},{2,4},{4,6},{6,0},{1,3},{3,5},{5,7},{7,1},{8,10},{10,12},{12... | collective-permute-start | bytes 135176 | tf_op jit(solution)/shard_map/ppermute | solution.py:392
  403.2 9.1 %collective-permute-start.53 = (f32[11264]{0:T(1024)S(1)}, f32[11264]{0:T(1024)S(1)}, u32[]{:S(2)}, u32[]{:S(2)}) collective-permute-start(f32[11264]{0:T(1024)S(1)} %add.385), channel_id=1, source_target_pairs={{0,4},{2,6},{4,0},{6,2},{1,5},{3,7},{5,1},{7,3},{8,12},{10,14},{12... | collective-permute-start | bytes 135176 | tf_op jit(solution)/shard_map/ppermute | solution.py:392
  405.2 8.2 %collective-permute-start.54 = (f32[11264]{0:T(1024)S(1)}, f32[11264]{0:T(1024)S(1)}, u32[]{:S(2)}, u32[]{:S(2)}) collective-permute-start(f32[11264]{0:T(1024)S(1)} %add.385), channel_id=1, source_target_pairs={{0,6},{2,0},{4,2},{6,4},{1,7},{3,1},{5,3},{7,5},{8,14},{10,8},{12,... | collective-permute-start | bytes 135176 | tf_op jit(solution)/shard_map/ppermute | solution.py:392
  407.4 11.2 %collective-permute-start.59 = (bf16[2,64,512]{2,1,0:T(8,128)(2,1)S(1)}, bf16[2,64,512]{2,1,0:T(8,128)(2,1)S(1)}, u32[]{:S(2)}, u32[]{:S(2)}) collective-permute-start(bf16[2,64,512]{2,1,0:T(8,128)(2,1)S(1)} %get-tuple-element.251), channel_id=1, source_target_pairs={{0,2},{2,4},{4,6},{6,0},{1,3},{3,5},{5,7},{7,1},{8,10},{10,12},{12... | collective-permute-start | bytes 393224 | tf_op jit(solution)/shard_map/ppermute | solution.py:512
  407.5 21.0 %collective-permute-start.60 = (bf16[2,64,512]{2,1,0:T(8,128)(2,1)S(1)}, bf16[2,64,512]{2,1,0:T(8,128)(2,1)S(1)}, u32[]{:S(2)}, u32[]{:S(2)}) collective-permute-start(bf16[2,64,512]{2,1,0:T(8,128)(2,1)S(1)} %get-tuple-element.252), channel_id=1, source_target_pairs={{0,4},{2,6},{4,0},{6,2},{1,5},{3,7},{5,1},{7,3},{8,12},{10,14},{12... | collective-permute-start | bytes 393224 | tf_op jit(solution)/shard_map/ppermute | solution.py:512
  408.8 19.7 %collective-permute-start.61 = (bf16[2,64,512]{2,1,0:T(8,128)(2,1)S(1)}, bf16[2,64,512]{2,1,0:T(8,128)(2,1)S(1)}, u32[]{:S(2)}, u32[]{:S(2)}) collective-permute-start(bf16[2,64,512]{2,1,0:T(8,128)(2,1)S(1)} %get-tuple-element.253), channel_id=1, source_target_pairs={{0,6},{2,0},{4,2},{6,4},{1,7},{3,1},{5,3},{7,5},{8,14},{10,8},{12,... | collective-permute-start | bytes 393224 | tf_op jit(solution)/shard_map/ppermute | solution.py:512
  (105 other events, 649.5 us)
Sparse Core Ops, SparseCore 0:
  41.0 31.6 all-gather.7
  74.8 31.6 all-gather.9
  108.7 32.3 all-gather.11
  301.4 31.9 reduce-scatter.4
  380.5 46.7 reduce-scatter.2

commit v2 on v1

--- a/solution.py
+++ b/solution.py
@@ -685,7 +685,7 @@
     squared, relu_up = (jnp.square(relu_up).astype(jnp.bfloat16), relu_up.astype(jnp.bfloat16))
     if stepwise:
         core2 = other_core([[part] for part in after(tuple(z2), (ffn_key, ffn_recept))])
-        yx2 = after(yx2, (squared, relu_up, core2))
+        yx2 = after(yx2, (ffn_key, ffn_recept))
         rest2 = other_core([part[1:] for part in yx2])
         core2 = [one + rest for one, rest in zip(core2, rest2)]
         (gate_mat,), (down_mat,) = assemble(yx2, core2, *plans[2], grid)

time: 450 us -> 438 us (0.973)
    unnamed x227 -> x213, local copies, waits for them, and re-layouts: 25.1 us -> 21.1 us
  transfers between devices with their start and end apart: 70 -> 70, of which waited for: 26 -> 24; matrix products, arithmetic and copies ran while one was open for 24% -> 25% of each run, Pallas kernels for 13% -> 13%
where the time goes in v2:
time: 438 us; the launch traced here: 431 us
  waiting for transfers between devices  104 us (24%)
  starting transfers between devices  64.7 us (15%)
  matrix products  63.5 us (14%)
  Pallas kernels  62.8 us (14%)
  other arithmetic  53.3 us (12%)
  local copies, waits for them, and re-layouts  44.7 us (10%)
  blocking collectives  21.4 us (5%)
  between operations  16.1 us (4%)
    ppermute x42, waiting for transfers between devices, spread(): lax.ppermute(block, axis, [(i, (i + k) % count) for i in range(count)])  63.9 us
    ppermute x42, starting transfers between devices, spread(): lax.ppermute(block, axis, [(i, (i + k) % count) for i in range(count)])  36 us
    dot_general x14, matrix products, outer(): jnp.einsum('nlc,nld->cd', left, right, preferred_element_type=jnp.float32)  35.4 us
    all_gather x1, blocking collectives, beside_z(): rows = lax.all_gather(own, 'z', axis=0)  21.4 us
    dot_general x5, matrix products, matmul(): return jnp.einsum(form, left, right, preferred_element_type=jnp.float32)  21.3 us
    unnamed x213, local copies, waits for them, and re-layouts  21.1 us
    pallas_call x3, Pallas kernels, assemble(): pl.pallas_call(functools.partial(assemble_kernel, entries, grid), out_sha...  21 us
    ppermute x14, waiting for transfers between devices, cross(): return lax.ppermute(block, ALL, route)  15.4 us
  transfers between devices with their start and end apart: 70, of which 24 were waited for; matrix products, arithmetic and copies ran while one was open for 25% of the time, Pallas kernels for 13%

profile of v2, /device:TPU:0, one launch (start us, length us, event | category | flops | bytes accessed | tf_op | source)
XLA Modules:
  0.0 430.5 jit_solution(8806491921996357222)
XLA Ops:
  9.1 3.0 collective-permute-start.1
  16.1 21.4 %all-gather = bf16[448,1024]{1,0:T(8,128)(2,1)S(1)} all-gather(bf16[112,1024]{1,0:T(8,128)(2,1)S(1)} %fusion.93), channel_id=2, replica_groups=mesh['y'=2,'core'=2,'z'=4,'x'=2] {'z'}, dimensions={0}, use_global_device_ids=true | all-gather | bytes 1146880 | tf_op jit(solution)/shard_map/all_gather | solution.py:412
  41.0 5.8 %collective-permute-done.5 = bf16[4,112,512]{2,1,0:T(8,128)(2,1)S(1)} collective-permute-done((bf16[4,112,512]{2,1,0:T(8,128)(2,1)S(1)}, bf16[4,112,512]{2,1,0:T(8,128)(2,1)S(1)}, u32[]{:S(2)}, u32[]{:S(2)}) %collective-permute-start.5) | collective-permute-done | bytes 458784 | tf_op jit(solution)/shard_map/ppermute | solution.py:392
  50.4 1.9 collective-permute-start.4
  52.9 14.1 %collective-permute-done.6.refs_3_ = bf16[2,4,112,512]{3,2,1,0:T(8,128)(2,1)} collective-permute-done((bf16[2,4,112,512]{3,2,1,0:T(8,128)(2,1)S(1)}, bf16[2,4,112,512]{3,2,1,0:T(8,128)(2,1)}, u32[]{:S(2)}, u32[]{:S(2)}) %collective-permute-start.6) | collective-permute-done | bytes 917536 | tf_op jit(solution)/shard_map/ppermute | solution.py:392
  68.4 4.3 all-gather.8.cloned.1.call-done
  72.7 2.2 fusion.107
  79.3 6.8 %shard_map.356 = (bf16[3,32,32,1024]{3,2,1,0:T(8,128)(2,1)}, bf16[1,32,16,1024]{3,2,1,0:T(8,128)(2,1)S(1)}) custom-call(s32[3]{0:T(128)S(1)} %pad_add_fusion.at_ref, bf16[2,4,112,512]{3,2,1,0:T(8,128)(2,1)S(1)} %pad_maximum_fusion.5.refs_0_, bf16[2,4,112,512]{3,2,1,0:T(8,128)(2,1)} %collective-permute-done.4.refs_1_, ...), custom_call_target="tpu_custom_call" | custom-call | tf_op jit(solution)/shard_map/pallas_call | solution.py:463
  87.7 10.1 %shard_map.357 = (bf16[2,256,1024]{2,1,0:T(8,128)(2,1)S(1)}, bf16[2,256,1024]{2,1,0:T(8,128)(2,1)S(1)}, bf16[2,256,1024]{2,1,0:T(8,128)(2,1)S(1)}, f32[3,2,256,1...) custom-call(s32[1]{0:T(128)} %bitcast.flag_ref, bf16[2,256,1024]{2,1,0:T(8,128)(2,1)S(1)} %copy-done.1, ...), custom_call_target="tpu_custom_call" | custom-call | flops 1048576 | bytes 65536 | tf_op jit(solution)/shard_map/pallas_call | solution.py:193
  98.8 2.2 pad_maximum_fusion.3.refs_2_
  101.7 2.3 pad_maximum_fusion.2.refs_0_
  104.0 3.8 collective-permute-start.15
  109.2 23.2 %collective-permute-done.16.refs_3_ = bf16[2,4,160,512]{3,2,1,0:T(8,128)(2,1)} collective-permute-done((bf16[2,4,160,512]{3,2,1,0:T(8,128)(2,1)S(1)}, bf16[2,4,160,512]{3,2,1,0:T(8,128)(2,1)}, u32[]{:S(2)}, u32[]{:S(2)}) %collective-permute-start.16) | collective-permute-done | bytes 1310752 | tf_op jit(solution)/shard_map/ppermute | solution.py:392
  133.0 3.2 collective-permute-done.15.refs_1_
  136.9 2.0 collective-permute-done.13
  138.9 2.4 collective-permute-start.14
  142.6 2.4 collective-permute-start.21
  146.4 2.8 copy-done
  149.2 4.7 %shard_map.358 = (f32[2,256,1024]{2,1,0:T(8,128)S(1)}, f32[2,256,1024]{2,1,0:T(8,128)S(1)}, bf16[2,256,1024]{2,1,0:T(8,128)(2,1)S(1)}) custom-call(f32[3,2,256,1024]{3,2,1,0:T(8,128)S(1)} %copy-done, f32[3,2,256,1024]{3,2,1,0:T(8,128)S(1)} %copy-done, f32[3,2,256,1024]{3,2,1,0:T(8,128)S(1)} %copy-done, f32[2,1024]{1,0:T(2,128)S(1)} %get-tuple-element.131.a0_ref, ...), custom_call_target="tpu_custom_call" | custom-call | flops 1048576 | bytes 65536 | tf_op jit(solution)/shard_map/pallas_call | solution.py:313
  156.6 7.8 %shard_map.359 = (bf16[1,32,32,1024]{3,2,1,0:T(8,128)(2,1)S(1)}, bf16[1,32,32,4096]{3,2,1,0:T(8,128)(2,1)}) custom-call(s32[3]{0:T(128)S(1)} %pad_add_fusion.at_ref, bf16[2,4,160,512]{3,2,1,0:T(8,128)(2,1)} %pad_maximum_fusion.2.refs_0_, bf16[2,4,160,512]{3,2,1,0:T(8,128)(2,1)} %collective-permute-done.15.refs_1_, ...), custom_call_target="tpu_custom_call" | custom-call | tf_op jit(solution)/shard_map/pallas_call | solution.py:463
  166.6 6.7 %collective-permute-done.21.refs_1_ = bf16[2,4,160,512]{3,2,1,0:T(8,128)(2,1)S(1)} collective-permute-done((bf16[2,4,160,512]{3,2,1,0:T(8,128)(2,1)}, bf16[2,4,160,512]{3,2,1,0:T(8,128)(2,1)S(1)}, u32[]{:S(2)}, u32[]{:S(2)}) %collective-permute-start.21) | collective-permute-done | bytes 1310752 | tf_op jit(solution)/shard_map/ppermute | solution.py:392
  174.8 1.6 copy.107
  178.5 1.7 add_convert_fusion.2
  181.9 6.9 %multiply_convert_fusion = (bf16[512,4096]{1,0:T(8,128)(2,1)}, bf16[512,4096]{1,0:T(8,128)(2,1)}) fusion(bf16[512,1024]{1,0:T(8,128)(2,1)S(1)} %bitcast.495, bf16[1024,4096]{1,0:T(8,128)(2,1)S(1)} %bitcast.470), kind=kOutput, calls=%fused_computation.6 | convolution fusion | flops 4303355904 | bytes 17825792 | tf_op jit(solution)/shard_map/dot_general | solution.py:684
  189.6 6.5 %shard_map.360 = (bf16[1,32,32,1024]{3,2,1,0:T(8,128)(2,1)S(1)}, bf16[1,32,128,1024]{3,2,1,0:T(8,128)(2,1)}) custom-call(s32[3]{0:T(128)S(1)} %pad_add_fusion.at_ref, bf16[2,4,160,512]{3,2,1,0:T(8,128)(2,1)S(1)} %bitcast.440, bf16[2,4,160,512]{3,2,1,0:T(8,128)(2,1)S(1)} %collective-permute-done.21.refs_1_, bf16[2,4,160,512]{3,2,1,0:T(8,128)(2,1)S(1)} %bitcast.443, ...), custom_call_target="tpu_custom_call" | custom-call | tf_op jit(solution)/shard_map/pallas_call | solution.py:463
  196.1 8.1 %fusion.114 = f32[2,256,1024]{2,1,0:T(8,128)S(1)} fusion(bf16[2,256,4096]{2,1,0:T(8,128)(2,1)S(1)} %bitcast.528, bf16[4096,1024,1]{1,0,2:T(8,128)(2,1)} %bitcast.471), kind=kOutput, calls=%fused_computation.326 | convolution fusion | flops 4294967296 | bytes 14680064 | tf_op jit(solution)/shard_map/nlf,fd->nld/dot_general | solution.py:341
  204.3 3.5 multiply_convert_fusion.1
  207.7 4.6 %bitcast_convert_fusion.1 = bf16[4096,512]{1,0:T(8,128)(2,1)} fusion(bf16[2,256,4096]{2,1,0:T(8,128)(2,1)S(1)} %bitcast.529, bf16[2,256,1024]{2,1,0:T(8,128)(2,1)S(1)} %get-tuple-element.158, pred[]{:T(512)S(6)} %eq.7), kind=kOutput, calls=%fused_computation.5 | convolution fusion | flops 2149842944 | bytes 9437185 | tf_op jit(solution)/shard_map/nlc,nld->cd/dot_general | solution.py:700
  215.7 2.4 bitcast_convert_fusion.6
  220.4 2.6 fusion.115
  225.2 5.1 %fusion.1 = bf16[4096,512]{1,0:T(8,128)(2,1)S(1)} fusion(bf16[4096,512]{1,0:T(8,128)(2,1)} %collective-permute-done.28, bf16[2,256,4096]{2,1,0:T(8,128)(2,1)S(1)} %bitcast.530, bf16[2,256,1024]{2,1,0:T(8,128)(2,1)S(1)} %get-tuple-element.158, pred[]{:T(512)S(6)} %eq.6), kind=kOutput, calls=%fused_computation.4 | convolution fusion | flops 2154037248 | bytes 13631489 | tf_op jit(solution)/shard_map/nlc,nld->cd/dot_general | solution.py:700
  232.5 1.6 bitcast_select_fusion.2
  235.6 13.5 %shard_map.361 = (bf16[512,4096]{1,0:T(8,128)(2,1)S(1)}, f32[512,1024]{1,0:T(8,128)S(1)}) custom-call(bf16[512,1024]{1,0:T(8,128)(2,1)S(1)} %bitcast.447, bf16[512,4096]{1,0:T(8,128)(2,1)S(1)} %maximum_convert_fusion.relu_ref, bf16[4096,1024]{1,0:T(8,128)(2,1)} %bitcast.472, bf16[1024,4096]{1,0:T(8,128)(2,1)} %bitcast.467), custom_call_target="tpu_custom_call" | custom-call | flops 1048576 | bytes 25165824 | tf_op jit(solution)/shard_map/pallas_call | solution.py:236
  253.5 4.5 %bitcast_convert_fusion = bf16[1024,2048]{1,0:T(8,128)(2,1)} fusion(bf16[2,256,1024]{2,1,0:T(8,128)(2,1)S(1)} %copy-done.66, bf16[2,256,4096]{2,1,0:T(8,128)(2,1)S(1)} %bitcast.451, pred[]{:T(512)S(6)} %eq.7), kind=kOutput, calls=%fused_computation.2 | convolution fusion | flops 2150629376 | bytes 9437185 | tf_op jit(solution)/shard_map/nlc,nld->cd/dot_general | solution.py:700
  259.1 1.7 multiply_reduce_fusion.2
  262.1 3.8 collective-permute-done.32
  266.0 2.8 add_convert_fusion.1
  268.9 2.4 collective-permute-start.36
  271.8 5.7 %fusion.25 = (bf16[2,256,1024]{2,1,0:T(8,128)(2,1)S(1)}, f32[2,256,1024]{2,1,0:T(8,128)S(1)}, f32[2,256,1024]{2,1,0:T(8,128)S(1)}, f32[2,256,1024]{2,1,0:T(8,128)}) fusion(f32[3,2,256,1024]{3,2,1,0:T(8,128)} %get-tuple-element.114.k_ref.v_ref.r_ref, f32[2,256,1024]{2,1,0:T(8,128)S(1)} %copy-done.5, f32[2,256,1024]{2,1,0:T(8,128)S(1)} %copy-done.3, ...), kind=kOutput, calls=%fused_computation.60 | convolution fusion | flops 1082654720 | bytes 22024192 | tf_op jit(solution)/shard_map/nld,cd->nlc/dot_general | solution.py:341
  279.1 1.8 bitcast_convert_fusion.5
  282.2 1.7 bitcast_convert_fusion.4
  283.9 3.4 collective-permute-done.34
  290.3 6.2 %fusion = bf16[1024,2048]{1,0:T(8,128)(2,1)S(1)} fusion(bf16[1024,2048]{1,0:T(8,128)(2,1)} %collective-permute-done.35, bf16[2,256,1024]{2,1,0:T(8,128)(2,1)} %copy-done.65, bf16[2,256,4096]{2,1,0:T(8,128)(2,1)} %bitcast.452, pred[]{:T(512)S(6)} %eq.6), kind=kOutput, calls=%fused_computation.1 | convolution fusion | flops 2154823680 | bytes 13631489 | tf_op jit(solution)/shard_map/nlc,nld->cd/dot_general | solution.py:700
  296.5 2.0 dynamic-slice_bitcast_fusion
  302.2 2.1 fusion.19
  306.1 2.3 fusion.18
  312.5 6.3 %shard_map.362 = (bf16[2,256,1024]{2,1,0:T(8,128)(2,1)S(1)}, bf16[2,256,1024]{2,1,0:T(8,128)(2,1)S(1)}, f32[1,1024]{1,0:T(1,128)S(1)}, f32[1,1024]{1,0:T(1,128)S(1)}) custom-call(f32[3,2,256,1024]{3,2,1,0:T(8,128)S(1)} %bitcast.433, f32[3,2,256,1024]{3,2,1,0:T(8,128)S(1)} %bitcast.433, f32[3,2,256,1024]{3,2,1,0:T(8,128)S(1)} %bitcast.433, ...), custom_call_target="tpu_custom_call" | custom-call | flops 1048576 | bytes 65536 | tf_op jit(solution)/shard_map/pallas_call | solution.py:327
  320.8 1.8 bitcast_convert_fusion.2
  326.8 5.9 %collective-permute-done.44 = bf16[4,2,2,32,512]{4,3,0,1,2:T(8,128)(2,1)} collective-permute-done((bf16[4,2,2,32,512]{4,3,0,1,2:T(8,128)(2,1)}, bf16[4,2,2,32,512]{4,3,0,1,2:T(8,128)(2,1)}, u32[]{:S(2)}, u32[]{:S(2)}) %collective-permute-start.44) | collective-permute-done | bytes 524320 | tf_op jit(solution)/shard_map/ppermute | solution.py:407
  332.7 5.6 %collective-permute-done.43 = bf16[4,2,2,32,512]{4,3,0,1,2:T(8,128)(2,1)} collective-permute-done((bf16[4,2,2,32,512]{4,3,0,1,2:T(8,128)(2,1)}, bf16[4,2,2,32,512]{4,3,0,1,2:T(8,128)(2,1)}, u32[]{:S(2)}, u32[]{:S(2)}) %collective-permute-start.43) | collective-permute-done | bytes 524320 | tf_op jit(solution)/shard_map/ppermute | solution.py:407
  340.5 2.6 add_convert_fusion
  350.5 7.1 %shard_map.363 = (f32[512,1024]{1,0:T(8,128)S(1)}, f32[512,1024]{1,0:T(8,128)S(1)}, f32[3,1024]{1,0:T(4,128)S(1)}) custom-call(bf16[512,1024]{1,0:T(8,128)(2,1)S(1)} %bitcast.445, bf16[512,1024]{1,0:T(8,128)(2,1)S(1)} %bitcast.446, bf16[512,1024]{1,0:T(8,128)(2,1)S(1)} %bitcast.444, f32[512,1024]{1,0:T(8,128)S(1)} %copy-done.8, ...), custom_call_target="tpu_custom_call" | custom-call | flops 1048576 | bytes 8388608 | tf_op jit(solution)/shard_map/pallas_call | solution.py:280
  365.3 1.7 slice.431
  368.3 2.6 fusion.11
  375.9 2.6 collective-permute-done.50
  379.8 1.8 add_convert_fusion.4
  382.4 1.7 add_convert_fusion.5
  385.4 3.9 fusion.10
  389.3 1.7 collective-permute-start.52
  391.0 2.0 collective-permute-start.53
  393.0 2.0 collective-permute-start.54
  396.6 3.5 collective-permute-start.61
  401.2 5.2 %collective-permute-done.59 = bf16[2,64,512]{2,1,0:T(8,128)(2,1)S(1)} collective-permute-done((bf16[2,64,512]{2,1,0:T(8,128)(2,1)S(1)}, bf16[2,64,512]{2,1,0:T(8,128)(2,1)S(1)}, u32[]{:S(2)}, u32[]{:S(2)}) %collective-permute-start.59) | collective-permute-done | bytes 131104 | tf_op jit(solution)/shard_map/ppermute | solution.py:512
  406.4 9.9 %collective-permute-done.60 = bf16[2,64,512]{2,1,0:T(8,128)(2,1)S(1)} collective-permute-done((bf16[2,64,512]{2,1,0:T(8,128)(2,1)S(1)}, bf16[2,64,512]{2,1,0:T(8,128)(2,1)S(1)}, u32[]{:S(2)}, u32[]{:S(2)}) %collective-permute-start.60) | collective-permute-done | bytes 131104 | tf_op jit(solution)/shard_map/ppermute | solution.py:512
  (471 shorter events, 115.0 us)
Async XLA Ops:
  7.2 65.5 %all-gather.8.cloned.1.call-start = ((), (), s32[]{:S(2)}) async-start(), calls=%async_computation.4 | async-start | bytes 1638400 | tf_op jit(solution)/shard_map/all_gather | solution.py:412
  9.1 28.5 %collective-permute-start.1 = (bf16[160,512]{1,0:T(8,128)(2,1)S(1)}, bf16[160,512]{1,0:T(8,128)(2,1)S(1)}, u32[]{:S(2)}, u32[]{:S(2)}) collective-permute-start(bf16[160,512]{1,0:T(8,128)(2,1)S(1)} %get-tuple-element.127), channel_id=1, source_target_pairs={{0,1},{1,0},{2,3},{3,2},{4,5},{5,4},{6,7},{7,6},{8,9},{9,8},{10,11... | collective-permute-start | bytes 491528 | tf_op jit(solution)/shard_map/ppermute | solution.py:392
  12.1 25.5 %collective-permute-start.2 = (bf16[160,512]{1,0:T(8,128)(2,1)S(1)}, bf16[160,512]{1,0:T(8,128)(2,1)S(1)}, u32[]{:S(2)}, u32[]{:S(2)}) collective-permute-start(bf16[160,512]{1,0:T(8,128)(2,1)S(1)} %get-tuple-element.129), channel_id=1, source_target_pairs={{0,16},{16,0},{1,17},{17,1},{2,18},{18,2},{3,19},{19,3},{4,20},{20... | collective-permute-start | bytes 491528 | tf_op jit(solution)/shard_map/ppermute | solution.py:392
  38.3 8.5 %collective-permute-start.5 = (bf16[4,112,512]{2,1,0:T(8,128)(2,1)S(1)}, bf16[4,112,512]{2,1,0:T(8,128)(2,1)S(1)}, u32[]{:S(2)}, u32[]{:S(2)}) collective-permute-start(bf16[4,112,512]{2,1,0:T(8,128)(2,1)S(1)} %get-tuple-element.111), channel_id=1, source_target_pairs={{0,16},{16,0},{1,17},{17,1},{2,18},{18,2},{3,19},{19,3},{4,20},{20... | collective-permute-start | bytes 1376264 | tf_op jit(solution)/shard_map/ppermute | solution.py:392
  38.8 10.6 %collective-permute-start.3 = (bf16[4,112,512]{2,1,0:T(8,128)(2,1)S(1)}, bf16[4,112,512]{2,1,0:T(8,128)(2,1)}, u32[]{:S(2)}, u32[]{:S(2)}) collective-permute-start(bf16[4,112,512]{2,1,0:T(8,128)(2,1)S(1)} %get-tuple-element.110), channel_id=1, source_target_pairs={{0,1},{1,0},{2,3},{3,2},{4,5},{5,4},{6,7},{7,6},{8,9},{9,8},{10,11... | collective-permute-start | bytes 1376264 | tf_op jit(solution)/shard_map/ppermute | solution.py:392
  40.9 101.6 %all-gather.10.cloned.1.call-start = ((), (), s32[]{:S(2)}) async-start(), calls=%async_computation.5 | async-start | bytes 1638400 | tf_op jit(solution)/shard_map/all_gather | solution.py:610
  48.8 18.3 %collective-permute-start.6 = (bf16[2,4,112,512]{3,2,1,0:T(8,128)(2,1)S(1)}, bf16[2,4,112,512]{3,2,1,0:T(8,128)(2,1)}, u32[]{:S(2)}, u32[]{:S(2)}) collective-permute-start(bf16[2,4,112,512]{3,2,1,0:T(8,128)(2,1)S(1)} %pad_maximum_fusion.6.refs_2_), channel_id=1, source_target_pairs={{0,1},{1,0},{2,3},{3,2},{4,5},{5,4},{6,7},{7,6},{8,9},{9,8},{10,11... | collective-permute-start | bytes 2752520 | tf_op jit(solution)/shard_map/ppermute | solution.py:392
  50.4 16.6 %collective-permute-start.4 = (bf16[2,4,112,512]{3,2,1,0:T(8,128)(2,1)S(1)}, bf16[2,4,112,512]{3,2,1,0:T(8,128)(2,1)}, u32[]{:S(2)}, u32[]{:S(2)}) collective-permute-start(bf16[2,4,112,512]{3,2,1,0:T(8,128)(2,1)S(1)} %pad_maximum_fusion.5.refs_0_), channel_id=1, source_target_pairs={{0,16},{16,0},{1,17},{17,1},{2,18},{18,2},{3,19},{19,3},{4,20},{20... | collective-permute-start | bytes 2752520 | tf_op jit(solution)/shard_map/ppermute | solution.py:392
  52.4 24.1 %collective-permute-start.9 = (bf16[2,4,112,512]{3,2,1,0:T(8,128)(2,1)S(1)}, bf16[2,4,112,512]{3,2,1,0:T(8,128)(2,1)}, u32[]{:S(2)}, u32[]{:S(2)}) collective-permute-start(bf16[2,4,112,512]{3,2,1,0:T(8,128)(2,1)S(1)} %pad_maximum_fusion.6.refs_2_), channel_id=1, source_target_pairs={{0,8},{8,0},{1,9},{9,1},{2,10},{10,2},{3,11},{11,3},{4,12},{12,4},... | collective-permute-start | bytes 2752520 | tf_op jit(solution)/shard_map/ppermute | solution.py:392
  52.4 25.6 %collective-permute-start.7 = (bf16[2,4,112,512]{3,2,1,0:T(8,128)(2,1)S(1)}, bf16[2,4,112,512]{3,2,1,0:T(8,128)(2,1)}, u32[]{:S(2)}, u32[]{:S(2)}) collective-permute-start(bf16[2,4,112,512]{3,2,1,0:T(8,128)(2,1)S(1)} %pad_maximum_fusion.5.refs_0_), channel_id=1, source_target_pairs={{0,8},{8,0},{1,9},{9,1},{2,10},{10,2},{3,11},{11,3},{4,12},{12,4},... | collective-permute-start | bytes 2752520 | tf_op jit(solution)/shard_map/ppermute | solution.py:392
  67.0 12.2 %collective-permute-start.10 = (bf16[2,4,112,512]{3,2,1,0:T(8,128)(2,1)}, bf16[2,4,112,512]{3,2,1,0:T(8,128)(2,1)}, u32[]{:S(2)}, u32[]{:S(2)}) collective-permute-start(bf16[2,4,112,512]{3,2,1,0:T(8,128)(2,1)} %collective-permute-done.6.refs_3_), channel_id=1, source_target_pairs={{0,8},{8,0},{1,9},{9,1},{2,10},{10,2},{3,11},{11,3},{4,12},{12,4},... | collective-permute-start | bytes 2752520 | tf_op jit(solution)/shard_map/ppermute | solution.py:392
  67.1 12.2 %collective-permute-start.8 = (bf16[2,4,112,512]{3,2,1,0:T(8,128)(2,1)}, bf16[2,4,112,512]{3,2,1,0:T(8,128)(2,1)}, u32[]{:S(2)}, u32[]{:S(2)}) collective-permute-start(bf16[2,4,112,512]{3,2,1,0:T(8,128)(2,1)} %collective-permute-done.4.refs_1_), channel_id=1, source_target_pairs={{0,8},{8,0},{1,9},{9,1},{2,10},{10,2},{3,11},{11,3},{4,12},{12,4},... | collective-permute-start | bytes 2752520 | tf_op jit(solution)/shard_map/ppermute | solution.py:392
  68.3 74.3 %all-gather.12.cloned.1.call-start = ((), (), s32[]{:S(2)}) async-start(), calls=%async_computation.6 | async-start | bytes 1638400 | tf_op jit(solution)/shard_map/all_gather | solution.py:610
  74.9 23.9 %collective-permute-start.11 = (bf16[4,160,512]{2,1,0:T(8,128)(2,1)S(1)}, bf16[4,160,512]{2,1,0:T(8,128)(2,1)}, u32[]{:S(2)}, u32[]{:S(2)}) collective-permute-start(bf16[4,160,512]{2,1,0:T(8,128)(2,1)S(1)} %get-tuple-element.122), channel_id=1, source_target_pairs={{0,1},{1,0},{2,3},{3,2},{4,5},{5,4},{6,7},{7,6},{8,9},{9,8},{10,11... | collective-permute-start | bytes 1966088 | tf_op jit(solution)/shard_map/ppermute | solution.py:392
  76.4 22.4 %collective-permute-start.12 = (bf16[4,160,512]{2,1,0:T(8,128)(2,1)}, bf16[4,160,512]{2,1,0:T(8,128)(2,1)}, u32[]{:S(2)}, u32[]{:S(2)}) collective-permute-start(bf16[4,160,512]{2,1,0:T(8,128)(2,1)} %get-tuple-element.124), channel_id=1, source_target_pairs={{0,16},{16,0},{1,17},{17,1},{2,18},{18,2},{3,19},{19,3},{4,20},{20... | collective-permute-start | bytes 1966088 | tf_op jit(solution)/shard_map/ppermute | solution.py:392
  78.0 9.7 %collective-permute-start = (bf16[2,1024]{1,0:T(2,128)(2,1)S(1)}, bf16[2,1024]{1,0:T(2,128)(2,1)S(1)}, u32[]{:S(2)}, u32[]{:S(2)}) collective-permute-start(bf16[2,1024]{1,0:T(2,128)(2,1)S(1)} %bitcast.515), channel_id=1, source_target_pairs={{0,8},{8,16},{16,24},{1,9},{9,17},{17,25},{2,10},{10,18},{18,26},{... | collective-permute-start | bytes 12296 | tf_op jit(solution)/shard_map/ppermute | solution.py:347
  101.0 31.4 %collective-permute-start.16 = (bf16[2,4,160,512]{3,2,1,0:T(8,128)(2,1)S(1)}, bf16[2,4,160,512]{3,2,1,0:T(8,128)(2,1)}, u32[]{:S(2)}, u32[]{:S(2)}) collective-permute-start(bf16[2,4,160,512]{3,2,1,0:T(8,128)(2,1)S(1)} %pad_maximum_fusion.3.refs_2_), channel_id=1, source_target_pairs={{0,1},{1,0},{2,3},{3,2},{4,5},{5,4},{6,7},{7,6},{8,9},{9,8},{10,11... | collective-permute-start | bytes 3932168 | tf_op jit(solution)/shard_map/ppermute | solution.py:392
  104.0 32.2 %collective-permute-start.15 = (bf16[2,4,160,512]{3,2,1,0:T(8,128)(2,1)}, bf16[2,4,160,512]{3,2,1,0:T(8,128)(2,1)}, u32[]{:S(2)}, u32[]{:S(2)}) collective-permute-start(bf16[2,4,160,512]{3,2,1,0:T(8,128)(2,1)} %pad_maximum_fusion.2.refs_0_), channel_id=1, source_target_pairs={{0,16},{16,0},{1,17},{17,1},{2,18},{18,2},{3,19},{19,3},{4,20},{20... | collective-permute-start | bytes 3932168 | tf_op jit(solution)/shard_map/ppermute | solution.py:392
  108.6 214.0 %reduce-scatter.5.cloned.1.call-start = ((), (), s32[]{:S(2)}) async-start(), calls=%async_computation.3 | async-start | bytes 1638400 | tf_op jit(solution)/shard_map/reduce_scatter | solution.py:519
  108.6 36.3 %collective-permute-start.18 = (bf16[2,4,160,512]{3,2,1,0:T(8,128)(2,1)S(1)}, bf16[2,4,160,512]{3,2,1,0:T(8,128)(2,1)}, u32[]{:S(2)}, u32[]{:S(2)}) collective-permute-start(bf16[2,4,160,512]{3,2,1,0:T(8,128)(2,1)S(1)} %pad_maximum_fusion.3.refs_2_), channel_id=1, source_target_pairs={{0,8},{8,0},{1,9},{9,1},{2,10},{10,2},{3,11},{11,3},{4,12},{12,4},... | collective-permute-start | bytes 3932168 | tf_op jit(solution)/shard_map/ppermute | solution.py:392
  108.7 37.7 %collective-permute-start.17 = (bf16[2,4,160,512]{3,2,1,0:T(8,128)(2,1)}, bf16[2,4,160,512]{3,2,1,0:T(8,128)(2,1)}, u32[]{:S(2)}, u32[]{:S(2)}) collective-permute-start(bf16[2,4,160,512]{3,2,1,0:T(8,128)(2,1)} %pad_maximum_fusion.2.refs_0_), channel_id=1, source_target_pairs={{0,8},{8,0},{1,9},{9,1},{2,10},{10,2},{3,11},{11,3},{4,12},{12,4},... | collective-permute-start | bytes 3932168 | tf_op jit(solution)/shard_map/ppermute | solution.py:392
  132.4 24.2 %collective-permute-start.20 = (bf16[2,4,160,512]{3,2,1,0:T(8,128)(2,1)}, bf16[2,4,160,512]{3,2,1,0:T(8,128)(2,1)}, u32[]{:S(2)}, u32[]{:S(2)}) collective-permute-start(bf16[2,4,160,512]{3,2,1,0:T(8,128)(2,1)} %collective-permute-done.16.refs_3_), channel_id=1, source_target_pairs={{0,8},{8,0},{1,9},{9,1},{2,10},{10,2},{3,11},{11,3},{4,12},{12,4},... | collective-permute-start | bytes 3932168 | tf_op jit(solution)/shard_map/ppermute | solution.py:392
  136.1 20.5 %collective-permute-start.19 = (bf16[2,4,160,512]{3,2,1,0:T(8,128)(2,1)}, bf16[2,4,160,512]{3,2,1,0:T(8,128)(2,1)}, u32[]{:S(2)}, u32[]{:S(2)}) collective-permute-start(bf16[2,4,160,512]{3,2,1,0:T(8,128)(2,1)} %collective-permute-done.15.refs_1_), channel_id=1, source_target_pairs={{0,8},{8,0},{1,9},{9,1},{2,10},{10,2},{3,11},{11,3},{4,12},{12,4},... | collective-permute-start | bytes 3932168 | tf_op jit(solution)/shard_map/ppermute | solution.py:392
  138.9 3.6 collective-permute-start.14
  142.6 30.7 %collective-permute-start.21 = (bf16[2,4,160,512]{3,2,1,0:T(8,128)(2,1)}, bf16[2,4,160,512]{3,2,1,0:T(8,128)(2,1)S(1)}, u32[]{:S(2)}, u32[]{:S(2)}) collective-permute-start(bf16[2,4,160,512]{3,2,1,0:T(8,128)(2,1)} %bitcast.438), channel_id=1, source_target_pairs={{0,16},{16,0},{1,17},{17,1},{2,18},{18,2},{3,19},{19,3},{4,20},{20... | collective-permute-start | bytes 3932168 | tf_op jit(solution)/shard_map/ppermute | solution.py:392
  144.9 29.8 %collective-permute-start.22 = (bf16[2,4,160,512]{3,2,1,0:T(8,128)(2,1)}, bf16[2,4,160,512]{3,2,1,0:T(8,128)(2,1)S(1)}, u32[]{:S(2)}, u32[]{:S(2)}) collective-permute-start(bf16[2,4,160,512]{3,2,1,0:T(8,128)(2,1)} %bitcast.441), channel_id=1, source_target_pairs={{0,1},{1,0},{2,3},{3,2},{4,5},{5,4},{6,7},{7,6},{8,9},{9,8},{10,11... | collective-permute-start | bytes 3932168 | tf_op jit(solution)/shard_map/ppermute | solution.py:392
  180.2 8.6 %collective-permute-start.24 = (bf16[2,4,160,512]{3,2,1,0:T(8,128)(2,1)S(1)}, bf16[2,4,160,512]{3,2,1,0:T(8,128)(2,1)S(1)}, u32[]{:S(2)}, u32[]{:S(2)}) collective-permute-start(bf16[2,4,160,512]{3,2,1,0:T(8,128)(2,1)S(1)} %bitcast.439), channel_id=1, source_target_pairs={{0,8},{8,0},{1,9},{9,1},{2,10},{10,2},{3,11},{11,3},{4,12},{12,4},... | collective-permute-start | bytes 3932168 | tf_op jit(solution)/shard_map/ppermute | solution.py:392
  181.3 7.6 %collective-permute-start.26 = (bf16[2,4,160,512]{3,2,1,0:T(8,128)(2,1)S(1)}, bf16[2,4,160,512]{3,2,1,0:T(8,128)(2,1)S(1)}, u32[]{:S(2)}, u32[]{:S(2)}) collective-permute-start(bf16[2,4,160,512]{3,2,1,0:T(8,128)(2,1)S(1)} %bitcast.442), channel_id=1, source_target_pairs={{0,8},{8,0},{1,9},{9,1},{2,10},{10,2},{3,11},{11,3},{4,12},{12,4},... | collective-permute-start | bytes 3932168 | tf_op jit(solution)/shard_map/ppermute | solution.py:392
  181.4 7.5 %collective-permute-start.25 = (bf16[2,4,160,512]{3,2,1,0:T(8,128)(2,1)S(1)}, bf16[2,4,160,512]{3,2,1,0:T(8,128)(2,1)S(1)}, u32[]{:S(2)}, u32[]{:S(2)}) collective-permute-start(bf16[2,4,160,512]{3,2,1,0:T(8,128)(2,1)S(1)} %collective-permute-done.21.refs_1_), channel_id=1, source_target_pairs={{0,8},{8,0},{1,9},{9,1},{2,10},{10,2},{3,11},{11,3},{4,12},{12,4},... | collective-permute-start | bytes 3932168 | tf_op jit(solution)/shard_map/ppermute | solution.py:392
  181.8 7.8 %collective-permute-start.27 = (bf16[2,4,160,512]{3,2,1,0:T(8,128)(2,1)S(1)}, bf16[2,4,160,512]{3,2,1,0:T(8,128)(2,1)S(1)}, u32[]{:S(2)}, u32[]{:S(2)}) collective-permute-start(bf16[2,4,160,512]{3,2,1,0:T(8,128)(2,1)S(1)} %collective-permute-done.22.refs_3_), channel_id=1, source_target_pairs={{0,8},{8,0},{1,9},{9,1},{2,10},{10,2},{3,11},{11,3},{4,12},{12,4},... | collective-permute-start | bytes 3932168 | tf_op jit(solution)/shard_map/ppermute | solution.py:392
  212.3 10.7 %collective-permute-start.28 = (bf16[4096,512]{1,0:T(8,128)(2,1)}, bf16[4096,512]{1,0:T(8,128)(2,1)}, u32[]{:S(2)}, u32[]{:S(2)}) collective-permute-start(bf16[4096,512]{1,0:T(8,128)(2,1)} %bitcast_convert_fusion.1), channel_id=1, source_target_pairs={{0,8},{8,0},{1,9},{9,1},{2,10},{10,2},{3,11},{11,3},{4,12},{12,4},... | collective-permute-start | bytes 12582920 | tf_op jit(solution)/shard_map/ppermute | solution.py:392
  218.1 4.9 %collective-permute-start.29 = (bf16[1024,512]{1,0:T(8,128)(2,1)S(1)}, bf16[1024,512]{1,0:T(8,128)(2,1)S(1)}, u32[]{:S(2)}, u32[]{:S(2)}) collective-permute-start(bf16[1024,512]{1,0:T(8,128)(2,1)S(1)} %bitcast_convert_fusion.6), channel_id=1, source_target_pairs={{0,8},{8,0},{1,9},{9,1},{2,10},{10,2},{3,11},{11,3},{4,12},{12,4},... | collective-permute-start | bytes 3145736 | tf_op jit(solution)/shard_map/ppermute | solution.py:392
  234.1 31.9 %collective-permute-start.31 = (bf16[4,2,2,128,512]{4,3,0,1,2:T(8,128)(2,1)}, bf16[4,2,2,128,512]{4,3,0,1,2:T(8,128)(2,1)}, u32[]{:S(2)}, u32[]{:S(2)}) collective-permute-start(bf16[4,2,2,128,512]{4,3,0,1,2:T(8,128)(2,1)} %bitcast_select_fusion.2), channel_id=1, source_target_pairs={{0,1},{1,0},{2,3},{3,2},{4,5},{5,4},{6,7},{7,6},{8,24},{9,25},{10,... | collective-permute-start | bytes 6291464 | tf_op jit(solution)/shard_map/ppermute | solution.py:407
  251.6 14.4 %collective-permute-start.32 = (bf16[4,2,2,32,512]{4,3,0,1,2:T(8,128)(2,1)S(1)}, bf16[4,2,2,32,512]{4,3,0,1,2:T(8,128)(2,1)S(1)}, u32[]{:S(2)}, u32[]{:S(2)}) collective-permute-start(bf16[4,2,2,32,512]{4,3,0,1,2:T(8,128)(2,1)S(1)} %copy-done.71), channel_id=1, source_target_pairs={{0,1},{1,0},{2,3},{3,2},{4,5},{5,4},{6,7},{7,6},{8,24},{9,25},{10,... | collective-permute-start | bytes 1572872 | tf_op jit(solution)/shard_map/ppermute | solution.py:407
  252.1 6.9 %collective-permute-start.30 = (f32[2,1024]{1,0:T(2,128)S(1)}, f32[2,1024]{1,0:T(2,128)S(1)}, u32[]{:S(2)}, u32[]{:S(2)}) collective-permute-start(f32[2,1024]{1,0:T(2,128)S(1)} %bitcast.513), channel_id=1, source_target_pairs={{8,0},{16,8},{24,16},{9,1},{17,9},{25,17},{10,2},{18,10},{26,18},{... | collective-permute-start | bytes 24584 | tf_op jit(solution)/shard_map/ppermute | solution.py:347
  257.9 32.4 %collective-permute-start.35 = (bf16[1024,2048]{1,0:T(8,128)(2,1)}, bf16[1024,2048]{1,0:T(8,128)(2,1)}, u32[]{:S(2)}, u32[]{:S(2)}) collective-permute-start(bf16[1024,2048]{1,0:T(8,128)(2,1)} %bitcast_convert_fusion), channel_id=1, source_target_pairs={{0,8},{8,0},{1,9},{9,1},{2,10},{10,2},{3,11},{11,3},{4,12},{12,4},... | collective-permute-start | bytes 12582920 | tf_op jit(solution)/shard_map/ppermute | solution.py:392
  268.9 18.5 %collective-permute-start.36 = (bf16[4,2,128,512]{3,2,0,1:T(8,128)(2,1)S(1)}, bf16[4,2,128,512]{3,2,0,1:T(8,128)(2,1)S(1)}, u32[]{:S(2)}, u32[]{:S(2)}) collective-permute-start(bf16[4,2,128,512]{3,2,0,1:T(8,128)(2,1)S(1)} %dynamic-slice_bitcast_fusion.3), channel_id=1, source_target_pairs={{0,16},{1,17},{2,18},{3,19},{4,20},{5,21},{6,22},{7,23},{8,9},{9,8... | collective-permute-start | bytes 3145736 | tf_op jit(solution)/shard_map/ppermute | solution.py:407
  271.7 15.7 %collective-permute-start.37 = (bf16[4,2,32,512]{3,2,0,1:T(8,128)(2,1)S(1)}, bf16[4,2,32,512]{3,2,0,1:T(8,128)(2,1)S(1)}, u32[]{:S(2)}, u32[]{:S(2)}) collective-permute-start(bf16[4,2,32,512]{3,2,0,1:T(8,128)(2,1)S(1)} %dynamic-slice_bitcast_fusion.18), channel_id=1, source_target_pairs={{0,16},{1,17},{2,18},{3,19},{4,20},{5,21},{6,22},{7,23},{8,9},{9,8... | collective-permute-start | bytes 786440 | tf_op jit(solution)/shard_map/ppermute | solution.py:407
  278.0 2.9 collective-permute-start.33
  280.9 6.4 %collective-permute-start.34 = (f32[2,2,1024]{2,1,0:T(2,128)S(1)}, f32[2,2,1024]{2,1,0:T(2,128)S(1)}, u32[]{:S(2)}, u32[]{:S(2)}) collective-permute-start(f32[2,2,1024]{2,1,0:T(2,128)S(1)} %select_add_fusion), channel_id=1, source_target_pairs={{16,0},{17,1},{18,2},{19,3},{20,4},{21,5},{22,6},{23,7},{24,8},{25... | collective-permute-start | bytes 49160 | tf_op jit(solution)/shard_map/ppermute | solution.py:347
  283.9 5.3 %collective-permute-start.39 = (bf16[1024,512]{1,0:T(8,128)(2,1)}, bf16[1024,512]{1,0:T(8,128)(2,1)}, u32[]{:S(2)}, u32[]{:S(2)}) collective-permute-start(bf16[1024,512]{1,0:T(8,128)(2,1)} %bitcast_convert_fusion.4), channel_id=1, source_target_pairs={{0,8},{8,0},{1,9},{9,1},{2,10},{10,2},{3,11},{11,3},{4,12},{12,4},... | collective-permute-start | bytes 3145736 | tf_op jit(solution)/shard_map/ppermute | solution.py:392
  287.3 3.0 collective-permute-start.38
  289.2 128.6 %reduce-scatter.3.cloned.1.call-start = ((), (), s32[]{:S(2)}) async-start(), calls=%async_computation.2 | async-start | bytes 1966080 | tf_op jit(solution)/shard_map/reduce_scatter | solution.py:519
  300.7 37.6 %collective-permute-start.42 = (bf16[4,2,2,32,2048]{4,3,0,1,2:T(8,128)(2,1)}, bf16[4,2,2,32,2048]{4,3,0,1,2:T(8,128)(2,1)}, u32[]{:S(2)}, u32[]{:S(2)}) collective-permute-start(bf16[4,2,2,32,2048]{4,3,0,1,2:T(8,128)(2,1)} %bitcast_select_fusion), channel_id=1, source_target_pairs={{0,1},{1,0},{2,3},{3,2},{4,5},{5,4},{6,7},{7,6},{8,24},{9,25},{10,... | collective-permute-start | bytes 6291464 | tf_op jit(solution)/shard_map/ppermute | solution.py:407
  310.5 22.2 %collective-permute-start.44 = (bf16[4,2,2,32,512]{4,3,0,1,2:T(8,128)(2,1)}, bf16[4,2,2,32,512]{4,3,0,1,2:T(8,128)(2,1)}, u32[]{:S(2)}, u32[]{:S(2)}) collective-permute-start(bf16[4,2,2,32,512]{4,3,0,1,2:T(8,128)(2,1)} %get-tuple-element.172), channel_id=1, source_target_pairs={{0,1},{1,0},{2,3},{3,2},{4,5},{5,4},{6,7},{7,6},{8,24},{9,25},{10,... | collective-permute-start | bytes 1572872 | tf_op jit(solution)/shard_map/ppermute | solution.py:407
  311.2 27.1 %collective-permute-start.43 = (bf16[4,2,2,32,512]{4,3,0,1,2:T(8,128)(2,1)}, bf16[4,2,2,32,512]{4,3,0,1,2:T(8,128)(2,1)}, u32[]{:S(2)}, u32[]{:S(2)}) collective-permute-start(bf16[4,2,2,32,512]{4,3,0,1,2:T(8,128)(2,1)} %get-tuple-element.169), channel_id=1, source_target_pairs={{0,1},{1,0},{2,3},{3,2},{4,5},{5,4},{6,7},{7,6},{8,24},{9,25},{10,... | collective-permute-start | bytes 1572872 | tf_op jit(solution)/shard_map/ppermute | solution.py:407
  324.5 22.3 %collective-permute-start.41 = (bf16[1024,512]{1,0:T(8,128)(2,1)S(1)}, bf16[1024,512]{1,0:T(8,128)(2,1)S(1)}, u32[]{:S(2)}, u32[]{:S(2)}) collective-permute-start(bf16[1024,512]{1,0:T(8,128)(2,1)S(1)} %copy-done.84), channel_id=1, source_target_pairs={{0,8},{8,0},{1,9},{9,1},{2,10},{10,2},{3,11},{11,3},{4,12},{12,4},... | collective-permute-start | bytes 3145736 | tf_op jit(solution)/shard_map/ppermute | solution.py:392
  325.0 21.8 %collective-permute-start.40 = (bf16[1024,512]{1,0:T(8,128)(2,1)S(1)}, bf16[1024,512]{1,0:T(8,128)(2,1)S(1)}, u32[]{:S(2)}, u32[]{:S(2)}) collective-permute-start(bf16[1024,512]{1,0:T(8,128)(2,1)S(1)} %bitcast_convert_fusion.3), channel_id=1, source_target_pairs={{0,8},{8,0},{1,9},{9,1},{2,10},{10,2},{3,11},{11,3},{4,12},{12,4},... | collective-permute-start | bytes 3145736 | tf_op jit(solution)/shard_map/ppermute | solution.py:392
  339.7 21.5 %collective-permute-start.47 = (bf16[4,2,32,512]{3,2,0,1:T(8,128)(2,1)S(1)}, bf16[4,2,32,512]{3,2,0,1:T(8,128)(2,1)S(1)}, u32[]{:S(2)}, u32[]{:S(2)}) collective-permute-start(bf16[4,2,32,512]{3,2,0,1:T(8,128)(2,1)S(1)} %dynamic-slice_bitcast_fusion.16), channel_id=1, source_target_pairs={{0,16},{1,17},{2,18},{3,19},{4,20},{5,21},{6,22},{7,23},{8,9},{9,8... | collective-permute-start | bytes 786440 | tf_op jit(solution)/shard_map/ppermute | solution.py:407
  343.3 17.9 %collective-permute-start.45 = (bf16[4,2,32,2048]{3,2,0,1:T(8,128)(2,1)S(1)}, bf16[4,2,32,2048]{3,2,0,1:T(8,128)(2,1)S(1)}, u32[]{:S(2)}, u32[]{:S(2)}) collective-permute-start(bf16[4,2,32,2048]{3,2,0,1:T(8,128)(2,1)S(1)} %dynamic-slice_bitcast_fusion.2), channel_id=1, source_target_pairs={{0,16},{1,17},{2,18},{3,19},{4,20},{5,21},{6,22},{7,23},{8,9},{9,8... | collective-permute-start | bytes 3145736 | tf_op jit(solution)/shard_map/ppermute | solution.py:407
  346.0 15.2 %collective-permute-start.46 = (bf16[4,2,32,512]{3,2,0,1:T(8,128)(2,1)S(1)}, bf16[4,2,32,512]{3,2,0,1:T(8,128)(2,1)S(1)}, u32[]{:S(2)}, u32[]{:S(2)}) collective-permute-start(bf16[4,2,32,512]{3,2,0,1:T(8,128)(2,1)S(1)} %dynamic-slice_bitcast_fusion.17), channel_id=1, source_target_pairs={{0,16},{1,17},{2,18},{3,19},{4,20},{5,21},{6,22},{7,23},{8,9},{9,8... | collective-permute-start | bytes 786440 | tf_op jit(solution)/shard_map/ppermute | solution.py:407
  361.2 18.6 %collective-permute-start.57 = (bf16[4,2,2,32,512]{4,3,0,1,2:T(8,128)(2,1)}, bf16[4,2,2,32,512]{4,3,0,1,2:T(8,128)(2,1)}, u32[]{:S(2)}, u32[]{:S(2)}) collective-permute-start(bf16[4,2,2,32,512]{4,3,0,1,2:T(8,128)(2,1)} %bitcast_select_fusion.4), channel_id=1, source_target_pairs={{0,1},{1,0},{2,3},{3,2},{4,5},{5,4},{6,7},{7,6},{8,24},{9,25},{10,... | collective-permute-start | bytes 1572872 | tf_op jit(solution)/shard_map/ppermute | solution.py:407
  362.7 19.7 %collective-permute-start.55 = (bf16[4,2,2,32,512]{4,3,0,1,2:T(8,128)(2,1)}, bf16[4,2,2,32,512]{4,3,0,1,2:T(8,128)(2,1)}, u32[]{:S(2)}, u32[]{:S(2)}) collective-permute-start(bf16[4,2,2,32,512]{4,3,0,1,2:T(8,128)(2,1)} %bitcast_select_fusion.5), channel_id=1, source_target_pairs={{0,1},{1,0},{2,3},{3,2},{4,5},{5,4},{6,7},{7,6},{8,24},{9,25},{10,... | collective-permute-start | bytes 1572872 | tf_op jit(solution)/shard_map/ppermute | solution.py:407
  363.8 4.4 %collective-permute-start.48 = (f32[2,1024]{1,0:T(2,128)S(1)}, f32[2,1024]{1,0:T(2,128)S(1)}, u32[]{:S(2)}, u32[]{:S(2)}) collective-permute-start(f32[2,1024]{1,0:T(2,128)S(1)} %bitcast.512), channel_id=1, source_target_pairs={{8,0},{16,8},{24,16},{9,1},{17,9},{25,17},{10,2},{18,10},{26,18},{... | collective-permute-start | bytes 24584 | tf_op jit(solution)/shard_map/ppermute | solution.py:347
  374.4 4.0 collective-permute-start.50
  378.4 10.8 %collective-permute-start.51 = (f32[11264]{0:T(1024)S(1)}, f32[11264]{0:T(1024)S(1)}, u32[]{:S(2)}, u32[]{:S(2)}) collective-permute-start(f32[11264]{0:T(1024)S(1)} %add.384), channel_id=1, source_target_pairs={{0,16},{16,0},{1,17},{17,1},{2,18},{18,2},{3,19},{19,3},{4,20},{20... | collective-permute-start | bytes 135176 | tf_op jit(solution)/shard_map/ppermute | solution.py:392
  381.6 13.4 %collective-permute-start.58 = (bf16[4,2,32,512]{3,2,0,1:T(8,128)(2,1)S(1)}, bf16[4,2,32,512]{3,2,0,1:T(8,128)(2,1)S(1)}, u32[]{:S(2)}, u32[]{:S(2)}) collective-permute-start(bf16[4,2,32,512]{3,2,0,1:T(8,128)(2,1)S(1)} %dynamic-slice_bitcast_fusion.14), channel_id=1, source_target_pairs={{0,16},{1,17},{2,18},{3,19},{4,20},{5,21},{6,22},{7,23},{8,9},{9,8... | collective-permute-start | bytes 786440 | tf_op jit(solution)/shard_map/ppermute | solution.py:407
  384.2 10.9 %collective-permute-start.56 = (bf16[4,2,32,512]{3,2,0,1:T(8,128)(2,1)S(1)}, bf16[4,2,32,512]{3,2,0,1:T(8,128)(2,1)S(1)}, u32[]{:S(2)}, u32[]{:S(2)}) collective-permute-start(bf16[4,2,32,512]{3,2,0,1:T(8,128)(2,1)S(1)} %dynamic-slice_bitcast_fusion.15), channel_id=1, source_target_pairs={{0,16},{1,17},{2,18},{3,19},{4,20},{5,21},{6,22},{7,23},{8,9},{9,8... | collective-permute-start | bytes 786440 | tf_op jit(solution)/shard_map/ppermute | solution.py:407
  389.3 7.3 %collective-permute-start.52 = (f32[11264]{0:T(1024)S(1)}, f32[11264]{0:T(1024)S(1)}, u32[]{:S(2)}, u32[]{:S(2)}) collective-permute-start(f32[11264]{0:T(1024)S(1)} %add.385), channel_id=1, source_target_pairs={{0,2},{2,4},{4,6},{6,0},{1,3},{3,5},{5,7},{7,1},{8,10},{10,12},{12... | collective-permute-start | bytes 135176 | tf_op jit(solution)/shard_map/ppermute | solution.py:392
  391.0 9.1 %collective-permute-start.53 = (f32[11264]{0:T(1024)S(1)}, f32[11264]{0:T(1024)S(1)}, u32[]{:S(2)}, u32[]{:S(2)}) collective-permute-start(f32[11264]{0:T(1024)S(1)} %add.385), channel_id=1, source_target_pairs={{0,4},{2,6},{4,0},{6,2},{1,5},{3,7},{5,1},{7,3},{8,12},{10,14},{12... | collective-permute-start | bytes 135176 | tf_op jit(solution)/shard_map/ppermute | solution.py:392
  393.0 8.2 %collective-permute-start.54 = (f32[11264]{0:T(1024)S(1)}, f32[11264]{0:T(1024)S(1)}, u32[]{:S(2)}, u32[]{:S(2)}) collective-permute-start(f32[11264]{0:T(1024)S(1)} %add.385), channel_id=1, source_target_pairs={{0,6},{2,0},{4,2},{6,4},{1,7},{3,1},{5,3},{7,5},{8,14},{10,8},{12,... | collective-permute-start | bytes 135176 | tf_op jit(solution)/shard_map/ppermute | solution.py:392
  395.2 11.2 %collective-permute-start.59 = (bf16[2,64,512]{2,1,0:T(8,128)(2,1)S(1)}, bf16[2,64,512]{2,1,0:T(8,128)(2,1)S(1)}, u32[]{:S(2)}, u32[]{:S(2)}) collective-permute-start(bf16[2,64,512]{2,1,0:T(8,128)(2,1)S(1)} %get-tuple-element.251), channel_id=1, source_target_pairs={{0,2},{2,4},{4,6},{6,0},{1,3},{3,5},{5,7},{7,1},{8,10},{10,12},{12... | collective-permute-start | bytes 393224 | tf_op jit(solution)/shard_map/ppermute | solution.py:512
  395.3 21.0 %collective-permute-start.60 = (bf16[2,64,512]{2,1,0:T(8,128)(2,1)S(1)}, bf16[2,64,512]{2,1,0:T(8,128)(2,1)S(1)}, u32[]{:S(2)}, u32[]{:S(2)}) collective-permute-start(bf16[2,64,512]{2,1,0:T(8,128)(2,1)S(1)} %get-tuple-element.252), channel_id=1, source_target_pairs={{0,4},{2,6},{4,0},{6,2},{1,5},{3,7},{5,1},{7,3},{8,12},{10,14},{12... | collective-permute-start | bytes 393224 | tf_op jit(solution)/shard_map/ppermute | solution.py:512
  396.6 19.7 %collective-permute-start.61 = (bf16[2,64,512]{2,1,0:T(8,128)(2,1)S(1)}, bf16[2,64,512]{2,1,0:T(8,128)(2,1)S(1)}, u32[]{:S(2)}, u32[]{:S(2)}) collective-permute-start(bf16[2,64,512]{2,1,0:T(8,128)(2,1)S(1)} %get-tuple-element.253), channel_id=1, source_target_pairs={{0,6},{2,0},{4,2},{6,4},{1,7},{3,1},{5,3},{7,5},{8,14},{10,8},{12,... | collective-permute-start | bytes 393224 | tf_op jit(solution)/shard_map/ppermute | solution.py:512
  (98 other events, 673.0 us)
Sparse Core Ops, SparseCore 0:
  41.0 31.6 all-gather.7
  74.8 31.6 all-gather.9
  108.7 32.4 all-gather.11
  289.3 31.9 reduce-scatter.4
  368.4 46.6 reduce-scatter.2
